TPU v7x, 32 devices: a whole 2x2x4 slice. The times are simulated.
32 devices in a mesh: section: 8 (over y, x, core), expert: 4 (over z).
Axes of the slice: x: 2, y: 2, z: 4, core: 2. Of those that a mesh axis runs over, the one named last changes fastest.
Arguments:
- cotangent: bfloat16 [8, 512, 4096], P('section', 'expert'), may hold values from -6 to 6
- routes: int32 [8, 512, 2], P('section', 'expert'), may hold values from 0 to 3, all different within a row; in each aligned block of 64 rows (0 to 63, 64 to 127, ..., all dimensions but the last counted through in order) at most 64 rows name the same one
- gate_prob: float32 [8, 512, 2], P('section', 'expert'), may hold values from 0.05 to 1
- hidden: bfloat16 [8, 4, 2, 4, 64, 1536], P('section', 'expert'), may hold values from -6 to 6
Outputs:
- grad_pair: bfloat16 [4, 4, 1536, 4096], P(None, 'expert', 'section')
Inputs may be any that keep to these rules, and one draw needn't show every extreme that they name: `routes`: each row names 2 different experts. In each aligned block of 64 rows (one micro-batch of one device) no expert is named by more than 64 rows.
All inputs are finite; a program needn't handle non-finite values.
Results may differ from a plain program's by a relative error of at most 0.0059.
Values may be sent and summed in bfloat16 or wider, within the bound.
No kernel may reach another device: no remote copies, remote signals or barrier semaphores. Data moves between devices by JAX's collectives and lax.ppermute only.
A program may use at most 128 MiB of HBM per device.

v0:
```python
from functools import partial

import jax
import jax.numpy as jnp
from jax import lax
from jax.sharding import PartitionSpec as P


def slot_index(route_blk, experts_total):
    labels = jnp.arange(experts_total, dtype=jnp.int32)
    hits = (route_blk[:, :, None] == labels).astype(jnp.int32)
    per_token = jnp.sum(hits, axis=1)
    before = jnp.cumsum(per_token, axis=0) - per_token
    return jnp.sum(hits * before[:, None, :], axis=2)


def pack_block(cot_blk, route_blk, prob_blk, experts_total, capacity):
    width = cot_blk.shape[1]
    slots = slot_index(route_blk, experts_total)
    flat = (route_blk * capacity + slots).reshape(-1)
    weighted = (prob_blk[:, :, None] * cot_blk[:, None, :].astype(jnp.float32)).astype(jnp.bfloat16)
    empty = jnp.zeros((experts_total * capacity, width), jnp.bfloat16)
    return empty.at[flat].set(weighted.reshape(-1, width)).reshape(experts_total, capacity, width)


def rows_product(acts, arrived):
    return lax.dot_general(
        acts, arrived, (((0,), (0,)), ((), ())), preferred_element_type=jnp.float32
    )


def pair_add(pieces, half):
    lower = pieces[:half].astype(jnp.float32)
    upper = jnp.flip(pieces[half:], 0).astype(jnp.float32)
    return (lower + upper).astype(jnp.bfloat16)


def local(cotangent, routes, gate_prob, hidden):
    n_section = lax.axis_size("section")
    half = n_section // 2
    mb_count = hidden.shape[2]
    sources = hidden.shape[3]
    capacity = hidden.shape[4]
    ff_width = hidden.shape[5]
    width = cotangent.shape[2]
    top_count = routes.shape[2]
    tok_block = cotangent.shape[1] // mb_count
    cot_blocks = cotangent.reshape(mb_count, tok_block, width)
    route_blocks = routes.reshape(mb_count, tok_block, top_count)
    prob_blocks = gate_prob.reshape(mb_count, tok_block, top_count)
    packer = partial(pack_block, experts_total=sources, capacity=capacity)
    packed = jax.vmap(packer)(cot_blocks, route_blocks, prob_blocks)
    acts = hidden.reshape(mb_count * sources * capacity, ff_width)
    arrived = lax.all_to_all(packed, "expert", split_axis=1, concat_axis=1, tiled=True)
    rows = arrived.reshape(mb_count * sources * capacity, width)
    part = rows_product(acts, rows).astype(jnp.bfloat16)
    pieces = lax.all_to_all(part[None], "section", split_axis=1, concat_axis=0, tiled=True)
    result = pair_add(pieces, half)
    return result[:, None]


def solution(mesh):
    return jax.shard_map(
        local,
        mesh=mesh,
        in_specs=(
            P("section", "expert", None),
            P("section", "expert", None),
            P("section", "expert", None),
            P("section", "expert", None, None, None, None),
        ),
        out_specs=P(None, "expert", "section", None),
        check_vma=False,
    )
```

profile of v0, /device:TPU:0, one launch (start us, length us, event | category | flops | bytes accessed | tf_op | source)
XLA Modules:
  0.0 569.4 jit_solution(8621104423681271870)
XLA Ops:
  0.0 0.0 copy-start
  0.0 0.9 eq.15
  0.9 0.7 broadcast_multiply_fusion
  1.6 0.1 copy.30
  1.7 0.1 reduce_window_sum.11
  1.8 0.1 copy.32
  1.9 0.1 copy.33
  2.0 0.1 reduce_sum.22
  2.2 0.1 copy.28
  2.3 0.1 mul.45
  2.4 5.3 mul.50
  7.8 0.0 copy-start.3
  7.8 6.1 %mul.51 = f32[2,128,4096]{2,1,0:T(8,128)} reshape(f32[2,64,2,4096]{3,2,1,0:T(2,128)} %mul.50) | data formatting | bytes 8388608 | tf_op jit(solution)/shard_map/vmap()/mul | solution.py:21
  13.9 0.0 copy-done.3
  13.9 0.1 copy.34
  14.0 0.1 mul.48
  14.1 4.0 multiply_convert_fusion
  18.1 2.5 broadcast_in_dim.12
  20.6 67.6 %scatter_fusion = bf16[2,256,4096]{2,1,0:T(8,128)(2,1)} fusion(bf16[2,256,4096]{2,1,0:T(8,128)(2,1)} %broadcast_in_dim.12, s32[256]{0:T(256)S(1)} %fusion.5, bf16[256,4096]{1,0:T(8,128)(2,1)} %bitcast.36), kind=kCustom, calls=%fused_computation | custom fusion | bytes 6293504 | tf_op jit(solution)/shard_map/vmap()/scatter | solution.py:23
  88.2 2.5 copy.35
  90.7 99.8 %all_to_all.17 = bf16[2,4,64,4096]{3,2,0,1:T(8,128)(2,1)S(1)} all-to-all(bf16[2,4,64,4096]{3,2,0,1:T(8,128)(2,1)S(1)} %copy.35), channel_id=1, replica_groups=mesh['section'=8,'expert'=4] {'expert'}, dimensions={1} | all-to-all | bytes 8388608 | tf_op jit(solution)/shard_map/all_to_all | solution.py:54
  190.5 0.5 copy.36
  191.0 0.0 copy-done
  191.0 9.7 %fusion = bf16[1,1536,4096]{1,2,0:T(8,128)(2,1)} fusion(bf16[512,4096]{1,0:T(8,128)(2,1)S(1)} %bitcast.37, bf16[512,1536]{1,0:T(8,128)(2,1)S(1)} %bitcast.29), kind=kOutput, calls=%fused_computation.2 | convolution fusion | flops 6448742400 | bytes 18350080 | tf_op jit(solution)/shard_map/dot_general | solution.py:27
  200.7 54.3 %copy.37 = bf16[1,1536,4096]{2,0,1:T(2,128)(2,1)} copy(bf16[1,1536,4096]{1,2,0:T(8,128)(2,1)} %fusion) | data formatting | bytes 25165824 | tf_op jit(solution)/shard_map/broadcast_in_dim | solution.py:57
  255.0 0.5 broadcast.51
  255.5 77.6 %reduce = bf16[1536,4096]{1,0:T(8,128)(2,1)} reduce(bf16[1536,1,4096]{2,1,0:T(2,128)(2,1)} %bitcast.33, bf16[]{:T(256)} %broadcast.51), dimensions={1}, to_apply=%bitcast.25.reduce_sub_computation | reduce | bytes 25165826
  333.1 14.5 %reshape.86 = bf16[8,2,393216]{2,1,0:T(2,128)(2,1)} reshape(bf16[1536,4096]{1,0:T(8,128)(2,1)} %reduce) | data formatting | bytes 25165824
  347.6 145.7 %all_to_all.18 = bf16[8,2,393216]{2,1,0:T(2,128)(2,1)} all-to-all(bf16[8,2,393216]{2,1,0:T(2,128)(2,1)} %reshape.86), channel_id=1, replica_groups=mesh['section'=8,'expert'=4] {'section'}, dimensions={0} | all-to-all | bytes 25165824 | tf_op jit(solution)/shard_map/all_to_all | solution.py:57
  493.3 17.9 %reshape.87 = bf16[1536,1,4096]{2,1,0:T(2,128)(2,1)} reshape(bf16[8,2,393216]{2,1,0:T(2,128)(2,1)} %all_to_all.18) | data formatting | bytes 25165824
  511.2 0.0 copy-start.2
  511.2 15.5 %slice.16 = bf16[1,768,4096]{2,0,1:T(2,128)(2,1)} slice(bf16[1,1536,4096]{2,0,1:T(2,128)(2,1)} %bitcast.30), slice={[0:1], [768:1536], [0:4096]} | slice | bytes 12582912 | tf_op jit(solution)/shard_map/slice | solution.py:34
  526.7 0.7 copy-done.2
  527.4 17.1 %copy.40 = bf16[1,1536,4096]{2,1,0:T(8,128)(2,1)} copy(bf16[1,1536,4096]{2,0,1:T(2,128)(2,1)S(1)} %bitcast.31) | data formatting | bytes 25165824
  544.5 14.4 %copy.41 = bf16[1,768,4096]{2,1,0:T(8,128)(2,1)} copy(bf16[1,768,4096]{2,0,1:T(2,128)(2,1)} %slice.16) | data formatting | bytes 12582912
  558.9 0.0 copy-start.1
  558.9 10.5 %fusion.2 = bf16[4,1,192,4096]{3,2,1,0:T(8,128)(2,1)} fusion(bf16[1,8,192,4096]{3,2,1,0:T(8,128)(2,1)} %bitcast.34, bf16[4,192,4096]{2,1,0:T(8,128)(2,1)} %bitcast.35), kind=kLoop, calls=%fused_computation.5 | loop fusion | flops 12582912 | bytes 18874368 | tf_op jit(solution)/shard_map/broadcast_in_dim | solution.py:59
  569.4 0.0 copy-done.1
  (5 shorter events, 0.1 us)
Async XLA Ops:
  0.0 191.0 %copy-start = (bf16[1,1,2,4,64,1536]{5,4,3,2,1,0:T(8,128)(2,1)S(1)}, bf16[1,1,2,4,64,1536]{5,4,3,2,1,0:T(8,128)(2,1)}, u32[]{:S(2)}) copy-start(bf16[1,1,2,4,64,1536]{5,4,3,2,1,0:T(8,128)(2,1)} %param.7) | copy-start | bytes 4718596
  7.8 6.1 %copy-start.3 = (f32[1,128,2]{1,2,0:T(2,128)S(1)}, f32[1,128,2]{1,2,0:T(2,128)}, u32[]{:S(2)}) copy-start(f32[1,128,2]{1,2,0:T(2,128)} %param.6) | copy-start | bytes 3076
  511.2 16.2 %copy-start.2 = (bf16[1536,1,4096]{2,1,0:T(2,128)(2,1)S(1)}, bf16[1536,1,4096]{2,1,0:T(2,128)(2,1)}, u32[]{:S(2)}) copy-start(bf16[1536,1,4096]{2,1,0:T(2,128)(2,1)} %reshape.87) | copy-start | bytes 37748740
  558.9 10.6 %copy-start.1 = (bf16[1,1,2,4,64,1536]{5,4,3,2,1,0:T(8,128)(2,1)S(1)}, bf16[1,1,2,4,64,1536]{5,4,3,2,1,0:T(8,128)(2,1)}, u32[]{:S(2)}) copy-start(bf16[1,1,2,4,64,1536]{5,4,3,2,1,0:T(8,128)(2,1)} %param.7) | copy-start | bytes 4718596
where the time goes:
time: 572 us; the launch traced here: 569 us
  blocking collectives  246 us (43%)
  local copies, waits for them, and re-layouts  221 us (39%)
  other arithmetic  93 us (16%)
  matrix products  9.71 us (2%)
    all_to_all x1, blocking collectives, local(): lax.all_to_all(part[None], 'section', split_axis=1, concat_axis=0, tiled=...  146 us
    all_to_all x1, blocking collectives, local(): lax.all_to_all(packed, 'expert', split_axis=1, concat_axis=1, tiled=True)  99.8 us
    unnamed x1, other arithmetic  77.6 us
    scatter x1, local copies, waits for them, and re-layouts, pack_block(): empty.at[flat].set(weighted.reshape(-1, width))  67.6 us
    unnamed x14, local copies, waits for them, and re-layouts  65.2 us
    broadcast_in_dim x1, local copies, waits for them, and re-layouts, local(): part[None]  54.3 us
    slice x1, local copies, waits for them, and re-layouts, pair_add(): upper = jnp.flip(pieces[half:], 0).astype(jnp.float32)  15.5 us
    mul x3, local copies, waits for them, and re-layouts, pack_block(): prob_blk[:, :, None] * cot_blk[:, None, :].astype(jnp.float32)  11.6 us

commit v1 on v0

v1 whole, which is shorter than its diff:
```python
from functools import partial

import jax
import jax.numpy as jnp
from jax import lax
from jax.experimental import pallas as pl
from jax.experimental.pallas import tpu as pltpu
from jax.sharding import PartitionSpec as P

VMEM = 56 * 1024 * 1024


def token_acts_kernel(sources_ref, ids_ref, meta_ref, hid_ref, *refs, groups, top, capacity, tok_block):
    outs, rows_ref = refs[:-1], refs[-1]
    count = hid_ref.shape[1]
    tokens = rows_ref.shape[-1] // count
    slots = hid_ref.shape[0] * hid_ref.shape[2]
    expert = ids_ref[0].astype(jnp.float32)

    def field(i):
        return meta_ref[:, i * tokens : (i + 1) * tokens]

    hit = jnp.zeros((count, tokens), jnp.float32)
    gate = jnp.zeros((count, tokens), jnp.float32)
    for k in range(top):
        named = (field(k) == expert).astype(jnp.float32)
        hit = hit + named
        gate = gate + named * field(top + k)
    row = lax.broadcasted_iota(jnp.int32, (tokens, tokens), 0)
    col = lax.broadcasted_iota(jnp.int32, (tokens, tokens), 1)
    earlier = ((row // tok_block == col // tok_block) & (row < col)).astype(jnp.float32)
    before = jnp.dot(hit, earlier, preferred_element_type=jnp.float32)
    block = lax.broadcasted_iota(jnp.int32, (count, tokens), 1) // tok_block
    place = jnp.where(hit > 0, block * capacity + before.astype(jnp.int32), -1)
    slot = lax.broadcasted_iota(jnp.int32, (slots, tokens), 0)
    for i in range(count):
        source = sources_ref[i]
        pick = (slot == place[i : i + 1]).astype(jnp.bfloat16)
        hid = hid_ref[:, source].reshape(slots, hid_ref.shape[-1])
        rows = lax.dot_general(hid, pick, (((0,), (0,)), ((), ())), preferred_element_type=jnp.float32)
        rows = (rows * gate[i : i + 1]).astype(jnp.bfloat16)
        at = pl.ds(pl.multiple_of(source * tokens, tokens), tokens)
        rows_ref[:, :, at] = rows.reshape(rows_ref.shape[0], rows_ref.shape[1], tokens)
    for masks, out in zip(groups, outs):
        for i, mask in enumerate(masks):
            out[i] = rows_ref[ids_ref[1] ^ mask]


def token_acts(sources, metas, hidden, groups, top, tok_block, tokens):
    sections = lax.axis_size("section")
    mb_count, count, capacity, ff_width = hidden.shape
    rows = ff_width // sections
    depth = count * tokens
    ids = jnp.stack([lax.axis_index("expert"), lax.axis_index("section")]).astype(jnp.int32)
    return pl.pallas_call(
        partial(token_acts_kernel, groups=groups, top=top, capacity=capacity, tok_block=tok_block),
        grid_spec=pltpu.PrefetchScalarGridSpec(
            num_scalar_prefetch=2,
            grid=(),
            in_specs=[pl.BlockSpec(memory_space=pltpu.VMEM)] * 2,
            out_specs=[pl.BlockSpec(memory_space=pltpu.VMEM)] * len(groups),
            scratch_shapes=[pltpu.VMEM((sections, rows, depth), jnp.bfloat16)],
        ),
        out_shape=[jax.ShapeDtypeStruct((len(masks), rows, depth), jnp.bfloat16) for masks in groups],
        compiler_params=pltpu.CompilerParams(vmem_limit_bytes=VMEM),
        cost_estimate=pl.CostEstimate(
            flops=2 * mb_count * capacity * ff_width * depth,
            bytes_accessed=2 * ff_width * count * (mb_count * capacity + tokens),
            transcendentals=0,
        ),
    )(sources, ids, metas, hidden)


def product_kernel(places_ref, own_ref, mirror_ref, *refs, tokens, terms):
    count, rows, depth = own_ref.shape
    cots, outs, packed = refs[: -1 - count], refs[-1 - count : -1], refs[-1]
    at = 0
    for group in terms:
        for i in range(cots[group[0]].shape[0]):
            block = cots[group[0]][i]
            for other in group[1:]:
                block = block + cots[other][i]
            place = places_ref[at] * tokens
            for part in range(block.shape[0] // tokens):
                start = pl.multiple_of(place + part * depth, tokens)
                packed[pl.ds(start, tokens)] = block[part * tokens : (part + 1) * tokens]
            at += 1
    own = jnp.dot(own_ref[...].reshape(count * rows, depth), packed[:depth], preferred_element_type=jnp.float32)
    mirror = jnp.dot(mirror_ref[...].reshape(count * rows, depth), packed[depth:], preferred_element_type=jnp.float32)
    for i, out in enumerate(outs):
        j = count - 1 - i
        total = own[i * rows : (i + 1) * rows] + mirror[j * rows : (j + 1) * rows]
        out[...] = total.astype(jnp.bfloat16)


def product(places, own_acts, mirror_acts, cots, tokens, tile):
    count, rows, depth = own_acts.shape
    arrays = [array for entry in cots for array in entry]
    terms, at = [], 0
    for entry in cots:
        terms.append(list(range(at, at + len(entry))))
        at += len(entry)
    width = arrays[0].shape[-1]
    acts_spec = pl.BlockSpec((count, rows, depth), lambda n, src: (0, 0, 0))
    cot_specs = [pl.BlockSpec((*array.shape[:2], tile), lambda n, src: (0, 0, n)) for array in arrays]
    return pl.pallas_call(
        partial(product_kernel, tokens=tokens, terms=terms),
        grid_spec=pltpu.PrefetchScalarGridSpec(
            num_scalar_prefetch=1,
            grid=(width // tile,),
            in_specs=[acts_spec, acts_spec] + cot_specs,
            out_specs=[pl.BlockSpec((rows, tile), lambda n, src: (0, n))] * count,
            scratch_shapes=[pltpu.VMEM((2 * depth, tile), jnp.bfloat16)],
        ),
        out_shape=[jax.ShapeDtypeStruct((rows, width), jnp.bfloat16)] * count,
        compiler_params=pltpu.CompilerParams(vmem_limit_bytes=VMEM),
        cost_estimate=pl.CostEstimate(
            flops=4 * count * rows * depth * width,
            bytes_accessed=4 * (count * rows * depth + depth * width) + 2 * count * rows * width,
            transcendentals=0,
        ),
    )(places, own_acts, mirror_acts, *arrays)


def join_kernel(*refs, sections, offset):
    pieces = refs[:sections]
    out, sem = refs[-2:]
    section = lax.axis_index("section")
    width = pieces[0].shape[-1]
    copies = []
    for mask, piece in enumerate(pieces):
        source = section ^ mask
        upper = (source >= sections // 2).astype(jnp.int32)
        pair = source + upper * (sections - 1 - 2 * source)
        column = pl.multiple_of(upper * (out.shape[-1] // 2) + offset, 128)
        copies.append(pltpu.make_async_copy(piece, out.at[pair, 0, :, pl.ds(column, width)], sem.at[mask]))
    for copy in copies:
        copy.start()
    for copy in copies:
        copy.wait()


def join(pieces, offset, half_width, out=None):
    sections = len(pieces)
    rows = pieces[0].shape[0]
    shape = jax.ShapeDtypeStruct((sections // 2, 1, rows, 2 * half_width), jnp.bfloat16)
    first = out is None
    operands = tuple(pieces) if first else (*pieces, out)
    return pl.pallas_call(
        partial(join_kernel, sections=sections, offset=offset),
        in_specs=[pl.BlockSpec(memory_space=pltpu.VMEM)] * sections + [pl.BlockSpec(memory_space=pl.ANY)] * (not first),
        out_specs=pl.BlockSpec(memory_space=pl.ANY),
        out_shape=shape,
        scratch_shapes=[pltpu.SemaphoreType.DMA((sections,))],
        input_output_aliases={} if first else {sections: 0},
        compiler_params=pltpu.CompilerParams(vmem_limit_bytes=VMEM),
    )(*operands)


def shift(block, axis, size, step):
    return lax.ppermute(block, axis, [(i, (i + step) % size) for i in range(size)])


def ring(block, axis, size):
    return [block] + [shift(block, axis, size, step) for step in range(1, size)]


def local(cotangent, routes, gate_prob, hidden):
    n_section = lax.axis_size("section")
    n_expert = lax.axis_size("expert")
    section = lax.axis_index("section")
    expert = lax.axis_index("expert")
    mb_count = hidden.shape[2]
    tokens, width = cotangent.shape[1:]
    top = routes.shape[2]
    half_width = width // 2
    widths = [half_width * 5 // 8, half_width * 3 // 8]
    offsets = [sum(widths[:c]) for c in range(len(widths))]
    mirror = [(i, n_section - 1 - i) for i in range(n_section)]
    upper = section >= n_section // 2
    quarter = n_section // 4
    near = list(range(quarter, n_section - quarter))
    groups = [near, [mask for mask in range(n_section) if mask not in near]]
    steps = jnp.arange(n_expert, dtype=jnp.int32)
    behind = lax.rem(expert - steps + n_expert, n_expert).astype(jnp.int32)
    short = n_expert == 4
    meta = jnp.concatenate([routes[0].astype(jnp.float32), gate_prob[0]], 1).T.reshape(-1)
    metas = jnp.stack(ring(meta, "expert", n_expert)) if short else lax.all_gather(meta, "expert")
    order = behind if short else steps
    acts = token_acts(order, metas, hidden[0, 0], groups, top, tokens // mb_count, tokens)
    cot = cotangent[0]
    kept, given = [], []
    for offset, span in zip(offsets, widths):
        low = cot[:, offset : offset + span]
        high = cot[:, half_width + offset : half_width + offset + span]
        kept.append(jnp.where(upper, high, low))
        given.append(jnp.where(upper, low, high))
    taken = [lax.ppermute(given[0], "section", mirror)]
    if short:
        kept_first, kept_back = shift(kept[0], "expert", n_expert, 1), shift(kept[0], "expert", n_expert, 3)
        *held, taken[0] = lax.optimization_barrier((*acts, taken[0]))
        mirror_acts = [lax.ppermute(group, "section", mirror) for group in held]
        taken.append(lax.ppermute(given[1], "section", mirror))
        kept_first, taken[0] = lax.optimization_barrier((kept_first, taken[0]))
        taken_first, taken_back = shift(taken[0], "expert", n_expert, 1), shift(taken[0], "expert", n_expert, 3)
        both = jnp.concatenate([kept[0], taken[0]])
        both, taken_first, taken_back, mirror_acts[0], taken[1] = lax.optimization_barrier(
            (both, taken_first, taken_back, mirror_acts[0], taken[1])
        )
        across = lax.ppermute(both, "expert", [(0, 2), (3, 1)])
        first = jnp.concatenate([kept_first, taken_first])
        back = jnp.concatenate([kept_back, taken_back])
        passed = lax.ppermute(jnp.where(expert == 2, first, back), "expert", [(2, 3), (1, 0)])
        across, passed, mirror_acts[1] = lax.optimization_barrier((across, passed, mirror_acts[1]))
        cots = [[(both[None],), (first[None],), (across[None], passed[None]), (back[None],)]]
        orders = [behind, steps]
        later = jnp.broadcast_to(jnp.concatenate([kept[1], taken[1]]), (n_expert, 2 * tokens, widths[1]))
    else:
        taken.append(lax.ppermute(given[1], "section", mirror))
        mirror_acts = [lax.ppermute(group, "section", mirror) for group in acts]
        cots = [[(lax.all_gather(jnp.concatenate([a, b]), "expert"),)] for a, b in zip(kept, taken)]
        orders = [steps] * len(cots)

    out = None
    for c, (offset, span) in enumerate(zip(offsets, widths)):
        pieces = [None] * n_section
        for g, masks in enumerate(groups):
            sums = product(orders[c], acts[g], mirror_acts[g], cots[c], tokens, span // 2)
            if short and c == 0 and g == 0:
                later, cots[0] = lax.optimization_barrier((later, cots[0]))
                cots.append([(lax.all_to_all(later, "expert", split_axis=0, concat_axis=0, tiled=True),)])
            for mask, rows in zip(masks, sums):
                pieces[mask] = rows
                if mask:
                    pieces[mask] = lax.ppermute(rows, "section", [(i, i ^ mask) for i in range(n_section)])
        if c == 0:
            sent = [1, 2, n_section - 2, n_section - 1]
            early, cots[1] = lax.optimization_barrier(([pieces[mask] for mask in sent], cots[1]))
            for mask, rows in zip(sent, early):
                pieces[mask] = rows
        out = join(pieces, offset, half_width, out)
    return out


def solution(mesh):
    return jax.shard_map(
        local,
        mesh=mesh,
        in_specs=(
            P("section", "expert", None),
            P("section", "expert", None),
            P("section", "expert", None),
            P("section", "expert", None, None, None),
        ),
        out_specs=P(None, "expert", "section", None),
        check_vma=False,
    )
```

time: 572 us -> 162 us (0.28)
  blocking collectives: 246 us -> 0 us
  local copies, waits for them, and re-layouts: 221 us -> 4.89 us
  other arithmetic: 93 us -> 7.01 us
  waiting for transfers between devices: 0 us -> 75 us
  starting transfers between devices: 0 us -> 39.6 us
  Pallas kernels: 0 us -> 35.1 us
  matrix products: 9.71 us -> 0 us
    all_to_all x2 -> x0, blocking collectives: 246 us -> none  [the longest x1 146 us: local(): lax.all_to_all(part[None], 'section', split_axis=1, concat_axis=0, tiled=...]
    unnamed x1 -> x0, other arithmetic: 77.6 us -> none
    ppermute x0 -> x27, waiting for transfers between devices: none -> 74.9 us  [the longest x14 41.9 us: local(): lax.ppermute(rows, 'section', [(i, i ^ mask) for i in range(n_section)])]
    scatter x1 -> x0, local copies, waits for them, and re-layouts: 67.6 us -> none  [pack_block(): empty.at[flat].set(weighted.reshape(-1, width))]
    unnamed x14 -> x46, local copies, waits for them, and re-layouts: 65.2 us -> 2.47 us
    broadcast_in_dim x2 -> x1, local copies, waits for them, and re-layouts: 56.8 us -> 1.24 us  [local(): jnp.broadcast_to(jnp.concatenate([kept[1], taken[1]]), (n_expert, 2 * tok...]
    pallas_call x0 -> x7, Pallas kernels: none -> 35.1 us  [the longest x4 23.9 us: product(): pl.pallas_call(partial(product_kernel, tokens=tokens, terms=terms), grid_...]
    ppermute x0 -> x27, starting transfers between devices: none -> 35 us  [the longest x14 12.3 us: local(): lax.ppermute(rows, 'section', [(i, i ^ mask) for i in range(n_section)])]
  transfers between devices with their start and end apart: 0 -> 28, of which waited for: 0 -> 13; matrix products, arithmetic and copies ran while one was open for 0% -> 4% of each run, Pallas kernels for 0% -> 20%
where the time goes in v1:
time: 162 us
  waiting for transfers between devices  75 us (46%)
  starting transfers between devices  39.6 us (24%)
  Pallas kernels  35.1 us (22%)
  other arithmetic  7.01 us (4%)
  local copies, waits for them, and re-layouts  4.89 us (3%)
    ppermute x14, waiting for transfers between devices, local(): lax.ppermute(rows, 'section', [(i, i ^ mask) for i in range(n_section)])  41.9 us
    pallas_call x4, Pallas kernels, product(): pl.pallas_call(partial(product_kernel, tokens=tokens, terms=terms), grid_...  23.9 us
    ppermute x14, starting transfers between devices, local(): lax.ppermute(rows, 'section', [(i, i ^ mask) for i in range(n_section)])  12.3 us
    ppermute x7, starting transfers between devices, shift(): lax.ppermute(block, axis, [(i, (i + step) % size) for i in range(size)])  12.3 us
    ppermute x1, waiting for transfers between devices, local(): taken.append(lax.ppermute(given[1], 'section', mirror))  12 us
    ppermute x7, waiting for transfers between devices, shift(): lax.ppermute(block, axis, [(i, (i + step) % size) for i in range(size)])  8.26 us
    pallas_call x2, Pallas kernels, join(): pl.pallas_call(partial(join_kernel, sections=sections, offset=offset), in...  7.1 us
    ppermute x2, waiting for transfers between devices, local(): mirror_acts = [lax.ppermute(group, 'section', mirror) for group in held]  6.08 us
  transfers between devices with their start and end apart: 28, of which 13 were waited for; matrix products, arithmetic and copies ran while one was open for 4% of the time, Pallas kernels for 20%

profile of v1, /device:TPU:0, one launch (start us, length us, event | category | flops | bytes accessed | tf_op | source)
XLA Modules:
  0.0 161.9 jit_solution(986277622593329208)
XLA Ops:
  0.0 0.7 convert_bitcast_fusion
  0.7 0.7 pad_maximum_fusion.3
  1.4 5.0 %collective-permute-start.2 = (f32[512]{0:T(512)S(1)}, f32[512]{0:T(512)S(1)}, u32[]{:S(2)}, u32[]{:S(2)}) collective-permute-start(f32[512]{0:T(512)S(1)} %get-tuple-element.94), channel_id=1, source_target_pairs={{0,3},{1,0},{2,1},{3,2},{4,7},{5,4},{6,5},{7,6},{8,11},{9,8},{10,9... | collective-permute-start | bytes 6152 | tf_op jit(solution)/shard_map/ppermute | solution.py:161
  6.4 1.0 collective-permute-start
  7.4 1.1 broadcast_select_fusion.1
  8.6 1.1 collective-permute-start.4
  9.7 3.1 %collective-permute-start.10 = (bf16[128,1280]{1,0:T(8,128)(2,1)S(1)}, bf16[128,1280]{1,0:T(8,128)(2,1)S(1)}, u32[]{:S(2)}, u32[]{:S(2)}) collective-permute-start(bf16[128,1280]{1,0:T(8,128)(2,1)S(1)} %get-tuple-element.92), channel_id=1, source_target_pairs={{0,3},{1,0},{2,1},{3,2},{4,7},{5,4},{6,5},{7,6},{8,11},{9,8},{10,9... | collective-permute-start | bytes 983048 | tf_op jit(solution)/shard_map/ppermute | solution.py:161
  13.9 0.6 pad_maximum_fusion.2.meta_ref
  14.5 4.1 %shard_map.46 = (bf16[4,192,512]{2,1,0:T(8,128)(2,1)}, bf16[4,192,512]{2,1,0:T(8,128)(2,1)}) custom-call(s32[4]{0:T(128)} %compare_select_fusion.sources_ref.places_ref, s32[2]{0:T(128)} %pad_add_fusion.ids_ref, f32[4,512]{1,0:T(4,128)} %pad_maximum_fusion.2.meta_ref, bf16[2,4,64,1536]{3,2,1,0:T(8,128)(2,1)} %bitcast.21), custom_call_target="tpu_custom_call" | custom-call | flops 201326592 | bytes 3145728 | tf_op jit(solution)/shard_map/pallas_call | solution.py:55
  18.7 0.8 collective-permute-done.4
  19.4 0.6 collective-permute-start.7
  20.1 1.7 %broadcast_select_fusion.3 = (bf16[128,768]{1,0:T(8,128)(2,1)S(1)}, bf16[128,768]{1,0:T(8,128)(2,1)}) fusion(pred[]{:T(512)S(6)} %ge.3, bf16[128,4096]{1,0:T(8,128)(2,1)} %bitcast.27), kind=kLoop, calls=%fused_computation.5 | loop fusion | flops 196608 | bytes 786433 | tf_op jit(solution)/shard_map/jit(_where)/select_n | solution.py:196
  21.8 2.0 %collective-permute-start.8 = (bf16[128,768]{1,0:T(8,128)(2,1)}, bf16[128,768]{1,0:T(8,128)(2,1)}, u32[]{:S(2)}, u32[]{:S(2)}) collective-permute-start(bf16[128,768]{1,0:T(8,128)(2,1)} %get-tuple-element.90), channel_id=1, source_target_pairs={{0,28},{4,24},{8,20},{12,16},{16,12},{20,8},{24,4},{28,0},{1,29},{... | collective-permute-start | bytes 589832 | tf_op jit(solution)/shard_map/ppermute | solution.py:203
  23.8 4.9 %collective-permute-done.3 = bf16[128,1280]{1,0:T(8,128)(2,1)S(1)} collective-permute-done((bf16[128,1280]{1,0:T(8,128)(2,1)S(1)}, bf16[128,1280]{1,0:T(8,128)(2,1)S(1)}, u32[]{:S(2)}, u32[]{:S(2)}) %collective-permute-start.3) | collective-permute-done | bytes 327712 | tf_op jit(solution)/shard_map/ppermute | solution.py:161
  28.8 3.2 %collective-permute-start.6 = (bf16[128,1280]{1,0:T(8,128)(2,1)S(1)}, bf16[128,1280]{1,0:T(8,128)(2,1)S(1)}, u32[]{:S(2)}, u32[]{:S(2)}) collective-permute-start(bf16[128,1280]{1,0:T(8,128)(2,1)S(1)} %collective-permute-done.4), channel_id=1, source_target_pairs={{0,3},{1,0},{2,1},{3,2},{4,7},{5,4},{6,5},{7,6},{8,11},{9,8},{10,9... | collective-permute-start | bytes 983048 | tf_op jit(solution)/shard_map/ppermute | solution.py:161
  32.4 12.0 %collective-permute-done.8 = bf16[128,768]{1,0:T(8,128)(2,1)} collective-permute-done((bf16[128,768]{1,0:T(8,128)(2,1)}, bf16[128,768]{1,0:T(8,128)(2,1)}, u32[]{:S(2)}, u32[]{:S(2)}) %collective-permute-start.8) | collective-permute-done | bytes 196640 | tf_op jit(solution)/shard_map/ppermute | solution.py:203
  44.4 3.3 %collective-permute-done.5 = bf16[128,1280]{1,0:T(8,128)(2,1)S(1)} collective-permute-done((bf16[128,1280]{1,0:T(8,128)(2,1)S(1)}, bf16[128,1280]{1,0:T(8,128)(2,1)S(1)}, u32[]{:S(2)}, u32[]{:S(2)}) %collective-permute-start.5) | collective-permute-done | bytes 327712 | tf_op jit(solution)/shard_map/ppermute | solution.py:161
  47.9 1.3 collective-permute-start.11
  49.2 4.9 %collective-permute-start.9 = (bf16[256,1280]{1,0:T(8,128)(2,1)S(1)}, bf16[256,1280]{1,0:T(8,128)(2,1)S(1)}, u32[]{:S(2)}, u32[]{:S(2)}) collective-permute-start(bf16[256,1280]{1,0:T(8,128)(2,1)S(1)} %pad_maximum_fusion), channel_id=1, source_target_pairs={{0,2},{3,1},{4,6},{7,5},{8,10},{11,9},{12,14},{15,13},{16,18},{19,... | collective-permute-start | bytes 1966088 | tf_op jit(solution)/shard_map/ppermute | solution.py:210
  54.1 1.0 pad_maximum_fusion.1
  55.1 6.1 %collective-permute-done.12.mirror_ref = bf16[4,192,512]{2,1,0:T(8,128)(2,1)S(1)} collective-permute-done((bf16[4,192,512]{2,1,0:T(8,128)(2,1)S(1)}, bf16[4,192,512]{2,1,0:T(8,128)(2,1)S(1)}, u32[]{:S(2)}, u32[]{:S(2)}) %collective-permute-start.12) | collective-permute-done | bytes 786464 | tf_op jit(solution)/shard_map/ppermute | solution.py:202
  61.2 4.7 %collective-permute-done.11 = bf16[256,1280]{1,0:T(8,128)(2,1)S(1)} collective-permute-done((bf16[256,1280]{1,0:T(8,128)(2,1)S(1)}, bf16[256,1280]{1,0:T(8,128)(2,1)S(1)}, u32[]{:S(2)}, u32[]{:S(2)}) %collective-permute-start.11) | collective-permute-done | bytes 655392 | tf_op jit(solution)/shard_map/ppermute | solution.py:213
  65.8 1.2 collective-permute-done.9
  67.1 0.8 copy-done.18
  67.9 1.2 broadcast_in_dim.18
  69.2 4.7 %all-to-all-start = ((bf16[4,256,768]{2,1,0:T(8,128)(2,1)}), bf16[4,256,768]{2,1,0:T(8,128)(2,1)S(1)}, u32[]{:S(2)}, u32[]{:S(2)}) async-start(bf16[4,256,768]{2,1,0:T(8,128)(2,1)} %broadcast_in_dim.18), calls=%async_computation | async-start | bytes 3145728 | tf_op jit(solution)/shard_map/all_to_all | solution.py:231
  73.8 6.7 %shard_map.47 = (bf16[192,1280]{1,0:T(8,128)(2,1)}, bf16[192,1280]{1,0:T(8,128)(2,1)}, bf16[192,1280]{1,0:T(8,128)(2,1)}, bf16[192,1280]{1,0:T(8,128)(2,1)}) custom-call(s32[4]{0:T(128)} %compare_select_fusion.sources_ref.places_ref, bf16[4,192,512]{2,1,0:T(8,128)(2,1)} %get-tuple-element.56.own_ref, bf16[4,192,512]{2,1,0:T(8,128)(2,1)} %copy-done.16, ...), custom_call_target="tpu_custom_call" | custom-call | flops 2013265920 | bytes 6160384 | tf_op jit(solution)/shard_map/pallas_call | solution.py:106
  80.6 0.7 collective-permute-start.15
  81.3 6.7 %shard_map.48 = (bf16[192,1280]{1,0:T(8,128)(2,1)}, bf16[192,1280]{1,0:T(8,128)(2,1)}, bf16[192,1280]{1,0:T(8,128)(2,1)}, bf16[192,1280]{1,0:T(8,128)(2,1)}) custom-call(s32[4]{0:T(128)} %compare_select_fusion.sources_ref.places_ref, bf16[4,192,512]{2,1,0:T(8,128)(2,1)} %get-tuple-element.51.own_ref, bf16[4,192,512]{2,1,0:T(8,128)(2,1)} %collective-permute-done.7.mirror_ref, ...), custom_call_target="tpu_custom_call" | custom-call | flops 2013265920 | bytes 6160384 | tf_op jit(solution)/shard_map/pallas_call | solution.py:106
  88.0 2.1 %collective-permute-start.16 = (bf16[192,1280]{1,0:T(8,128)(2,1)S(1)}, bf16[192,1280]{1,0:T(8,128)(2,1)S(1)}, u32[]{:S(2)}, u32[]{:S(2)}) collective-permute-start(bf16[192,1280]{1,0:T(8,128)(2,1)S(1)} %copy-done.19), channel_id=1, source_target_pairs={{0,28},{4,24},{8,20},{12,16},{16,12},{20,8},{24,4},{28,0},{1,29},{... | collective-permute-start | bytes 1474568 | tf_op jit(solution)/shard_map/ppermute | solution.py:235
  90.6 1.2 collective-permute-start.24
  92.3 3.5 %collective-permute-done.15.refs_6_ = bf16[192,1280]{1,0:T(8,128)(2,1)S(1)} collective-permute-done((bf16[192,1280]{1,0:T(8,128)(2,1)}, bf16[192,1280]{1,0:T(8,128)(2,1)S(1)}, u32[]{:S(2)}, u32[]{:S(2)}) %collective-permute-start.15) | collective-permute-done | bytes 491552 | tf_op jit(solution)/shard_map/ppermute | solution.py:235
  95.9 9.6 %collective-permute-done.16.refs_7_ = bf16[192,1280]{1,0:T(8,128)(2,1)S(1)} collective-permute-done((bf16[192,1280]{1,0:T(8,128)(2,1)S(1)}, bf16[192,1280]{1,0:T(8,128)(2,1)S(1)}, u32[]{:S(2)}, u32[]{:S(2)}) %collective-permute-start.16) | collective-permute-done | bytes 491552 | tf_op jit(solution)/shard_map/ppermute | solution.py:235
  105.5 10.4 %collective-permute-done.14.refs_2_ = bf16[192,1280]{1,0:T(8,128)(2,1)S(1)} collective-permute-done((bf16[192,1280]{1,0:T(8,128)(2,1)}, bf16[192,1280]{1,0:T(8,128)(2,1)S(1)}, u32[]{:S(2)}, u32[]{:S(2)}) %collective-permute-start.14) | collective-permute-done | bytes 491552 | tf_op jit(solution)/shard_map/ppermute | solution.py:235
  115.9 0.6 iota.9.places_ref
  117.1 5.2 %shard_map.50 = (bf16[192,768]{1,0:T(8,128)(2,1)}, bf16[192,768]{1,0:T(8,128)(2,1)}, bf16[192,768]{1,0:T(8,128)(2,1)}, bf16[192,768]{1,0:T(8,128)(2,1)}) custom-call(s32[4]{0:T(128)} %iota.9.places_ref, bf16[4,192,512]{2,1,0:T(8,128)(2,1)} %get-tuple-element.51.own_ref, bf16[4,192,512]{2,1,0:T(8,128)(2,1)} %collective-permute-done.7.mirror_ref, ...), custom_call_target="tpu_custom_call" | custom-call | flops 1207959552 | bytes 4325376 | tf_op jit(solution)/shard_map/pallas_call | solution.py:106
  122.3 0.8 collective-permute-start.18
  123.6 5.3 %shard_map.49 = (bf16[192,768]{1,0:T(8,128)(2,1)}, bf16[192,768]{1,0:T(8,128)(2,1)}, bf16[192,768]{1,0:T(8,128)(2,1)}, bf16[192,768]{1,0:T(8,128)(2,1)}) custom-call(s32[4]{0:T(128)} %iota.7.places_ref, bf16[4,192,512]{2,1,0:T(8,128)(2,1)} %get-tuple-element.56.own_ref, bf16[4,192,512]{2,1,0:T(8,128)(2,1)} %copy-done.16, bf16[4,256,768]{2,1,0:T(8,128)(2,1)} %copy-done), custom_call_target="tpu_custom_call" | custom-call | flops 1207959552 | bytes 4325376 | tf_op jit(solution)/shard_map/pallas_call | solution.py:106
  128.9 1.5 collective-permute-start.20
  130.5 1.3 collective-permute-start.21
  131.8 1.0 collective-permute-done.18.refs_2_
  132.8 1.5 collective-permute-start.22
  134.3 3.9 %collective-permute-done.19.refs_3_ = bf16[192,768]{1,0:T(8,128)(2,1)S(1)} collective-permute-done((bf16[192,768]{1,0:T(8,128)(2,1)}, bf16[192,768]{1,0:T(8,128)(2,1)S(1)}, u32[]{:S(2)}, u32[]{:S(2)}) %collective-permute-start.19) | collective-permute-done | bytes 294944 | tf_op jit(solution)/shard_map/ppermute | solution.py:235
  138.2 2.1 %collective-permute-start.23 = (bf16[192,768]{1,0:T(8,128)(2,1)}, bf16[192,768]{1,0:T(8,128)(2,1)S(1)}, u32[]{:S(2)}, u32[]{:S(2)}) collective-permute-start(bf16[192,768]{1,0:T(8,128)(2,1)} %get-tuple-element.80), channel_id=1, source_target_pairs={{0,28},{4,24},{8,20},{12,16},{16,12},{20,8},{24,4},{28,0},{1,29},{... | collective-permute-start | bytes 884744 | tf_op jit(solution)/shard_map/ppermute | solution.py:235
  140.3 4.0 %shard_map.51.refs_8_ = bf16[4,1,192,4096]{3,2,1,0:T(8,128)(2,1)} custom-call(bf16[192,1280]{1,0:T(8,128)(2,1)} %get-tuple-element.81.refs_0_, bf16[192,1280]{1,0:T(8,128)(2,1)} %copy-done.4, bf16[192,1280]{1,0:T(8,128)(2,1)} %copy-done.7, bf16[192,1280]{1,0:T(8,128)(2,1)} %collective-permute-done.24.refs_3_, ...), custom_call_target="tpu_custom_call" | custom-call | tf_op jit(solution)/shard_map/pallas_call | solution.py:149
  144.4 13.4 %collective-permute-done.21.refs_5_ = bf16[192,768]{1,0:T(8,128)(2,1)S(1)} collective-permute-done((bf16[192,768]{1,0:T(8,128)(2,1)S(1)}, bf16[192,768]{1,0:T(8,128)(2,1)S(1)}, u32[]{:S(2)}, u32[]{:S(2)}) %collective-permute-start.21) | collective-permute-done | bytes 294944 | tf_op jit(solution)/shard_map/ppermute | solution.py:235
  157.9 0.7 copy-done.11
  158.9 3.0 %shard_map.52 = bf16[4,1,192,4096]{3,2,1,0:T(8,128)(2,1)} custom-call(bf16[192,768]{1,0:T(8,128)(2,1)} %get-tuple-element.73.refs_0_, bf16[192,768]{1,0:T(8,128)(2,1)} %copy-done.12, bf16[192,768]{1,0:T(8,128)(2,1)} %copy-done.8, bf16[192,768]{1,0:T(8,128)(2,1)} %copy-done.9, bf16[192,768]{1,0:T(8,128)(2,1)} %copy-done.10, ...), custom_call_target="tpu_custom_call", output_to_operand_aliasing={{}: (8, {})} | custom-call | tf_op jit(solution)/shard_map/pallas_call | solution.py:149
  (76 shorter events, 4.3 us)
Async XLA Ops:
  1.4 12.5 %collective-permute-start.2 = (f32[512]{0:T(512)S(1)}, f32[512]{0:T(512)S(1)}, u32[]{:S(2)}, u32[]{:S(2)}) collective-permute-start(f32[512]{0:T(512)S(1)} %get-tuple-element.94), channel_id=1, source_target_pairs={{0,3},{1,0},{2,1},{3,2},{4,7},{5,4},{6,5},{7,6},{8,11},{9,8},{10,9... | collective-permute-start | bytes 6152 | tf_op jit(solution)/shard_map/ppermute | solution.py:161
  6.4 7.5 %collective-permute-start.1 = (f32[512]{0:T(512)S(1)}, f32[512]{0:T(512)S(1)}, u32[]{:S(2)}, u32[]{:S(2)}) collective-permute-start(f32[512]{0:T(512)S(1)} %get-tuple-element.94), channel_id=1, source_target_pairs={{0,2},{1,3},{2,0},{3,1},{4,6},{5,7},{6,4},{7,5},{8,10},{9,11},{10,... | collective-permute-start | bytes 6152 | tf_op jit(solution)/shard_map/ppermute | solution.py:161
  6.4 7.5 %collective-permute-start = (f32[512]{0:T(512)S(1)}, f32[512]{0:T(512)S(1)}, u32[]{:S(2)}, u32[]{:S(2)}) collective-permute-start(f32[512]{0:T(512)S(1)} %get-tuple-element.94), channel_id=1, source_target_pairs={{0,1},{1,2},{2,3},{3,0},{4,5},{5,6},{6,7},{7,4},{8,9},{9,10},{10,1... | collective-permute-start | bytes 6152 | tf_op jit(solution)/shard_map/ppermute | solution.py:161
  8.6 10.9 %collective-permute-start.4 = (bf16[128,1280]{1,0:T(8,128)(2,1)S(1)}, bf16[128,1280]{1,0:T(8,128)(2,1)S(1)}, u32[]{:S(2)}, u32[]{:S(2)}) collective-permute-start(bf16[128,1280]{1,0:T(8,128)(2,1)S(1)} %get-tuple-element.91), channel_id=1, source_target_pairs={{0,28},{4,24},{8,20},{12,16},{16,12},{20,8},{24,4},{28,0},{1,29},{... | collective-permute-start | bytes 983048 | tf_op jit(solution)/shard_map/ppermute | solution.py:198
  9.7 22.3 %collective-permute-start.10 = (bf16[128,1280]{1,0:T(8,128)(2,1)S(1)}, bf16[128,1280]{1,0:T(8,128)(2,1)S(1)}, u32[]{:S(2)}, u32[]{:S(2)}) collective-permute-start(bf16[128,1280]{1,0:T(8,128)(2,1)S(1)} %get-tuple-element.92), channel_id=1, source_target_pairs={{0,3},{1,0},{2,1},{3,2},{4,7},{5,4},{6,5},{7,6},{8,11},{9,8},{10,9... | collective-permute-start | bytes 983048 | tf_op jit(solution)/shard_map/ppermute | solution.py:161
  13.9 14.9 %collective-permute-start.3 = (bf16[128,1280]{1,0:T(8,128)(2,1)S(1)}, bf16[128,1280]{1,0:T(8,128)(2,1)S(1)}, u32[]{:S(2)}, u32[]{:S(2)}) collective-permute-start(bf16[128,1280]{1,0:T(8,128)(2,1)S(1)} %get-tuple-element.92), channel_id=1, source_target_pairs={{0,1},{1,2},{2,3},{3,0},{4,5},{5,6},{6,7},{7,4},{8,9},{9,10},{10,1... | collective-permute-start | bytes 983048 | tf_op jit(solution)/shard_map/ppermute | solution.py:161
  19.4 28.3 %collective-permute-start.7 = (bf16[4,192,512]{2,1,0:T(8,128)(2,1)}, bf16[4,192,512]{2,1,0:T(8,128)(2,1)}, u32[]{:S(2)}, u32[]{:S(2)}) collective-permute-start(bf16[4,192,512]{2,1,0:T(8,128)(2,1)} %get-tuple-element.51.own_ref), channel_id=1, source_target_pairs={{0,28},{4,24},{8,20},{12,16},{16,12},{20,8},{24,4},{28,0},{1,29},{... | collective-permute-start | bytes 2359304 | tf_op jit(solution)/shard_map/ppermute | solution.py:202
  21.8 22.6 %collective-permute-start.8 = (bf16[128,768]{1,0:T(8,128)(2,1)}, bf16[128,768]{1,0:T(8,128)(2,1)}, u32[]{:S(2)}, u32[]{:S(2)}) collective-permute-start(bf16[128,768]{1,0:T(8,128)(2,1)} %get-tuple-element.90), channel_id=1, source_target_pairs={{0,28},{4,24},{8,20},{12,16},{16,12},{20,8},{24,4},{28,0},{1,29},{... | collective-permute-start | bytes 589832 | tf_op jit(solution)/shard_map/ppermute | solution.py:203
  23.8 8.2 %copy-start.15 = (bf16[4,192,512]{2,1,0:T(8,128)(2,1)S(1)}, bf16[4,192,512]{2,1,0:T(8,128)(2,1)}, u32[]{:S(2)}) copy-start(bf16[4,192,512]{2,1,0:T(8,128)(2,1)} %get-tuple-element.56.own_ref) | copy-start | bytes 2359300
  28.8 20.4 %copy-start.3 = (bf16[256,1280]{1,0:T(8,128)(2,1)}, bf16[256,1280]{1,0:T(8,128)(2,1)S(1)}, u32[]{:S(2)}) copy-start(bf16[256,1280]{1,0:T(8,128)(2,1)S(1)} %pad_maximum_fusion) | copy-start | bytes 1966084
  28.8 15.6 %collective-permute-start.6 = (bf16[128,1280]{1,0:T(8,128)(2,1)S(1)}, bf16[128,1280]{1,0:T(8,128)(2,1)S(1)}, u32[]{:S(2)}, u32[]{:S(2)}) collective-permute-start(bf16[128,1280]{1,0:T(8,128)(2,1)S(1)} %collective-permute-done.4), channel_id=1, source_target_pairs={{0,3},{1,0},{2,1},{3,2},{4,7},{5,4},{6,5},{7,6},{8,11},{9,8},{10,9... | collective-permute-start | bytes 983048 | tf_op jit(solution)/shard_map/ppermute | solution.py:161
  31.9 15.8 %collective-permute-start.5 = (bf16[128,1280]{1,0:T(8,128)(2,1)S(1)}, bf16[128,1280]{1,0:T(8,128)(2,1)S(1)}, u32[]{:S(2)}, u32[]{:S(2)}) collective-permute-start(bf16[128,1280]{1,0:T(8,128)(2,1)S(1)} %collective-permute-done.4), channel_id=1, source_target_pairs={{0,1},{1,2},{2,3},{3,0},{4,5},{5,6},{6,7},{7,4},{8,9},{9,10},{10,1... | collective-permute-start | bytes 983048 | tf_op jit(solution)/shard_map/ppermute | solution.py:161
  32.0 29.2 %collective-permute-start.12 = (bf16[4,192,512]{2,1,0:T(8,128)(2,1)S(1)}, bf16[4,192,512]{2,1,0:T(8,128)(2,1)S(1)}, u32[]{:S(2)}, u32[]{:S(2)}) collective-permute-start(bf16[4,192,512]{2,1,0:T(8,128)(2,1)S(1)} %copy-done.15), channel_id=1, source_target_pairs={{0,28},{4,24},{8,20},{12,16},{16,12},{20,8},{24,4},{28,0},{1,29},{... | collective-permute-start | bytes 2359304 | tf_op jit(solution)/shard_map/ppermute | solution.py:202
  47.7 7.3 %copy-start.1 = (bf16[256,1280]{1,0:T(8,128)(2,1)}, bf16[256,1280]{1,0:T(8,128)(2,1)S(1)}, u32[]{:S(2)}) copy-start(bf16[256,1280]{1,0:T(8,128)(2,1)S(1)} %constant_dynamic-update-slice_fusion) | copy-start | bytes 1966084
  47.8 21.4 %copy-start.2 = (bf16[256,1280]{1,0:T(8,128)(2,1)}, bf16[256,1280]{1,0:T(8,128)(2,1)S(1)}, u32[]{:S(2)}) copy-start(bf16[256,1280]{1,0:T(8,128)(2,1)S(1)} %constant_dynamic-update-slice_fusion.2) | copy-start | bytes 1966084
  47.9 18.0 %collective-permute-start.11 = (bf16[256,1280]{1,0:T(8,128)(2,1)S(1)}, bf16[256,1280]{1,0:T(8,128)(2,1)S(1)}, u32[]{:S(2)}, u32[]{:S(2)}) collective-permute-start(bf16[256,1280]{1,0:T(8,128)(2,1)S(1)} %broadcast_select_fusion), channel_id=1, source_target_pairs={{2,3},{1,0},{6,7},{5,4},{10,11},{9,8},{14,15},{13,12},{18,19},{17,... | collective-permute-start | bytes 1966088 | tf_op jit(solution)/shard_map/ppermute | solution.py:213
  49.2 17.9 %collective-permute-start.9 = (bf16[256,1280]{1,0:T(8,128)(2,1)S(1)}, bf16[256,1280]{1,0:T(8,128)(2,1)S(1)}, u32[]{:S(2)}, u32[]{:S(2)}) collective-permute-start(bf16[256,1280]{1,0:T(8,128)(2,1)S(1)} %pad_maximum_fusion), channel_id=1, source_target_pairs={{0,2},{3,1},{4,6},{7,5},{8,10},{11,9},{12,14},{15,13},{16,18},{19,... | collective-permute-start | bytes 1966088 | tf_op jit(solution)/shard_map/ppermute | solution.py:210
  61.2 5.9 %copy-start.16 = (bf16[4,192,512]{2,1,0:T(8,128)(2,1)}, bf16[4,192,512]{2,1,0:T(8,128)(2,1)S(1)}, u32[]{:S(2)}) copy-start(bf16[4,192,512]{2,1,0:T(8,128)(2,1)S(1)} %collective-permute-done.12.mirror_ref) | copy-start | bytes 2359300
  65.8 1.2 copy-start.17
  67.1 0.8 copy-start.18
  69.2 46.8 %all-to-all-start = ((bf16[4,256,768]{2,1,0:T(8,128)(2,1)}), bf16[4,256,768]{2,1,0:T(8,128)(2,1)S(1)}, u32[]{:S(2)}, u32[]{:S(2)}) async-start(bf16[4,256,768]{2,1,0:T(8,128)(2,1)} %broadcast_in_dim.18), calls=%async_computation | async-start | bytes 3145728 | tf_op jit(solution)/shard_map/all_to_all | solution.py:231
  80.5 11.3 %collective-permute-start.13 = (bf16[192,1280]{1,0:T(8,128)(2,1)}, bf16[192,1280]{1,0:T(8,128)(2,1)S(1)}, u32[]{:S(2)}, u32[]{:S(2)}) collective-permute-start(bf16[192,1280]{1,0:T(8,128)(2,1)} %get-tuple-element.66), channel_id=1, source_target_pairs={{0,4},{4,0},{8,12},{12,8},{16,20},{20,16},{24,28},{28,24},{1,5},{5... | collective-permute-start | bytes 1474568 | tf_op jit(solution)/shard_map/ppermute | solution.py:235
  80.6 7.5 %copy-start.19 = (bf16[192,1280]{1,0:T(8,128)(2,1)S(1)}, bf16[192,1280]{1,0:T(8,128)(2,1)}, u32[]{:S(2)}) copy-start(bf16[192,1280]{1,0:T(8,128)(2,1)} %get-tuple-element.70) | copy-start | bytes 1474564
  80.6 15.3 %collective-permute-start.15 = (bf16[192,1280]{1,0:T(8,128)(2,1)}, bf16[192,1280]{1,0:T(8,128)(2,1)S(1)}, u32[]{:S(2)}, u32[]{:S(2)}) collective-permute-start(bf16[192,1280]{1,0:T(8,128)(2,1)} %get-tuple-element.69), channel_id=1, source_target_pairs={{0,24},{4,28},{8,16},{12,20},{16,8},{20,12},{24,0},{28,4},{1,25},{... | collective-permute-start | bytes 1474568 | tf_op jit(solution)/shard_map/ppermute | solution.py:235
  88.0 17.5 %collective-permute-start.16 = (bf16[192,1280]{1,0:T(8,128)(2,1)S(1)}, bf16[192,1280]{1,0:T(8,128)(2,1)S(1)}, u32[]{:S(2)}, u32[]{:S(2)}) collective-permute-start(bf16[192,1280]{1,0:T(8,128)(2,1)S(1)} %copy-done.19), channel_id=1, source_target_pairs={{0,28},{4,24},{8,20},{12,16},{16,12},{20,8},{24,4},{28,0},{1,29},{... | collective-permute-start | bytes 1474568 | tf_op jit(solution)/shard_map/ppermute | solution.py:235
  90.1 25.8 %collective-permute-start.14 = (bf16[192,1280]{1,0:T(8,128)(2,1)}, bf16[192,1280]{1,0:T(8,128)(2,1)S(1)}, u32[]{:S(2)}, u32[]{:S(2)}) collective-permute-start(bf16[192,1280]{1,0:T(8,128)(2,1)} %get-tuple-element.68), channel_id=1, source_target_pairs={{0,8},{4,12},{8,0},{12,4},{16,24},{20,28},{24,16},{28,20},{1,9},{5... | collective-permute-start | bytes 1474568 | tf_op jit(solution)/shard_map/ppermute | solution.py:235
  90.6 38.3 %collective-permute-start.24 = (bf16[192,1280]{1,0:T(8,128)(2,1)}, bf16[192,1280]{1,0:T(8,128)(2,1)}, u32[]{:S(2)}, u32[]{:S(2)}) collective-permute-start(bf16[192,1280]{1,0:T(8,128)(2,1)} %get-tuple-element.84), channel_id=1, source_target_pairs={{0,12},{4,8},{8,4},{12,0},{16,28},{20,24},{24,20},{28,16},{1,13},{... | collective-permute-start | bytes 1474568 | tf_op jit(solution)/shard_map/ppermute | solution.py:235
  91.8 48.5 %copy-start.4 = (bf16[192,1280]{1,0:T(8,128)(2,1)}, bf16[192,1280]{1,0:T(8,128)(2,1)S(1)}, u32[]{:S(2)}) copy-start(bf16[192,1280]{1,0:T(8,128)(2,1)S(1)} %collective-permute-done.13.refs_1_) | copy-start | bytes 1474564
  91.8 38.6 %collective-permute-start.25 = (bf16[192,1280]{1,0:T(8,128)(2,1)}, bf16[192,1280]{1,0:T(8,128)(2,1)}, u32[]{:S(2)}, u32[]{:S(2)}) collective-permute-start(bf16[192,1280]{1,0:T(8,128)(2,1)} %get-tuple-element.85), channel_id=1, source_target_pairs={{0,16},{4,20},{8,24},{12,28},{16,0},{20,4},{24,8},{28,12},{1,17},{... | collective-permute-start | bytes 1474568 | tf_op jit(solution)/shard_map/ppermute | solution.py:235
  95.8 44.5 %copy-start.5 = (bf16[192,1280]{1,0:T(8,128)(2,1)}, bf16[192,1280]{1,0:T(8,128)(2,1)S(1)}, u32[]{:S(2)}) copy-start(bf16[192,1280]{1,0:T(8,128)(2,1)S(1)} %collective-permute-done.15.refs_6_) | copy-start | bytes 1474564
  95.8 35.9 %collective-permute-start.26 = (bf16[192,1280]{1,0:T(8,128)(2,1)}, bf16[192,1280]{1,0:T(8,128)(2,1)}, u32[]{:S(2)}, u32[]{:S(2)}) collective-permute-start(bf16[192,1280]{1,0:T(8,128)(2,1)} %get-tuple-element.86), channel_id=1, source_target_pairs={{0,20},{4,16},{8,28},{12,24},{16,4},{20,0},{24,12},{28,8},{1,21},{... | collective-permute-start | bytes 1474568 | tf_op jit(solution)/shard_map/ppermute | solution.py:235
  105.5 34.8 %copy-start.6 = (bf16[192,1280]{1,0:T(8,128)(2,1)}, bf16[192,1280]{1,0:T(8,128)(2,1)S(1)}, u32[]{:S(2)}) copy-start(bf16[192,1280]{1,0:T(8,128)(2,1)S(1)} %collective-permute-done.16.refs_7_) | copy-start | bytes 1474564
  115.9 24.4 %copy-start.7 = (bf16[192,1280]{1,0:T(8,128)(2,1)}, bf16[192,1280]{1,0:T(8,128)(2,1)S(1)}, u32[]{:S(2)}) copy-start(bf16[192,1280]{1,0:T(8,128)(2,1)S(1)} %collective-permute-done.14.refs_2_) | copy-start | bytes 1474564
  115.9 1.2 copy-start
  122.3 10.5 %collective-permute-start.18 = (bf16[192,768]{1,0:T(8,128)(2,1)}, bf16[192,768]{1,0:T(8,128)(2,1)S(1)}, u32[]{:S(2)}, u32[]{:S(2)}) collective-permute-start(bf16[192,768]{1,0:T(8,128)(2,1)} %get-tuple-element.75), channel_id=1, source_target_pairs={{0,8},{4,12},{8,0},{12,4},{16,24},{20,28},{24,16},{28,20},{1,9},{5... | collective-permute-start | bytes 884744 | tf_op jit(solution)/shard_map/ppermute | solution.py:235
  123.1 15.1 %collective-permute-start.19 = (bf16[192,768]{1,0:T(8,128)(2,1)}, bf16[192,768]{1,0:T(8,128)(2,1)S(1)}, u32[]{:S(2)}, u32[]{:S(2)}) collective-permute-start(bf16[192,768]{1,0:T(8,128)(2,1)} %get-tuple-element.76), channel_id=1, source_target_pairs={{0,12},{4,8},{8,4},{12,0},{16,28},{20,24},{24,20},{28,16},{1,13},{... | collective-permute-start | bytes 884744 | tf_op jit(solution)/shard_map/ppermute | solution.py:235
  123.6 5.3 %copy-start.21 = (bf16[192,768]{1,0:T(8,128)(2,1)S(1)}, bf16[192,768]{1,0:T(8,128)(2,1)}, u32[]{:S(2)}) copy-start(bf16[192,768]{1,0:T(8,128)(2,1)} %get-tuple-element.77) | copy-start | bytes 884740
  123.6 6.9 %copy-start.20 = (bf16[192,768]{1,0:T(8,128)(2,1)S(1)}, bf16[192,768]{1,0:T(8,128)(2,1)}, u32[]{:S(2)}) copy-start(bf16[192,768]{1,0:T(8,128)(2,1)} %get-tuple-element.78) | copy-start | bytes 884740
  128.9 15.5 %collective-permute-start.20 = (bf16[192,768]{1,0:T(8,128)(2,1)S(1)}, bf16[192,768]{1,0:T(8,128)(2,1)S(1)}, u32[]{:S(2)}, u32[]{:S(2)}) collective-permute-start(bf16[192,768]{1,0:T(8,128)(2,1)S(1)} %copy-done.21), channel_id=1, source_target_pairs={{0,16},{4,20},{8,24},{12,28},{16,0},{20,4},{24,8},{28,12},{1,17},{... | collective-permute-start | bytes 884744 | tf_op jit(solution)/shard_map/ppermute | solution.py:235
  130.5 27.4 %collective-permute-start.21 = (bf16[192,768]{1,0:T(8,128)(2,1)S(1)}, bf16[192,768]{1,0:T(8,128)(2,1)S(1)}, u32[]{:S(2)}, u32[]{:S(2)}) collective-permute-start(bf16[192,768]{1,0:T(8,128)(2,1)S(1)} %copy-done.20), channel_id=1, source_target_pairs={{0,20},{4,16},{8,28},{12,24},{16,4},{20,0},{24,12},{28,8},{1,21},{... | collective-permute-start | bytes 884744 | tf_op jit(solution)/shard_map/ppermute | solution.py:235
  131.8 26.1 %collective-permute-start.17 = (bf16[192,768]{1,0:T(8,128)(2,1)}, bf16[192,768]{1,0:T(8,128)(2,1)S(1)}, u32[]{:S(2)}, u32[]{:S(2)}) collective-permute-start(bf16[192,768]{1,0:T(8,128)(2,1)} %get-tuple-element.74), channel_id=1, source_target_pairs={{0,4},{4,0},{8,12},{12,8},{16,20},{20,16},{24,28},{28,24},{1,5},{5... | collective-permute-start | bytes 884744 | tf_op jit(solution)/shard_map/ppermute | solution.py:235
  132.8 11.6 %copy-start.8 = (bf16[192,768]{1,0:T(8,128)(2,1)}, bf16[192,768]{1,0:T(8,128)(2,1)S(1)}, u32[]{:S(2)}) copy-start(bf16[192,768]{1,0:T(8,128)(2,1)S(1)} %collective-permute-done.18.refs_2_) | copy-start | bytes 884740
  132.8 25.1 %collective-permute-start.22 = (bf16[192,768]{1,0:T(8,128)(2,1)}, bf16[192,768]{1,0:T(8,128)(2,1)S(1)}, u32[]{:S(2)}, u32[]{:S(2)}) collective-permute-start(bf16[192,768]{1,0:T(8,128)(2,1)} %get-tuple-element.79), channel_id=1, source_target_pairs={{0,24},{4,28},{8,16},{12,20},{16,8},{20,12},{24,0},{28,4},{1,25},{... | collective-permute-start | bytes 884744 | tf_op jit(solution)/shard_map/ppermute | solution.py:235
  138.2 6.2 %copy-start.9 = (bf16[192,768]{1,0:T(8,128)(2,1)}, bf16[192,768]{1,0:T(8,128)(2,1)S(1)}, u32[]{:S(2)}) copy-start(bf16[192,768]{1,0:T(8,128)(2,1)S(1)} %collective-permute-done.19.refs_3_) | copy-start | bytes 884740
  138.2 19.7 %collective-permute-start.23 = (bf16[192,768]{1,0:T(8,128)(2,1)}, bf16[192,768]{1,0:T(8,128)(2,1)S(1)}, u32[]{:S(2)}, u32[]{:S(2)}) collective-permute-start(bf16[192,768]{1,0:T(8,128)(2,1)} %get-tuple-element.80), channel_id=1, source_target_pairs={{0,28},{4,24},{8,20},{12,16},{16,12},{20,8},{24,4},{28,0},{1,29},{... | collective-permute-start | bytes 884744 | tf_op jit(solution)/shard_map/ppermute | solution.py:235
  144.4 13.5 %copy-start.10 = (bf16[192,768]{1,0:T(8,128)(2,1)}, bf16[192,768]{1,0:T(8,128)(2,1)S(1)}, u32[]{:S(2)}) copy-start(bf16[192,768]{1,0:T(8,128)(2,1)S(1)} %collective-permute-done.20.refs_4_) | copy-start | bytes 884740
  157.9 0.9 copy-start.13
  157.9 1.0 copy-start.14
  (2 other events, 1.6 us)

commit v2 on v1

v2 whole, which is shorter than its diff:
```python
from functools import partial

import jax
import jax.numpy as jnp
from jax import lax
from jax.experimental import pallas as pl
from jax.experimental.pallas import tpu as pltpu
from jax.sharding import PartitionSpec as P

VMEM = 60 * 1024 * 1024
LONG = pl.CostEstimate(flops=10**11, bytes_accessed=10**6, transcendentals=0)
SHORT = pl.CostEstimate(flops=10**6, bytes_accessed=10**3, transcendentals=0)


def token_acts_kernel(meta_ref, hid_ref, *refs, groups, top, capacity, tok_block, in_ring):
    outs, rows_ref = refs[:-1], refs[-1]
    count = hid_ref.shape[1]
    tokens = rows_ref.shape[-1] // count
    slots = hid_ref.shape[0] * hid_ref.shape[2]
    me, section = lax.axis_index("expert"), lax.axis_index("section")
    expert = me.astype(jnp.float32)

    def field(i):
        return meta_ref[:, i * tokens : (i + 1) * tokens]

    hit = jnp.zeros((count, tokens), jnp.float32)
    gate = jnp.zeros((count, tokens), jnp.float32)
    for k in range(top):
        named = (field(k) == expert).astype(jnp.float32)
        hit = hit + named
        gate = gate + named * field(top + k)
    row = lax.broadcasted_iota(jnp.int32, (tokens, tokens), 0)
    col = lax.broadcasted_iota(jnp.int32, (tokens, tokens), 1)
    earlier = ((row // tok_block == col // tok_block) & (row < col)).astype(jnp.float32)
    before = jnp.dot(hit, earlier, preferred_element_type=jnp.float32)
    block = lax.broadcasted_iota(jnp.int32, (count, tokens), 1) // tok_block
    place = jnp.where(hit > 0, block * capacity + before.astype(jnp.int32), -1)
    slot = lax.broadcasted_iota(jnp.int32, (slots, tokens), 0)
    for i in range(count):
        source = lax.rem(me + (count - i), count) if in_ring else i
        pick = (slot == place[i : i + 1]).astype(jnp.bfloat16)
        hid = hid_ref[:, source].reshape(slots, hid_ref.shape[-1])
        rows = lax.dot_general(hid, pick, (((0,), (0,)), ((), ())), preferred_element_type=jnp.float32)
        rows = (rows * gate[i : i + 1]).astype(jnp.bfloat16)
        at = pl.ds(pl.multiple_of(source * tokens, tokens), tokens)
        rows_ref[:, :, at] = rows.reshape(rows_ref.shape[0], rows_ref.shape[1], tokens)
    for masks, out in zip(groups, outs):
        for i, mask in enumerate(masks):
            out[i] = rows_ref[section ^ mask]


def token_acts(metas, hidden, groups, top, tok_block, in_ring):
    sections = lax.axis_size("section")
    mb_count, count, capacity, ff_width = hidden.shape
    rows = ff_width // sections
    depth = count * metas.shape[1] // (2 * top)
    return pl.pallas_call(
        partial(token_acts_kernel, groups=groups, top=top, capacity=capacity, tok_block=tok_block, in_ring=in_ring),
        in_specs=[pl.BlockSpec(memory_space=pltpu.VMEM)] * 2,
        out_specs=[pl.BlockSpec(memory_space=pltpu.VMEM)] * len(groups),
        out_shape=[jax.ShapeDtypeStruct((len(masks), rows, depth), jnp.bfloat16) for masks in groups],
        scratch_shapes=[pltpu.VMEM((sections, rows, depth), jnp.bfloat16)],
        compiler_params=pltpu.CompilerParams(vmem_limit_bytes=VMEM),
        cost_estimate=LONG,
    )(metas, hidden)


def product_kernel(own_ref, mirror_ref, *refs, tokens, layout):
    count, rows, depth = own_ref.shape
    cots, outs, packed = refs[: -1 - count], refs[-1 - count : -1], refs[-1]
    sources = depth // tokens
    me = lax.axis_index("expert")
    for cot, (behind, replica) in zip(cots, layout):
        for i in range(cot.shape[0]):
            source = i if behind is None else lax.rem(me + (sources - behind), sources)
            for part in range(cot.shape[1] // tokens):
                start = pl.multiple_of(source * tokens + (replica + part) * depth, tokens)
                packed[pl.ds(start, tokens)] = cot[i, part * tokens : (part + 1) * tokens]
    own = jnp.dot(own_ref[...].reshape(count * rows, depth), packed[:depth], preferred_element_type=jnp.float32)
    mirror = jnp.dot(mirror_ref[...].reshape(count * rows, depth), packed[depth:], preferred_element_type=jnp.float32)
    for i, out in enumerate(outs):
        j = count - 1 - i
        total = own[i * rows : (i + 1) * rows] + mirror[j * rows : (j + 1) * rows]
        out[...] = total.astype(jnp.bfloat16)


def product(own_acts, mirror_acts, cots, layout, tokens, tile):
    count, rows, depth = own_acts.shape
    width = cots[0].shape[-1]
    acts_spec = pl.BlockSpec((count, rows, depth), lambda n: (0, 0, 0))
    return pl.pallas_call(
        partial(product_kernel, tokens=tokens, layout=layout),
        grid=(width // tile,),
        in_specs=[acts_spec, acts_spec] + [pl.BlockSpec((*cot.shape[:2], tile), lambda n: (0, 0, n)) for cot in cots],
        out_specs=[pl.BlockSpec((rows, tile), lambda n: (0, n))] * count,
        out_shape=[jax.ShapeDtypeStruct((rows, width), jnp.bfloat16)] * count,
        scratch_shapes=[pltpu.VMEM((2 * depth, tile), jnp.bfloat16)],
        compiler_params=pltpu.CompilerParams(vmem_limit_bytes=VMEM),
        cost_estimate=SHORT,
    )(own_acts, mirror_acts, *cots)


def join_kernel(*refs, sections, offset):
    pieces = refs[:sections]
    out, sem = refs[-2:]
    section = lax.axis_index("section")
    width = pieces[0].shape[-1]
    copies = []
    for mask, piece in enumerate(pieces):
        source = section ^ mask
        upper = (source >= sections // 2).astype(jnp.int32)
        pair = source + upper * (sections - 1 - 2 * source)
        column = pl.multiple_of(upper * (out.shape[-1] // 2) + offset, 128)
        copies.append(pltpu.make_async_copy(piece, out.at[pair, 0, :, pl.ds(column, width)], sem.at[mask]))
    for copy in copies:
        copy.start()
    for copy in copies:
        copy.wait()


def join(pieces, offset, half_width, out=None):
    sections = len(pieces)
    rows = pieces[0].shape[0]
    shape = jax.ShapeDtypeStruct((sections // 2, 1, rows, 2 * half_width), jnp.bfloat16)
    first = out is None
    operands = tuple(pieces) if first else (*pieces, out)
    return pl.pallas_call(
        partial(join_kernel, sections=sections, offset=offset),
        in_specs=[pl.BlockSpec(memory_space=pltpu.VMEM)] * sections + [pl.BlockSpec(memory_space=pl.ANY)] * (not first),
        out_specs=pl.BlockSpec(memory_space=pl.ANY),
        out_shape=shape,
        scratch_shapes=[pltpu.SemaphoreType.DMA((sections,))],
        input_output_aliases={} if first else {sections: 0},
        compiler_params=pltpu.CompilerParams(vmem_limit_bytes=VMEM),
    )(*operands)


def shift(block, axis, size, step):
    return lax.ppermute(block, axis, [(i, (i + step) % size) for i in range(size)])


def ring(block, axis, size):
    return [block] + [shift(block, axis, size, step) for step in range(1, size)]


def repeat_kernel(*refs):
    blocks, out = refs[:-2], refs[-1]
    at = 0
    for block in blocks:
        out[0, at : at + block.shape[0]] = block[...]
        at += block.shape[0]


def repeat(blocks, after, count):
    rows, width = sum(block.shape[0] for block in blocks), blocks[0].shape[1]
    return pl.pallas_call(
        repeat_kernel,
        grid=(count,),
        in_specs=[pl.BlockSpec(block.shape, lambda i: (0, 0)) for block in blocks] + [pl.BlockSpec(memory_space=pl.ANY)],
        out_specs=pl.BlockSpec((1, rows, width), lambda i: (i, 0, 0)),
        out_shape=jax.ShapeDtypeStruct((count, rows, width), blocks[0].dtype),
        compiler_params=pltpu.CompilerParams(vmem_limit_bytes=VMEM),
        cost_estimate=LONG,
    )(*blocks, after)


def local(cotangent, routes, gate_prob, hidden):
    n_section = lax.axis_size("section")
    n_expert = lax.axis_size("expert")
    section = lax.axis_index("section")
    expert = lax.axis_index("expert")
    mb_count = hidden.shape[2]
    tokens, width = cotangent.shape[1:]
    top = routes.shape[2]
    half_width = width // 2
    widths = [half_width * 9 // 16, half_width * 7 // 16]
    offsets = [sum(widths[:c]) for c in range(len(widths))]
    mirror = [(i, n_section - 1 - i) for i in range(n_section)]
    upper = section >= n_section // 2
    quarter = n_section // 4
    near = [start + i for i in range(quarter // 2) for start in (quarter, 2 * quarter)]
    near += [n_section - 1 - mask for mask in reversed(near)]
    groups = [[mask for mask in range(n_section) if mask not in near], near]
    short = n_expert == 4
    meta = jnp.concatenate([routes[0].astype(jnp.float32), gate_prob[0]], 1).T.reshape(-1)
    metas = jnp.stack(ring(meta, "expert", n_expert)) if short else lax.all_gather(meta, "expert")
    acts = token_acts(metas, hidden[0, 0], groups, top, tokens // mb_count, short)
    cot = cotangent[0]
    kept, given = [], []
    for offset, span in zip(offsets, widths):
        low = cot[:, offset : offset + span]
        high = cot[:, half_width + offset : half_width + offset + span]
        kept.append(jnp.where(upper, high, low))
        given.append(jnp.where(upper, low, high))
    taken = [lax.ppermute(block, "section", mirror) for block in given]
    if short:
        kept_first = shift(kept[0], "expert", n_expert, 1)
        *held, taken[0], kept_first = lax.optimization_barrier((*acts, taken[0], kept_first))
        mirror_acts = [lax.ppermute(group, "section", mirror) for group in held]
        both = jnp.concatenate([kept[0], taken[0]])
        taken_first = shift(taken[0], "expert", n_expert, 1)
        back = shift(both, "expert", n_expert, 3)
        both, taken_first, back, mirror_acts[0], taken[1] = lax.optimization_barrier(
            (both, taken_first, back, mirror_acts[0], taken[1])
        )
        chosen = jnp.where(expert == 2, jnp.concatenate([kept_first, taken_first]), jnp.where(expert == 1, back, both))
        passed = lax.ppermute(chosen, "expert", [(0, 2), (2, 3), (3, 1), (1, 0)])
        passed, mirror_acts[1] = lax.optimization_barrier((passed, mirror_acts[1]))
        later = repeat([kept[1], taken[1]], chosen, n_expert)
        later, passed = lax.optimization_barrier((later, passed))
        later = lax.all_to_all(later, "expert", split_axis=0, concat_axis=0, tiled=True)
        cots = [[block[None] for block in (both, kept_first, taken_first, passed, back)], [later]]
        layouts = [[(0, 0), (1, 0), (1, 1), (2, 0), (3, 0)], [(None, 0)]]
    else:
        mirror_acts = [lax.ppermute(group, "section", mirror) for group in acts]
        cots = [[lax.all_gather(jnp.concatenate([a, b]), "expert")] for a, b in zip(kept, taken)]
        layouts = [[(None, 0)]] * len(cots)

    out = None
    for c, (offset, span) in enumerate(zip(offsets, widths)):
        pieces = [None] * n_section
        for g, masks in enumerate(groups):
            sums = list(product(acts[g], mirror_acts[g], cots[c], layouts[c], tokens, span // 3 if span % 384 == 0 else span))
            for mask, rows in zip(masks, sums):
                pieces[mask] = rows
                if mask:
                    pieces[mask] = lax.ppermute(rows, "section", [(i, i ^ mask) for i in range(n_section)])
        if c == 0:
            sent = [1, near[0], near[1], n_section - 2, n_section - 1]
            early, cots[c + 1] = lax.optimization_barrier(([pieces[mask] for mask in sent], cots[c + 1]))
            for mask, rows in zip(sent, early):
                pieces[mask] = rows
        out = join(pieces, offset, half_width, out)
    return out


def solution(mesh):
    return jax.shard_map(
        local,
        mesh=mesh,
        in_specs=(
            P("section", "expert", None),
            P("section", "expert", None),
            P("section", "expert", None),
            P("section", "expert", None, None, None),
        ),
        out_specs=P(None, "expert", "section", None),
        check_vma=False,
    )
```

time: 162 us -> 157 us (0.969)
  starting transfers between devices: 39.6 us -> 28.9 us
  waiting for transfers between devices: 75 us -> 81.7 us
  local copies, waits for them, and re-layouts: 4.89 us -> 3.13 us
    ppermute x4 -> x3, starting transfers between devices: 9.31 us -> 2.78 us  [the longest x2 2.33 us: local(): taken = [lax.ppermute(block, 'section', mirror) for block in given]]
    ppermute x7 -> x6, waiting for transfers between devices: 8.26 us -> 2.15 us  [shift(): lax.ppermute(block, axis, [(i, (i + step) % size) for i in range(size)])]
    ppermute x2, waiting for transfers between devices: 6.08 us -> 11.3 us  [local(): mirror_acts = [lax.ppermute(group, 'section', mirror) for group in held]]
    all_to_all x1, waiting for transfers between devices: 0.01 us -> 4.39 us  [local(): lax.all_to_all(later, 'expert', split_axis=0, concat_axis=0, tiled=True)]
    ppermute x4 -> x3, waiting for transfers between devices: 18.7 us -> 22.6 us  [the longest x2 20.6 us: local(): taken = [lax.ppermute(block, 'section', mirror) for block in given]]
    ppermute x14, starting transfers between devices: 12.3 us -> 9.61 us  [local(): lax.ppermute(rows, 'section', [(i, i ^ mask) for i in range(n_section)])]
    ppermute x7 -> x6, starting transfers between devices: 12.3 us -> 10.6 us  [shift(): lax.ppermute(block, axis, [(i, (i + step) % size) for i in range(size)])]
    pallas_call x4 -> x5, Pallas kernels: 23.9 us -> 24.6 us  [the longest x4 21.8 us: product(): pl.pallas_call(partial(product_kernel, tokens=tokens, layout=layout), gri...]
  transfers between devices with their start and end apart: 28 -> 26, of which waited for: 13 -> 11; matrix products, arithmetic and copies ran while one was open for 4% -> 4% of each run, Pallas kernels for 20% -> 20%
where the time goes in v2:
time: 157 us; the launch traced here: 156 us
  waiting for transfers between devices  81.7 us (52%)
  Pallas kernels  35 us (22%)
  starting transfers between devices  28.9 us (18%)
  other arithmetic  7.23 us (5%)
  local copies, waits for them, and re-layouts  3.13 us (2%)
    ppermute x14, waiting for transfers between devices, local(): lax.ppermute(rows, 'section', [(i, i ^ mask) for i in range(n_section)])  41.2 us
    pallas_call x4, Pallas kernels, product(): pl.pallas_call(partial(product_kernel, tokens=tokens, layout=layout), gri...  21.8 us
    ppermute x2, waiting for transfers between devices, local(): taken = [lax.ppermute(block, 'section', mirror) for block in given]  20.6 us
    ppermute x2, waiting for transfers between devices, local(): mirror_acts = [lax.ppermute(group, 'section', mirror) for group in held]  11.3 us
    ppermute x6, starting transfers between devices, shift(): lax.ppermute(block, axis, [(i, (i + step) % size) for i in range(size)])  10.6 us
    ppermute x14, starting transfers between devices, local(): lax.ppermute(rows, 'section', [(i, i ^ mask) for i in range(n_section)])  9.61 us
    pallas_call x2, Pallas kernels, join(): pl.pallas_call(partial(join_kernel, sections=sections, offset=offset), in...  7.09 us
    all_to_all x1, waiting for transfers between devices, local(): lax.all_to_all(later, 'expert', split_axis=0, concat_axis=0, tiled=True)  4.39 us
  transfers between devices with their start and end apart: 26, of which 11 were waited for; matrix products, arithmetic and copies ran while one was open for 4% of the time, Pallas kernels for 20%

profile of v2, /device:TPU:0, one launch (start us, length us, event | category | flops | bytes accessed | tf_op | source)
XLA Modules:
  0.0 156.2 jit_solution(16059857941448619584)
XLA Ops:
  0.0 0.7 convert_bitcast_fusion
  0.7 0.7 pad_maximum_fusion.2
  1.4 5.0 %collective-permute-start.2 = (f32[512]{0:T(512)S(1)}, f32[512]{0:T(512)S(1)}, u32[]{:S(2)}, u32[]{:S(2)}) collective-permute-start(f32[512]{0:T(512)S(1)} %get-tuple-element.84), channel_id=1, source_target_pairs={{0,3},{1,0},{2,1},{3,2},{4,7},{5,4},{6,5},{7,6},{8,11},{9,8},{10,9... | collective-permute-start | bytes 6152 | tf_op jit(solution)/shard_map/ppermute | solution.py:139
  6.4 1.0 collective-permute-start
  7.4 1.1 broadcast_select_fusion.1
  8.5 1.1 collective-permute-start.3
  9.7 2.5 %collective-permute-start.4 = (bf16[128,1152]{1,0:T(8,128)(2,1)S(1)}, bf16[128,1152]{1,0:T(8,128)(2,1)S(1)}, u32[]{:S(2)}, u32[]{:S(2)}) collective-permute-start(bf16[128,1152]{1,0:T(8,128)(2,1)S(1)} %get-tuple-element.81), channel_id=1, source_target_pairs={{0,1},{1,2},{2,3},{3,0},{4,5},{5,6},{6,7},{7,4},{8,9},{9,10},{10,1... | collective-permute-start | bytes 884744 | tf_op jit(solution)/shard_map/ppermute | solution.py:139
  12.1 0.6 pad_maximum_fusion.1.meta_ref
  12.8 3.4 %shard_map.46 = (bf16[4,192,512]{2,1,0:T(8,128)(2,1)}, bf16[4,192,512]{2,1,0:T(8,128)(2,1)}) custom-call(f32[4,512]{1,0:T(4,128)} %pad_maximum_fusion.1.meta_ref, bf16[2,4,64,1536]{3,2,1,0:T(8,128)(2,1)} %bitcast.32), custom_call_target="tpu_custom_call" | custom-call | flops 99999997952 | bytes 1000000 | tf_op jit(solution)/shard_map/pallas_call | solution.py:57
  16.1 2.6 %collective-permute-done.3 = bf16[128,1152]{1,0:T(8,128)(2,1)S(1)} collective-permute-done((bf16[128,1152]{1,0:T(8,128)(2,1)S(1)}, bf16[128,1152]{1,0:T(8,128)(2,1)S(1)}, u32[]{:S(2)}, u32[]{:S(2)}) %collective-permute-start.3) | collective-permute-done | bytes 294944 | tf_op jit(solution)/shard_map/ppermute | solution.py:195
  18.7 2.1 %collective-permute-done.4 = bf16[128,1152]{1,0:T(8,128)(2,1)S(1)} collective-permute-done((bf16[128,1152]{1,0:T(8,128)(2,1)S(1)}, bf16[128,1152]{1,0:T(8,128)(2,1)S(1)}, u32[]{:S(2)}, u32[]{:S(2)}) %collective-permute-start.4) | collective-permute-done | bytes 294944 | tf_op jit(solution)/shard_map/ppermute | solution.py:139
  20.9 0.9 collective-permute-start.7
  21.8 1.1 collective-permute-start.6
  22.9 1.0 collective-permute-start.5
  23.9 1.9 %broadcast_select_fusion.2 = (bf16[128,896]{1,0:T(8,128)(2,1)}, bf16[128,896]{1,0:T(8,128)(2,1)}) fusion(pred[]{:T(512)S(6)} %ge.3, bf16[128,4096]{1,0:T(8,128)(2,1)} %bitcast.26), kind=kLoop, calls=%fused_computation.4 | loop fusion | flops 229376 | bytes 917505 | tf_op jit(solution)/shard_map/jit(_where)/select_n | solution.py:193
  25.7 1.2 collective-permute-start.8
  26.9 1.4 collective-permute-start.10
  28.4 18.1 %collective-permute-done.8.refs_1_ = bf16[128,896]{1,0:T(8,128)(2,1)} collective-permute-done((bf16[128,896]{1,0:T(8,128)(2,1)}, bf16[128,896]{1,0:T(8,128)(2,1)}, u32[]{:S(2)}, u32[]{:S(2)}) %collective-permute-start.8) | collective-permute-done | bytes 229408 | tf_op jit(solution)/shard_map/ppermute | solution.py:195
  46.5 2.2 %maximum_select_fusion.refs_2_ = bf16[256,1152]{1,0:T(8,128)(2,1)} fusion(bf16[128,1152]{1,0:T(8,128)(2,1)} %collective-permute-done.5, bf16[128,1152]{1,0:T(8,128)(2,1)S(1)} %collective-permute-done.4, bf16[256,1152]{1,0:T(8,128)(2,1)S(1)} %collective-permute-done.6, bf16[256,1152]{1,0:T(8,128)(2,1)S(1)} %pad_maximum_fusion, pred[]{:T(512)S(6)} %eq.7, pred[]{:T(512)S(6)} %eq.6), kind=kLoop, calls=%fused_computation.1 | loop fusion | flops 1769472 | bytes 2359298 | tf_op jit(solution)/shard_map/jit(_where)/select_n | solution.py:206
  48.7 0.4 collective-permute-start.9
  49.2 2.8 %shard_map.47 = bf16[4,256,896]{2,1,0:T(8,128)(2,1)} custom-call(bf16[128,896]{1,0:T(8,128)(2,1)} %get-tuple-element.79.refs_0_, bf16[128,896]{1,0:T(8,128)(2,1)} %collective-permute-done.8.refs_1_, bf16[256,1152]{1,0:T(8,128)(2,1)} %maximum_select_fusion.refs_2_), custom_call_target="tpu_custom_call" | custom-call | flops 99999997952 | bytes 1000000 | tf_op jit(solution)/shard_map/pallas_call | solution.py:156
  52.0 11.3 %collective-permute-done.10.mirror_ref = bf16[4,192,512]{2,1,0:T(8,128)(2,1)} collective-permute-done((bf16[4,192,512]{2,1,0:T(8,128)(2,1)S(1)}, bf16[4,192,512]{2,1,0:T(8,128)(2,1)}, u32[]{:S(2)}, u32[]{:S(2)}) %collective-permute-start.10) | collective-permute-done | bytes 786464 | tf_op jit(solution)/shard_map/ppermute | solution.py:199
  63.3 2.0 %collective-permute-done.9 = bf16[256,1152]{1,0:T(8,128)(2,1)} collective-permute-done((bf16[256,1152]{1,0:T(8,128)(2,1)}, bf16[256,1152]{1,0:T(8,128)(2,1)}, u32[]{:S(2)}, u32[]{:S(2)}) %collective-permute-start.9) | collective-permute-done | bytes 589856 | tf_op jit(solution)/shard_map/ppermute | solution.py:207
  65.2 3.6 %all-to-all-start = ((bf16[4,256,896]{2,1,0:T(8,128)(2,1)}), bf16[4,256,896]{2,1,0:T(8,128)(2,1)S(1)}, u32[]{:S(2)}, u32[]{:S(2)}) async-start(bf16[4,256,896]{2,1,0:T(8,128)(2,1)} %shard_map.47), calls=%async_computation | async-start | bytes 3670016 | tf_op jit(solution)/shard_map/all_to_all | solution.py:211
  68.8 6.1 %shard_map.49 = (bf16[192,1152]{1,0:T(8,128)(2,1)}, bf16[192,1152]{1,0:T(8,128)(2,1)}, bf16[192,1152]{1,0:T(8,128)(2,1)}, bf16[192,1152]{1,0:T(8,128)(2,1)}) custom-call(bf16[4,192,512]{2,1,0:T(8,128)(2,1)} %get-tuple-element.52.own_ref, bf16[4,192,512]{2,1,0:T(8,128)(2,1)} %collective-permute-done.10.mirror_ref, bf16[1,256,1152]{2,1,0:T(8,128)(2,1)} %bitcast.19, ...), custom_call_target="tpu_custom_call" | custom-call | flops 1000000 | bytes 1000 | tf_op jit(solution)/shard_map/pallas_call | solution.py:91
  75.0 0.6 collective-permute-start.12
  75.6 1.0 collective-permute-start.13
  76.6 6.1 %shard_map.48 = (bf16[192,1152]{1,0:T(8,128)(2,1)}, bf16[192,1152]{1,0:T(8,128)(2,1)}, bf16[192,1152]{1,0:T(8,128)(2,1)}, bf16[192,1152]{1,0:T(8,128)(2,1)}) custom-call(bf16[4,192,512]{2,1,0:T(8,128)(2,1)} %get-tuple-element.45.own_ref, bf16[4,192,512]{2,1,0:T(8,128)(2,1)} %copy-done.3, bf16[1,256,1152]{2,1,0:T(8,128)(2,1)} %bitcast.20, ...), custom_call_target="tpu_custom_call" | custom-call | flops 1000000 | bytes 1000 | tf_op jit(solution)/shard_map/pallas_call | solution.py:91
  82.7 2.0 %collective-permute-start.14 = (bf16[192,1152]{1,0:T(8,128)(2,1)}, bf16[192,1152]{1,0:T(8,128)(2,1)S(1)}, u32[]{:S(2)}, u32[]{:S(2)}) collective-permute-start(bf16[192,1152]{1,0:T(8,128)(2,1)} %get-tuple-element.59), channel_id=1, source_target_pairs={{0,24},{4,28},{8,16},{12,20},{16,8},{20,12},{24,0},{28,4},{1,25},{... | collective-permute-start | bytes 1327112 | tf_op jit(solution)/shard_map/ppermute | solution.py:227
  84.8 0.7 collective-permute-start.15
  85.5 2.7 %collective-permute-done.12.refs_2_ = bf16[192,1152]{1,0:T(8,128)(2,1)S(1)} collective-permute-done((bf16[192,1152]{1,0:T(8,128)(2,1)}, bf16[192,1152]{1,0:T(8,128)(2,1)S(1)}, u32[]{:S(2)}, u32[]{:S(2)}) %collective-permute-start.12) | collective-permute-done | bytes 442400 | tf_op jit(solution)/shard_map/ppermute | solution.py:227
  88.2 18.4 %collective-permute-done.13.refs_4_ = bf16[192,1152]{1,0:T(8,128)(2,1)S(1)} collective-permute-done((bf16[192,1152]{1,0:T(8,128)(2,1)}, bf16[192,1152]{1,0:T(8,128)(2,1)S(1)}, u32[]{:S(2)}, u32[]{:S(2)}) %collective-permute-start.13) | collective-permute-done | bytes 442400 | tf_op jit(solution)/shard_map/ppermute | solution.py:227
  106.7 0.8 copy-done.9
  107.5 4.4 %all-to-all-done.refs_0_ = bf16[4,256,896]{2,1,0:T(8,128)(2,1)S(1)} async-done(((bf16[4,256,896]{2,1,0:T(8,128)(2,1)}), bf16[4,256,896]{2,1,0:T(8,128)(2,1)S(1)}, u32[]{:S(2)}, u32[]{:S(2)}) %all-to-all-start) | async-done | bytes 1835040 | tf_op jit(solution)/shard_map/all_to_all | solution.py:211
  111.9 1.2 copy-done
  113.1 4.8 %shard_map.51 = (bf16[192,896]{1,0:T(8,128)(2,1)}, bf16[192,896]{1,0:T(8,128)(2,1)}, bf16[192,896]{1,0:T(8,128)(2,1)}, bf16[192,896]{1,0:T(8,128)(2,1)}) custom-call(bf16[4,192,512]{2,1,0:T(8,128)(2,1)} %get-tuple-element.52.own_ref, bf16[4,192,512]{2,1,0:T(8,128)(2,1)} %collective-permute-done.10.mirror_ref, bf16[4,256,896]{2,1,0:T(8,128)(2,1)} %copy-done), custom_call_target="tpu_custom_call" | custom-call | flops 1000000 | bytes 1000 | tf_op jit(solution)/shard_map/pallas_call | solution.py:91
  117.9 0.5 collective-permute-start.17
  118.5 0.3 collective-permute-start.19
  118.9 4.7 %shard_map.50 = (bf16[192,896]{1,0:T(8,128)(2,1)}, bf16[192,896]{1,0:T(8,128)(2,1)}, bf16[192,896]{1,0:T(8,128)(2,1)}, bf16[192,896]{1,0:T(8,128)(2,1)}) custom-call(bf16[4,192,512]{2,1,0:T(8,128)(2,1)} %get-tuple-element.45.own_ref, bf16[4,192,512]{2,1,0:T(8,128)(2,1)} %copy-done.3, bf16[4,256,896]{2,1,0:T(8,128)(2,1)} %copy-done), custom_call_target="tpu_custom_call" | custom-call | flops 1000000 | bytes 1000 | tf_op jit(solution)/shard_map/pallas_call | solution.py:91
  123.6 2.6 %collective-permute-start.20 = (bf16[192,896]{1,0:T(8,128)(2,1)S(1)}, bf16[192,896]{1,0:T(8,128)(2,1)S(1)}, u32[]{:S(2)}, u32[]{:S(2)}) collective-permute-start(bf16[192,896]{1,0:T(8,128)(2,1)S(1)} %copy-done.17), channel_id=1, source_target_pairs={{0,20},{4,16},{8,28},{12,24},{16,4},{20,0},{24,12},{28,8},{1,21},{... | collective-permute-start | bytes 1032200 | tf_op jit(solution)/shard_map/ppermute | solution.py:227
  126.3 2.9 %collective-permute-done.17.refs_2_ = bf16[192,896]{1,0:T(8,128)(2,1)S(1)} collective-permute-done((bf16[192,896]{1,0:T(8,128)(2,1)}, bf16[192,896]{1,0:T(8,128)(2,1)S(1)}, u32[]{:S(2)}, u32[]{:S(2)}) %collective-permute-start.17) | collective-permute-done | bytes 344096 | tf_op jit(solution)/shard_map/ppermute | solution.py:227
  129.2 5.5 %collective-permute-done.18.refs_3_ = bf16[192,896]{1,0:T(8,128)(2,1)S(1)} collective-permute-done((bf16[192,896]{1,0:T(8,128)(2,1)}, bf16[192,896]{1,0:T(8,128)(2,1)S(1)}, u32[]{:S(2)}, u32[]{:S(2)}) %collective-permute-start.18) | collective-permute-done | bytes 344096 | tf_op jit(solution)/shard_map/ppermute | solution.py:227
  134.7 1.6 %collective-permute-start.22 = (bf16[192,896]{1,0:T(8,128)(2,1)}, bf16[192,896]{1,0:T(8,128)(2,1)S(1)}, u32[]{:S(2)}, u32[]{:S(2)}) collective-permute-start(bf16[192,896]{1,0:T(8,128)(2,1)} %get-tuple-element.70), channel_id=1, source_target_pairs={{0,28},{4,24},{8,20},{12,16},{16,12},{20,8},{24,4},{28,0},{1,29},{... | collective-permute-start | bytes 1032200 | tf_op jit(solution)/shard_map/ppermute | solution.py:227
  136.3 3.8 %shard_map.52.refs_8_ = bf16[4,1,192,4096]{3,2,1,0:T(8,128)(2,1)} custom-call(bf16[192,1152]{1,0:T(8,128)(2,1)} %get-tuple-element.71.refs_0_, bf16[192,1152]{1,0:T(8,128)(2,1)} %copy-done.8, bf16[192,1152]{1,0:T(8,128)(2,1)} %copy-done.6, bf16[192,1152]{1,0:T(8,128)(2,1)} %collective-permute-done.23.refs_3_, bf16[192,1152]{1,0:T(8,128)(2,1)} %copy-done.7, ...), custom_call_target="tpu_custom_call" | custom-call | tf_op jit(solution)/shard_map/pallas_call | solution.py:127
  140.1 11.7 %collective-permute-done.20.refs_5_ = bf16[192,896]{1,0:T(8,128)(2,1)S(1)} collective-permute-done((bf16[192,896]{1,0:T(8,128)(2,1)S(1)}, bf16[192,896]{1,0:T(8,128)(2,1)S(1)}, u32[]{:S(2)}, u32[]{:S(2)}) %collective-permute-start.20) | collective-permute-done | bytes 344096 | tf_op jit(solution)/shard_map/ppermute | solution.py:227
  151.8 0.7 copy-done.13
  152.6 0.1 copy-done.15
  152.9 3.3 %shard_map.53 = bf16[4,1,192,4096]{3,2,1,0:T(8,128)(2,1)} custom-call(bf16[192,896]{1,0:T(8,128)(2,1)} %get-tuple-element.63.refs_0_, bf16[192,896]{1,0:T(8,128)(2,1)} %copy-done.14, bf16[192,896]{1,0:T(8,128)(2,1)} %copy-done.10, bf16[192,896]{1,0:T(8,128)(2,1)} %copy-done.11, bf16[192,896]{1,0:T(8,128)(2,1)} %copy-done.12, ...), custom_call_target="tpu_custom_call", output_to_operand_aliasing={{}: (8, {})} | custom-call | tf_op jit(solution)/shard_map/pallas_call | solution.py:127
  (55 shorter events, 0.5 us)
Async XLA Ops:
  1.4 10.8 %collective-permute-start.2 = (f32[512]{0:T(512)S(1)}, f32[512]{0:T(512)S(1)}, u32[]{:S(2)}, u32[]{:S(2)}) collective-permute-start(f32[512]{0:T(512)S(1)} %get-tuple-element.84), channel_id=1, source_target_pairs={{0,3},{1,0},{2,1},{3,2},{4,7},{5,4},{6,5},{7,6},{8,11},{9,8},{10,9... | collective-permute-start | bytes 6152 | tf_op jit(solution)/shard_map/ppermute | solution.py:139
  6.4 5.7 %collective-permute-start.1 = (f32[512]{0:T(512)S(1)}, f32[512]{0:T(512)S(1)}, u32[]{:S(2)}, u32[]{:S(2)}) collective-permute-start(f32[512]{0:T(512)S(1)} %get-tuple-element.84), channel_id=1, source_target_pairs={{0,2},{1,3},{2,0},{3,1},{4,6},{5,7},{6,4},{7,5},{8,10},{9,11},{10,... | collective-permute-start | bytes 6152 | tf_op jit(solution)/shard_map/ppermute | solution.py:139
  6.4 5.7 %collective-permute-start = (f32[512]{0:T(512)S(1)}, f32[512]{0:T(512)S(1)}, u32[]{:S(2)}, u32[]{:S(2)}) collective-permute-start(f32[512]{0:T(512)S(1)} %get-tuple-element.84), channel_id=1, source_target_pairs={{0,1},{1,2},{2,3},{3,0},{4,5},{5,6},{6,7},{7,4},{8,9},{9,10},{10,1... | collective-permute-start | bytes 6152 | tf_op jit(solution)/shard_map/ppermute | solution.py:139
  8.5 10.2 %collective-permute-start.3 = (bf16[128,1152]{1,0:T(8,128)(2,1)S(1)}, bf16[128,1152]{1,0:T(8,128)(2,1)S(1)}, u32[]{:S(2)}, u32[]{:S(2)}) collective-permute-start(bf16[128,1152]{1,0:T(8,128)(2,1)S(1)} %get-tuple-element.82), channel_id=1, source_target_pairs={{0,28},{4,24},{8,20},{12,16},{16,12},{20,8},{24,4},{28,0},{1,29},{... | collective-permute-start | bytes 884744 | tf_op jit(solution)/shard_map/ppermute | solution.py:195
  9.7 11.2 %collective-permute-start.4 = (bf16[128,1152]{1,0:T(8,128)(2,1)S(1)}, bf16[128,1152]{1,0:T(8,128)(2,1)S(1)}, u32[]{:S(2)}, u32[]{:S(2)}) collective-permute-start(bf16[128,1152]{1,0:T(8,128)(2,1)S(1)} %get-tuple-element.81), channel_id=1, source_target_pairs={{0,1},{1,2},{2,3},{3,0},{4,5},{5,6},{6,7},{7,4},{8,9},{9,10},{10,1... | collective-permute-start | bytes 884744 | tf_op jit(solution)/shard_map/ppermute | solution.py:139
  16.1 10.8 %copy-start.4 = (bf16[4,192,512]{2,1,0:T(8,128)(2,1)S(1)}, bf16[4,192,512]{2,1,0:T(8,128)(2,1)}, u32[]{:S(2)}) copy-start(bf16[4,192,512]{2,1,0:T(8,128)(2,1)} %get-tuple-element.52.own_ref) | copy-start | bytes 2359300
  20.9 27.8 %copy-start.5 = (bf16[128,1152]{1,0:T(8,128)(2,1)}, bf16[128,1152]{1,0:T(8,128)(2,1)S(1)}, u32[]{:S(2)}) copy-start(bf16[128,1152]{1,0:T(8,128)(2,1)S(1)} %collective-permute-done.4) | copy-start | bytes 884740
  20.9 25.6 %collective-permute-start.7 = (bf16[4,192,512]{2,1,0:T(8,128)(2,1)}, bf16[4,192,512]{2,1,0:T(8,128)(2,1)S(1)}, u32[]{:S(2)}, u32[]{:S(2)}) collective-permute-start(bf16[4,192,512]{2,1,0:T(8,128)(2,1)} %get-tuple-element.45.own_ref), channel_id=1, source_target_pairs={{0,28},{4,24},{8,20},{12,16},{16,12},{20,8},{24,4},{28,0},{1,29},{... | collective-permute-start | bytes 2359304 | tf_op jit(solution)/shard_map/ppermute | solution.py:199
  21.8 26.9 %copy-start.1 = (bf16[256,1152]{1,0:T(8,128)(2,1)}, bf16[256,1152]{1,0:T(8,128)(2,1)S(1)}, u32[]{:S(2)}) copy-start(bf16[256,1152]{1,0:T(8,128)(2,1)S(1)} %pad_maximum_fusion) | copy-start | bytes 1769476
  21.8 24.6 %collective-permute-start.6 = (bf16[256,1152]{1,0:T(8,128)(2,1)S(1)}, bf16[256,1152]{1,0:T(8,128)(2,1)S(1)}, u32[]{:S(2)}, u32[]{:S(2)}) collective-permute-start(bf16[256,1152]{1,0:T(8,128)(2,1)S(1)} %pad_maximum_fusion), channel_id=1, source_target_pairs={{0,3},{1,0},{2,1},{3,2},{4,7},{5,4},{6,5},{7,6},{8,11},{9,8},{10,9... | collective-permute-start | bytes 1769480 | tf_op jit(solution)/shard_map/ppermute | solution.py:139
  22.9 23.5 %collective-permute-start.5 = (bf16[128,1152]{1,0:T(8,128)(2,1)S(1)}, bf16[128,1152]{1,0:T(8,128)(2,1)}, u32[]{:S(2)}, u32[]{:S(2)}) collective-permute-start(bf16[128,1152]{1,0:T(8,128)(2,1)S(1)} %collective-permute-done.3), channel_id=1, source_target_pairs={{0,1},{1,2},{2,3},{3,0},{4,5},{5,6},{6,7},{7,4},{8,9},{9,10},{10,1... | collective-permute-start | bytes 884744 | tf_op jit(solution)/shard_map/ppermute | solution.py:139
  25.7 20.7 %collective-permute-start.8 = (bf16[128,896]{1,0:T(8,128)(2,1)}, bf16[128,896]{1,0:T(8,128)(2,1)}, u32[]{:S(2)}, u32[]{:S(2)}) collective-permute-start(bf16[128,896]{1,0:T(8,128)(2,1)} %get-tuple-element.80), channel_id=1, source_target_pairs={{0,28},{4,24},{8,20},{12,16},{16,12},{20,8},{24,4},{28,0},{1,29},{... | collective-permute-start | bytes 688136 | tf_op jit(solution)/shard_map/ppermute | solution.py:195
  26.9 36.3 %collective-permute-start.10 = (bf16[4,192,512]{2,1,0:T(8,128)(2,1)S(1)}, bf16[4,192,512]{2,1,0:T(8,128)(2,1)}, u32[]{:S(2)}, u32[]{:S(2)}) collective-permute-start(bf16[4,192,512]{2,1,0:T(8,128)(2,1)S(1)} %copy-done.4), channel_id=1, source_target_pairs={{0,28},{4,24},{8,20},{12,16},{16,12},{20,8},{24,4},{28,0},{1,29},{... | collective-permute-start | bytes 2359304 | tf_op jit(solution)/shard_map/ppermute | solution.py:199
  46.4 2.3 %copy-start.2 = (bf16[256,1152]{1,0:T(8,128)(2,1)}, bf16[256,1152]{1,0:T(8,128)(2,1)S(1)}, u32[]{:S(2)}) copy-start(bf16[256,1152]{1,0:T(8,128)(2,1)S(1)} %collective-permute-done.6) | copy-start | bytes 1769476
  46.4 2.3 %copy-start.3 = (bf16[4,192,512]{2,1,0:T(8,128)(2,1)}, bf16[4,192,512]{2,1,0:T(8,128)(2,1)S(1)}, u32[]{:S(2)}) copy-start(bf16[4,192,512]{2,1,0:T(8,128)(2,1)S(1)} %collective-permute-done.7.mirror_ref) | copy-start | bytes 2359300
  48.7 16.5 %collective-permute-start.9 = (bf16[256,1152]{1,0:T(8,128)(2,1)}, bf16[256,1152]{1,0:T(8,128)(2,1)}, u32[]{:S(2)}, u32[]{:S(2)}) collective-permute-start(bf16[256,1152]{1,0:T(8,128)(2,1)} %maximum_select_fusion.refs_2_), channel_id=1, source_target_pairs={{0,2},{2,3},{3,1},{1,0},{4,6},{6,7},{7,5},{5,4},{8,10},{10,11},{11... | collective-permute-start | bytes 1769480 | tf_op jit(solution)/shard_map/ppermute | solution.py:207
  65.2 46.6 %all-to-all-start = ((bf16[4,256,896]{2,1,0:T(8,128)(2,1)}), bf16[4,256,896]{2,1,0:T(8,128)(2,1)S(1)}, u32[]{:S(2)}, u32[]{:S(2)}) async-start(bf16[4,256,896]{2,1,0:T(8,128)(2,1)} %shard_map.47), calls=%async_computation | async-start | bytes 3670016 | tf_op jit(solution)/shard_map/all_to_all | solution.py:211
  75.0 13.2 %collective-permute-start.12 = (bf16[192,1152]{1,0:T(8,128)(2,1)}, bf16[192,1152]{1,0:T(8,128)(2,1)S(1)}, u32[]{:S(2)}, u32[]{:S(2)}) collective-permute-start(bf16[192,1152]{1,0:T(8,128)(2,1)} %get-tuple-element.57), channel_id=1, source_target_pairs={{0,8},{4,12},{8,0},{12,4},{16,24},{20,28},{24,16},{28,20},{1,9},{5... | collective-permute-start | bytes 1327112 | tf_op jit(solution)/shard_map/ppermute | solution.py:227
  75.6 31.0 %collective-permute-start.13 = (bf16[192,1152]{1,0:T(8,128)(2,1)}, bf16[192,1152]{1,0:T(8,128)(2,1)S(1)}, u32[]{:S(2)}, u32[]{:S(2)}) collective-permute-start(bf16[192,1152]{1,0:T(8,128)(2,1)} %get-tuple-element.58), channel_id=1, source_target_pairs={{0,16},{4,20},{8,24},{12,28},{16,0},{20,4},{24,8},{28,12},{1,17},{... | collective-permute-start | bytes 1327112 | tf_op jit(solution)/shard_map/ppermute | solution.py:227
  82.7 24.0 %collective-permute-start.11 = (bf16[192,1152]{1,0:T(8,128)(2,1)}, bf16[192,1152]{1,0:T(8,128)(2,1)S(1)}, u32[]{:S(2)}, u32[]{:S(2)}) collective-permute-start(bf16[192,1152]{1,0:T(8,128)(2,1)} %get-tuple-element.55), channel_id=1, source_target_pairs={{0,4},{4,0},{8,12},{12,8},{16,20},{20,16},{24,28},{28,24},{1,5},{5... | collective-permute-start | bytes 1327112 | tf_op jit(solution)/shard_map/ppermute | solution.py:227
  82.7 23.9 %collective-permute-start.14 = (bf16[192,1152]{1,0:T(8,128)(2,1)}, bf16[192,1152]{1,0:T(8,128)(2,1)S(1)}, u32[]{:S(2)}, u32[]{:S(2)}) collective-permute-start(bf16[192,1152]{1,0:T(8,128)(2,1)} %get-tuple-element.59), channel_id=1, source_target_pairs={{0,24},{4,28},{8,16},{12,20},{16,8},{20,12},{24,0},{28,4},{1,25},{... | collective-permute-start | bytes 1327112 | tf_op jit(solution)/shard_map/ppermute | solution.py:227
  84.8 22.7 %collective-permute-start.15 = (bf16[192,1152]{1,0:T(8,128)(2,1)}, bf16[192,1152]{1,0:T(8,128)(2,1)}, u32[]{:S(2)}, u32[]{:S(2)}) collective-permute-start(bf16[192,1152]{1,0:T(8,128)(2,1)} %get-tuple-element.60), channel_id=1, source_target_pairs={{0,28},{4,24},{8,20},{12,16},{16,12},{20,8},{24,4},{28,0},{1,29},{... | collective-permute-start | bytes 1327112 | tf_op jit(solution)/shard_map/ppermute | solution.py:227
  88.2 48.1 %copy-start.6 = (bf16[192,1152]{1,0:T(8,128)(2,1)}, bf16[192,1152]{1,0:T(8,128)(2,1)S(1)}, u32[]{:S(2)}) copy-start(bf16[192,1152]{1,0:T(8,128)(2,1)S(1)} %collective-permute-done.12.refs_2_) | copy-start | bytes 1327108
  88.2 35.4 %collective-permute-start.23 = (bf16[192,1152]{1,0:T(8,128)(2,1)}, bf16[192,1152]{1,0:T(8,128)(2,1)}, u32[]{:S(2)}, u32[]{:S(2)}) collective-permute-start(bf16[192,1152]{1,0:T(8,128)(2,1)} %get-tuple-element.74), channel_id=1, source_target_pairs={{0,12},{4,8},{8,4},{12,0},{16,28},{20,24},{24,20},{28,16},{1,13},{... | collective-permute-start | bytes 1327112 | tf_op jit(solution)/shard_map/ppermute | solution.py:227
  106.6 29.7 %copy-start.7 = (bf16[192,1152]{1,0:T(8,128)(2,1)}, bf16[192,1152]{1,0:T(8,128)(2,1)S(1)}, u32[]{:S(2)}) copy-start(bf16[192,1152]{1,0:T(8,128)(2,1)S(1)} %collective-permute-done.13.refs_4_) | copy-start | bytes 1327108
  106.6 19.6 %collective-permute-start.24 = (bf16[192,1152]{1,0:T(8,128)(2,1)}, bf16[192,1152]{1,0:T(8,128)(2,1)}, u32[]{:S(2)}, u32[]{:S(2)}) collective-permute-start(bf16[192,1152]{1,0:T(8,128)(2,1)} %get-tuple-element.76), channel_id=1, source_target_pairs={{0,20},{4,16},{8,28},{12,24},{16,4},{20,0},{24,12},{28,8},{1,21},{... | collective-permute-start | bytes 1327112 | tf_op jit(solution)/shard_map/ppermute | solution.py:227
  106.6 29.7 %copy-start.8 = (bf16[192,1152]{1,0:T(8,128)(2,1)}, bf16[192,1152]{1,0:T(8,128)(2,1)S(1)}, u32[]{:S(2)}) copy-start(bf16[192,1152]{1,0:T(8,128)(2,1)S(1)} %collective-permute-done.11.refs_1_) | copy-start | bytes 1327108
  106.6 0.8 copy-start.9
  111.9 1.2 copy-start
  117.9 11.2 %collective-permute-start.17 = (bf16[192,896]{1,0:T(8,128)(2,1)}, bf16[192,896]{1,0:T(8,128)(2,1)S(1)}, u32[]{:S(2)}, u32[]{:S(2)}) collective-permute-start(bf16[192,896]{1,0:T(8,128)(2,1)} %get-tuple-element.65), channel_id=1, source_target_pairs={{0,8},{4,12},{8,0},{12,4},{16,24},{20,28},{24,16},{28,20},{1,9},{5... | collective-permute-start | bytes 1032200 | tf_op jit(solution)/shard_map/ppermute | solution.py:227
  118.5 16.2 %collective-permute-start.18 = (bf16[192,896]{1,0:T(8,128)(2,1)}, bf16[192,896]{1,0:T(8,128)(2,1)S(1)}, u32[]{:S(2)}, u32[]{:S(2)}) collective-permute-start(bf16[192,896]{1,0:T(8,128)(2,1)} %get-tuple-element.66), channel_id=1, source_target_pairs={{0,12},{4,8},{8,4},{12,0},{16,28},{20,24},{24,20},{28,16},{1,13},{... | collective-permute-start | bytes 1032200 | tf_op jit(solution)/shard_map/ppermute | solution.py:227
  118.5 5.1 %copy-start.17 = (bf16[192,896]{1,0:T(8,128)(2,1)S(1)}, bf16[192,896]{1,0:T(8,128)(2,1)}, u32[]{:S(2)}) copy-start(bf16[192,896]{1,0:T(8,128)(2,1)} %get-tuple-element.68) | copy-start | bytes 1032196
  118.5 21.6 %collective-permute-start.19 = (bf16[192,896]{1,0:T(8,128)(2,1)}, bf16[192,896]{1,0:T(8,128)(2,1)S(1)}, u32[]{:S(2)}, u32[]{:S(2)}) collective-permute-start(bf16[192,896]{1,0:T(8,128)(2,1)} %get-tuple-element.67), channel_id=1, source_target_pairs={{0,16},{4,20},{8,24},{12,28},{16,0},{20,4},{24,8},{28,12},{1,17},{... | collective-permute-start | bytes 1032200 | tf_op jit(solution)/shard_map/ppermute | solution.py:227
  123.6 28.2 %collective-permute-start.20 = (bf16[192,896]{1,0:T(8,128)(2,1)S(1)}, bf16[192,896]{1,0:T(8,128)(2,1)S(1)}, u32[]{:S(2)}, u32[]{:S(2)}) collective-permute-start(bf16[192,896]{1,0:T(8,128)(2,1)S(1)} %copy-done.17), channel_id=1, source_target_pairs={{0,20},{4,16},{8,28},{12,24},{16,4},{20,0},{24,12},{28,8},{1,21},{... | collective-permute-start | bytes 1032200 | tf_op jit(solution)/shard_map/ppermute | solution.py:227
  126.3 25.5 %collective-permute-start.16 = (bf16[192,896]{1,0:T(8,128)(2,1)}, bf16[192,896]{1,0:T(8,128)(2,1)S(1)}, u32[]{:S(2)}, u32[]{:S(2)}) collective-permute-start(bf16[192,896]{1,0:T(8,128)(2,1)} %get-tuple-element.64), channel_id=1, source_target_pairs={{0,4},{4,0},{8,12},{12,8},{16,20},{20,16},{24,28},{28,24},{1,5},{5... | collective-permute-start | bytes 1032200 | tf_op jit(solution)/shard_map/ppermute | solution.py:227
  129.2 10.9 %copy-start.10 = (bf16[192,896]{1,0:T(8,128)(2,1)}, bf16[192,896]{1,0:T(8,128)(2,1)S(1)}, u32[]{:S(2)}) copy-start(bf16[192,896]{1,0:T(8,128)(2,1)S(1)} %collective-permute-done.17.refs_2_) | copy-start | bytes 1032196
  129.2 22.6 %collective-permute-start.21 = (bf16[192,896]{1,0:T(8,128)(2,1)}, bf16[192,896]{1,0:T(8,128)(2,1)S(1)}, u32[]{:S(2)}, u32[]{:S(2)}) collective-permute-start(bf16[192,896]{1,0:T(8,128)(2,1)} %get-tuple-element.69), channel_id=1, source_target_pairs={{0,24},{4,28},{8,16},{12,20},{16,8},{20,12},{24,0},{28,4},{1,25},{... | collective-permute-start | bytes 1032200 | tf_op jit(solution)/shard_map/ppermute | solution.py:227
  134.7 5.4 %copy-start.11 = (bf16[192,896]{1,0:T(8,128)(2,1)}, bf16[192,896]{1,0:T(8,128)(2,1)S(1)}, u32[]{:S(2)}) copy-start(bf16[192,896]{1,0:T(8,128)(2,1)S(1)} %collective-permute-done.18.refs_3_) | copy-start | bytes 1032196
  134.7 17.1 %collective-permute-start.22 = (bf16[192,896]{1,0:T(8,128)(2,1)}, bf16[192,896]{1,0:T(8,128)(2,1)S(1)}, u32[]{:S(2)}, u32[]{:S(2)}) collective-permute-start(bf16[192,896]{1,0:T(8,128)(2,1)} %get-tuple-element.70), channel_id=1, source_target_pairs={{0,28},{4,24},{8,20},{12,16},{16,12},{20,8},{24,4},{28,0},{1,29},{... | collective-permute-start | bytes 1032200 | tf_op jit(solution)/shard_map/ppermute | solution.py:227
  140.1 11.7 %copy-start.12 = (bf16[192,896]{1,0:T(8,128)(2,1)}, bf16[192,896]{1,0:T(8,128)(2,1)S(1)}, u32[]{:S(2)}) copy-start(bf16[192,896]{1,0:T(8,128)(2,1)S(1)} %collective-permute-done.19.refs_4_) | copy-start | bytes 1032196
  151.8 0.7 copy-start.13
  151.8 0.8 copy-start.14
  151.8 1.0 copy-start.15
  151.8 1.0 copy-start.16

commit v3 on v2

--- a/solution.py
+++ b/solution.py
@@ -61,7 +61,7 @@
         out_shape=[jax.ShapeDtypeStruct((len(masks), rows, depth), jnp.bfloat16) for masks in groups],
         scratch_shapes=[pltpu.VMEM((sections, rows, depth), jnp.bfloat16)],
         compiler_params=pltpu.CompilerParams(vmem_limit_bytes=VMEM),
-        cost_estimate=LONG,
+        cost_estimate=SHORT,
     )(metas, hidden)
 
 
@@ -100,37 +100,40 @@
     )(own_acts, mirror_acts, *cots)
 
 
-def join_kernel(*refs, sections, offset):
-    pieces = refs[:sections]
+def tile_of(width):
+    return next((width // parts for parts in (3, 2) if width % (128 * parts) == 0), width)
+
+
+def join_kernel(*refs, masks, sections, offset):
+    pieces = refs[: len(masks)]
     out, sem = refs[-2:]
     section = lax.axis_index("section")
     width = pieces[0].shape[-1]
     copies = []
-    for mask, piece in enumerate(pieces):
+    for i, (mask, piece) in enumerate(zip(masks, pieces)):
         source = section ^ mask
         upper = (source >= sections // 2).astype(jnp.int32)
         pair = source + upper * (sections - 1 - 2 * source)
         column = pl.multiple_of(upper * (out.shape[-1] // 2) + offset, 128)
-        copies.append(pltpu.make_async_copy(piece, out.at[pair, 0, :, pl.ds(column, width)], sem.at[mask]))
+        copies.append(pltpu.make_async_copy(piece, out.at[pair, 0, :, pl.ds(column, width)], sem.at[i]))
     for copy in copies:
         copy.start()
     for copy in copies:
         copy.wait()
 
 
-def join(pieces, offset, half_width, out=None):
-    sections = len(pieces)
+def join(pieces, masks, sections, offset, half_width, out=None):
     rows = pieces[0].shape[0]
     shape = jax.ShapeDtypeStruct((sections // 2, 1, rows, 2 * half_width), jnp.bfloat16)
     first = out is None
     operands = tuple(pieces) if first else (*pieces, out)
     return pl.pallas_call(
-        partial(join_kernel, sections=sections, offset=offset),
-        in_specs=[pl.BlockSpec(memory_space=pltpu.VMEM)] * sections + [pl.BlockSpec(memory_space=pl.ANY)] * (not first),
+        partial(join_kernel, masks=masks, sections=sections, offset=offset),
+        in_specs=[pl.BlockSpec(memory_space=pltpu.VMEM)] * len(masks) + [pl.BlockSpec(memory_space=pl.ANY)] * (not first),
         out_specs=pl.BlockSpec(memory_space=pl.ANY),
         out_shape=shape,
-        scratch_shapes=[pltpu.SemaphoreType.DMA((sections,))],
-        input_output_aliases={} if first else {sections: 0},
+        scratch_shapes=[pltpu.SemaphoreType.DMA((len(masks),))],
+        input_output_aliases={} if first else {len(masks): 0},
         compiler_params=pltpu.CompilerParams(vmem_limit_bytes=VMEM),
     )(*operands)
 
@@ -141,6 +144,12 @@
 
 def ring(block, axis, size):
     return [block] + [shift(block, axis, size, step) for step in range(1, size)]
+
+
+def pass_on(own, first, back, axis):
+    me = lax.axis_index(axis)
+    chosen = jnp.where(me == 2, first, jnp.where(me == 1, back, own))
+    return lax.ppermute(chosen, axis, [(0, 2), (2, 3), (3, 1), (1, 0)])
 
 
 def repeat_kernel(*refs):
@@ -173,7 +182,7 @@
     tokens, width = cotangent.shape[1:]
     top = routes.shape[2]
     half_width = width // 2
-    widths = [half_width * 9 // 16, half_width * 7 // 16]
+    widths = [half_width * 5 // 8, half_width * 3 // 8]
     offsets = [sum(widths[:c]) for c in range(len(widths))]
     mirror = [(i, n_section - 1 - i) for i in range(n_section)]
     upper = section >= n_section // 2
@@ -192,25 +201,26 @@
         high = cot[:, half_width + offset : half_width + offset + span]
         kept.append(jnp.where(upper, high, low))
         given.append(jnp.where(upper, low, high))
-    taken = [lax.ppermute(block, "section", mirror) for block in given]
+    taken = lax.ppermute(jnp.concatenate(given, 1), "section", mirror)
+    taken = [taken[:, offset : offset + span] for offset, span in zip(offsets, widths)]
     if short:
         kept_first = shift(kept[0], "expert", n_expert, 1)
-        *held, taken[0], kept_first = lax.optimization_barrier((*acts, taken[0], kept_first))
+        *held, _ = lax.optimization_barrier((*acts, taken[0]))
         mirror_acts = [lax.ppermute(group, "section", mirror) for group in held]
-        both = jnp.concatenate([kept[0], taken[0]])
-        taken_first = shift(taken[0], "expert", n_expert, 1)
-        back = shift(both, "expert", n_expert, 3)
-        both, taken_first, back, mirror_acts[0], taken[1] = lax.optimization_barrier(
-            (both, taken_first, back, mirror_acts[0], taken[1])
+        kept_back = shift(kept[0], "expert", n_expert, 3)
+        kept_passed = pass_on(kept[0], kept_first, kept_back, "expert")
+        taken_first, taken_back = shift(taken[0], "expert", n_expert, 1), shift(taken[0], "expert", n_expert, 3)
+        taken_first, taken_back, mirror_acts[0] = lax.optimization_barrier((taken_first, taken_back, mirror_acts[0]))
+        taken_passed = pass_on(taken[0], taken_first, taken_back, "expert")
+        kept_passed, taken_passed, mirror_acts[1] = lax.optimization_barrier(
+            (kept_passed, taken_passed, mirror_acts[1])
         )
-        chosen = jnp.where(expert == 2, jnp.concatenate([kept_first, taken_first]), jnp.where(expert == 1, back, both))
-        passed = lax.ppermute(chosen, "expert", [(0, 2), (2, 3), (3, 1), (1, 0)])
-        passed, mirror_acts[1] = lax.optimization_barrier((passed, mirror_acts[1]))
-        later = repeat([kept[1], taken[1]], chosen, n_expert)
-        later, passed = lax.optimization_barrier((later, passed))
+        later = repeat([kept[1], taken[1]], taken_first, n_expert)
+        later, taken_passed = lax.optimization_barrier((later, taken_passed))
         later = lax.all_to_all(later, "expert", split_axis=0, concat_axis=0, tiled=True)
-        cots = [[block[None] for block in (both, kept_first, taken_first, passed, back)], [later]]
-        layouts = [[(0, 0), (1, 0), (1, 1), (2, 0), (3, 0)], [(None, 0)]]
+        blocks = [kept[0], kept_first, kept_passed, kept_back, taken[0], taken_first, taken_passed, taken_back]
+        cots = [[block[None] for block in blocks], [later]]
+        layouts = [[(step, replica) for replica in range(2) for step in range(n_expert)], [(None, 0)]]
     else:
         mirror_acts = [lax.ppermute(group, "section", mirror) for group in acts]
         cots = [[lax.all_gather(jnp.concatenate([a, b]), "expert")] for a, b in zip(kept, taken)]
@@ -220,17 +230,17 @@
     for c, (offset, span) in enumerate(zip(offsets, widths)):
         pieces = [None] * n_section
         for g, masks in enumerate(groups):
-            sums = list(product(acts[g], mirror_acts[g], cots[c], layouts[c], tokens, span // 3 if span % 384 == 0 else span))
+            sums = list(product(acts[g], mirror_acts[g], cots[c], layouts[c], tokens, tile_of(span)))
             for mask, rows in zip(masks, sums):
                 pieces[mask] = rows
                 if mask:
                     pieces[mask] = lax.ppermute(rows, "section", [(i, i ^ mask) for i in range(n_section)])
         if c == 0:
-            sent = [1, near[0], near[1], n_section - 2, n_section - 1]
+            sent = [1, near[0], near[1], n_section - 2]
             early, cots[c + 1] = lax.optimization_barrier(([pieces[mask] for mask in sent], cots[c + 1]))
             for mask, rows in zip(sent, early):
                 pieces[mask] = rows
-        out = join(pieces, offset, half_width, out)
+        out = join(pieces, list(range(n_section)), n_section, offset, half_width, out)
     return out
 
 

time: 157 us -> 147 us (0.936)
  waiting for transfers between devices: 81.7 us -> 58.8 us
  starting transfers between devices: 28.9 us -> 41 us
  local copies, waits for them, and re-layouts: 3.13 us -> 6.39 us
  other arithmetic: 7.23 us -> 5.34 us
    ppermute x3, waiting for transfers between devices: 22.6 us -> 3.2 us  [the longest x2 3.19 us: pass_on(): return lax.ppermute(chosen, axis, [(0, 2), (2, 3), (3, 1), (1, 0)])]
    ppermute x14, waiting for transfers between devices: 41.2 us -> 27.9 us  [local(): lax.ppermute(rows, 'section', [(i, i ^ mask) for i in range(n_section)])]
    ppermute x6 -> x7, waiting for transfers between devices: 2.15 us -> 14.5 us  [shift(): lax.ppermute(block, axis, [(i, (i + step) % size) for i in range(size)])]
    ppermute x14, starting transfers between devices: 9.61 us -> 16 us  [local(): lax.ppermute(rows, 'section', [(i, i ^ mask) for i in range(n_section)])]
    ppermute x3, starting transfers between devices: 2.78 us -> 7.3 us  [the longest x2 3.9 us: pass_on(): return lax.ppermute(chosen, axis, [(0, 2), (2, 3), (3, 1), (1, 0)])]
    ppermute x2, waiting for transfers between devices: 11.3 us -> 7.46 us  [local(): mirror_acts = [lax.ppermute(group, 'section', mirror) for group in held]]
    slice x0 -> x2, local copies, waits for them, and re-layouts: none -> 2.39 us  [local(): taken[:, offset:offset + span]]
    unnamed x36 -> x52, local copies, waits for them, and re-layouts: 3.13 us -> 4 us
  transfers between devices with their start and end apart: 26 -> 27, of which waited for: 11 -> 16; matrix products, arithmetic and copies ran while one was open for 4% -> 3% of each run, Pallas kernels for 20% -> 21%
where the time goes in v3:
time: 147 us; the launch traced here: 146 us
  waiting for transfers between devices  58.8 us (40%)
  starting transfers between devices  41 us (28%)
  Pallas kernels  34.4 us (23%)
  local copies, waits for them, and re-layouts  6.39 us (4%)
  other arithmetic  5.34 us (4%)
    ppermute x14, waiting for transfers between devices, local(): lax.ppermute(rows, 'section', [(i, i ^ mask) for i in range(n_section)])  27.9 us
    pallas_call x4, Pallas kernels, product(): pl.pallas_call(partial(product_kernel, tokens=tokens, layout=layout), gri...  21.3 us
    ppermute x14, starting transfers between devices, local(): lax.ppermute(rows, 'section', [(i, i ^ mask) for i in range(n_section)])  16 us
    ppermute x7, waiting for transfers between devices, shift(): lax.ppermute(block, axis, [(i, (i + step) % size) for i in range(size)])  14.5 us
    ppermute x7, starting transfers between devices, shift(): lax.ppermute(block, axis, [(i, (i + step) % size) for i in range(size)])  11.1 us
    ppermute x2, waiting for transfers between devices, local(): mirror_acts = [lax.ppermute(group, 'section', mirror) for group in held]  7.46 us
    pallas_call x2, Pallas kernels, join(): pl.pallas_call(partial(join_kernel, masks=masks, sections=sections, offse...  7.1 us
    all_to_all x1, waiting for transfers between devices, local(): lax.all_to_all(later, 'expert', split_axis=0, concat_axis=0, tiled=True)  5.7 us
  transfers between devices with their start and end apart: 27, of which 16 were waited for; matrix products, arithmetic and copies ran while one was open for 3% of the time, Pallas kernels for 21%

profile of v3, /device:TPU:0, one launch (start us, length us, event | category | flops | bytes accessed | tf_op | source)
XLA Modules:
  0.0 146.1 jit_solution(1840568387526263744)
XLA Ops:
  0.0 1.8 %broadcast_select_fusion.2 = (bf16[128,768]{1,0:T(8,128)(2,1)}, bf16[128,768]{1,0:T(8,128)(2,1)S(1)}) fusion(pred[]{:T(512)S(6)} %ge.3, bf16[128,4096]{1,0:T(8,128)(2,1)} %bitcast.38), kind=kLoop, calls=%fused_computation.5 | loop fusion | flops 196608 | bytes 786433 | tf_op jit(solution)/shard_map/jit(_where)/select_n | solution.py:202
  1.8 1.1 broadcast_select_fusion
  2.9 3.4 %collective-permute-start.3 = (bf16[128,2048]{1,0:T(8,128)(2,1)S(1)}, bf16[128,2048]{1,0:T(8,128)(2,1)S(1)}, u32[]{:S(2)}, u32[]{:S(2)}) collective-permute-start(bf16[128,2048]{1,0:T(8,128)(2,1)S(1)} %pad_maximum_fusion), channel_id=1, source_target_pairs={{0,28},{4,24},{8,20},{12,16},{16,12},{20,8},{24,4},{28,0},{1,29},{... | collective-permute-start | bytes 1572872 | tf_op jit(solution)/shard_map/ppermute | solution.py:204
  6.4 3.7 %collective-permute-start.2 = (f32[512]{0:T(512)S(1)}, f32[512]{0:T(512)S(1)}, u32[]{:S(2)}, u32[]{:S(2)}) collective-permute-start(f32[512]{0:T(512)S(1)} %get-tuple-element.78), channel_id=1, source_target_pairs={{0,3},{1,0},{2,1},{3,2},{4,7},{5,4},{6,5},{7,6},{8,11},{9,8},{10,9... | collective-permute-start | bytes 6152 | tf_op jit(solution)/shard_map/ppermute | solution.py:142
  10.0 1.0 collective-permute-start
  11.0 2.8 %collective-permute-start.8 = (bf16[128,1280]{1,0:T(8,128)(2,1)S(1)}, bf16[128,1280]{1,0:T(8,128)(2,1)S(1)}, u32[]{:S(2)}, u32[]{:S(2)}) collective-permute-start(bf16[128,1280]{1,0:T(8,128)(2,1)S(1)} %get-tuple-element.73), channel_id=1, source_target_pairs={{0,3},{1,0},{2,1},{3,2},{4,7},{5,4},{6,5},{7,6},{8,11},{9,8},{10,9... | collective-permute-start | bytes 983048 | tf_op jit(solution)/shard_map/ppermute | solution.py:142
  13.9 0.8 collective-permute-done.1
  14.6 0.8 collective-permute-done
  16.0 3.4 %shard_map.46 = (bf16[4,192,512]{2,1,0:T(8,128)(2,1)}, bf16[4,192,512]{2,1,0:T(8,128)(2,1)}) custom-call(f32[4,512]{1,0:T(4,128)} %pad_maximum_fusion.1.meta_ref, bf16[2,4,64,1536]{3,2,1,0:T(8,128)(2,1)} %bitcast.33), custom_call_target="tpu_custom_call" | custom-call | flops 1000000 | bytes 1000 | tf_op jit(solution)/shard_map/pallas_call | solution.py:57
  19.4 0.8 slice.28
  20.3 2.3 %collective-permute-start.6 = (bf16[4,192,512]{2,1,0:T(8,128)(2,1)}, bf16[4,192,512]{2,1,0:T(8,128)(2,1)S(1)}, u32[]{:S(2)}, u32[]{:S(2)}) collective-permute-start(bf16[4,192,512]{2,1,0:T(8,128)(2,1)} %get-tuple-element.40.own_ref), channel_id=1, source_target_pairs={{0,28},{4,24},{8,20},{12,16},{16,12},{20,8},{24,4},{28,0},{1,29},{... | collective-permute-start | bytes 2359304 | tf_op jit(solution)/shard_map/ppermute | solution.py:209
  22.6 3.6 %collective-permute-start.5 = (bf16[128,1280]{1,0:T(8,128)(2,1)}, bf16[128,1280]{1,0:T(8,128)(2,1)S(1)}, u32[]{:S(2)}, u32[]{:S(2)}) collective-permute-start(bf16[128,1280]{1,0:T(8,128)(2,1)} %slice.28), channel_id=1, source_target_pairs={{0,3},{1,0},{2,1},{3,2},{4,7},{5,4},{6,5},{7,6},{8,11},{9,8},{10,9... | collective-permute-start | bytes 983048 | tf_op jit(solution)/shard_map/ppermute | solution.py:142
  26.3 3.7 %collective-permute-done.7 = bf16[128,1280]{1,0:T(8,128)(2,1)S(1)} collective-permute-done((bf16[128,1280]{1,0:T(8,128)(2,1)S(1)}, bf16[128,1280]{1,0:T(8,128)(2,1)S(1)}, u32[]{:S(2)}, u32[]{:S(2)}) %collective-permute-start.7) | collective-permute-done | bytes 327712 | tf_op jit(solution)/shard_map/ppermute | solution.py:142
  30.0 0.8 select_select_fusion.1
  30.8 2.5 %collective-permute-start.9 = (bf16[128,1280]{1,0:T(8,128)(2,1)}, bf16[128,1280]{1,0:T(8,128)(2,1)S(1)}, u32[]{:S(2)}, u32[]{:S(2)}) collective-permute-start(bf16[128,1280]{1,0:T(8,128)(2,1)} %select_select_fusion.1), channel_id=1, source_target_pairs={{0,2},{2,3},{3,1},{1,0},{4,6},{6,7},{7,5},{5,4},{8,10},{10,11},{11... | collective-permute-start | bytes 983048 | tf_op jit(solution)/shard_map/ppermute | solution.py:152
  33.3 1.6 %slice.29.refs_1_ = bf16[128,768]{1,0:T(8,128)(2,1)} slice(bf16[128,2048]{1,0:T(8,128)(2,1)} %copy-done.9), slice={[0:128], [1280:2048]} | slice | bytes 393216 | tf_op jit(solution)/shard_map/slice | solution.py:205
  34.9 2.2 %collective-permute-done.5 = bf16[128,1280]{1,0:T(8,128)(2,1)S(1)} collective-permute-done((bf16[128,1280]{1,0:T(8,128)(2,1)}, bf16[128,1280]{1,0:T(8,128)(2,1)S(1)}, u32[]{:S(2)}, u32[]{:S(2)}) %collective-permute-start.5) | collective-permute-done | bytes 327712 | tf_op jit(solution)/shard_map/ppermute | solution.py:142
  37.1 7.0 %collective-permute-done.4.refs_2_ = bf16[128,1280]{1,0:T(8,128)(2,1)S(1)} collective-permute-done((bf16[128,1280]{1,0:T(8,128)(2,1)}, bf16[128,1280]{1,0:T(8,128)(2,1)S(1)}, u32[]{:S(2)}, u32[]{:S(2)}) %collective-permute-start.4) | collective-permute-done | bytes 327712 | tf_op jit(solution)/shard_map/ppermute | solution.py:142
  44.2 1.0 slice_bitcast_fusion
  45.2 1.4 collective-permute-start.10
  46.6 2.7 %shard_map.47 = bf16[4,256,768]{2,1,0:T(8,128)(2,1)} custom-call(bf16[128,768]{1,0:T(8,128)(2,1)} %get-tuple-element.71.refs_0_, bf16[128,768]{1,0:T(8,128)(2,1)} %slice.29.refs_1_, bf16[128,1280]{1,0:T(8,128)(2,1)} %copy-done.8), custom_call_target="tpu_custom_call" | custom-call | flops 99999997952 | bytes 1000000 | tf_op jit(solution)/shard_map/pallas_call | solution.py:165
  49.3 1.1 collective-permute-done.9
  50.4 7.5 %collective-permute-done.11.mirror_ref = bf16[4,192,512]{2,1,0:T(8,128)(2,1)S(1)} collective-permute-done((bf16[4,192,512]{2,1,0:T(8,128)(2,1)S(1)}, bf16[4,192,512]{2,1,0:T(8,128)(2,1)S(1)}, u32[]{:S(2)}, u32[]{:S(2)}) %collective-permute-start.11) | collective-permute-done | bytes 786464 | tf_op jit(solution)/shard_map/ppermute | solution.py:209
  57.9 0.9 copy-done.4
  58.8 2.1 %collective-permute-done.10 = bf16[128,1280]{1,0:T(8,128)(2,1)S(1)} collective-permute-done((bf16[128,1280]{1,0:T(8,128)(2,1)}, bf16[128,1280]{1,0:T(8,128)(2,1)S(1)}, u32[]{:S(2)}, u32[]{:S(2)}) %collective-permute-start.10) | collective-permute-done | bytes 327712 | tf_op jit(solution)/shard_map/ppermute | solution.py:152
  60.9 0.7 copy-done.12
  61.6 4.2 %all-to-all-start = ((bf16[4,256,768]{2,1,0:T(8,128)(2,1)}), bf16[4,256,768]{2,1,0:T(8,128)(2,1)S(1)}, u32[]{:S(2)}, u32[]{:S(2)}) async-start(bf16[4,256,768]{2,1,0:T(8,128)(2,1)} %shard_map.47), calls=%async_computation | async-start | bytes 3145728 | tf_op jit(solution)/shard_map/all_to_all | solution.py:220
  65.8 6.0 %shard_map.49 = (bf16[192,1280]{1,0:T(8,128)(2,1)}, bf16[192,1280]{1,0:T(8,128)(2,1)}, bf16[192,1280]{1,0:T(8,128)(2,1)}, bf16[192,1280]{1,0:T(8,128)(2,1)}) custom-call(bf16[4,192,512]{2,1,0:T(8,128)(2,1)} %get-tuple-element.44.own_ref, bf16[4,192,512]{2,1,0:T(8,128)(2,1)} %copy-done.4, bf16[1,128,1280]{2,1,0:T(8,128)(2,1)} %bitcast.23, ...), custom_call_target="tpu_custom_call" | custom-call | flops 1000000 | bytes 1000 | tf_op jit(solution)/shard_map/pallas_call | solution.py:91
  72.4 1.1 collective-permute-start.14
  73.6 6.1 %shard_map.48 = (bf16[192,1280]{1,0:T(8,128)(2,1)}, bf16[192,1280]{1,0:T(8,128)(2,1)}, bf16[192,1280]{1,0:T(8,128)(2,1)}, bf16[192,1280]{1,0:T(8,128)(2,1)}) custom-call(bf16[4,192,512]{2,1,0:T(8,128)(2,1)} %get-tuple-element.40.own_ref, bf16[4,192,512]{2,1,0:T(8,128)(2,1)} %copy-done.2, bf16[1,128,1280]{2,1,0:T(8,128)(2,1)} %bitcast.24, ...), custom_call_target="tpu_custom_call" | custom-call | flops 1000000 | bytes 1000 | tf_op jit(solution)/shard_map/pallas_call | solution.py:91
  79.7 1.9 %collective-permute-start.15 = (bf16[192,1280]{1,0:T(8,128)(2,1)}, bf16[192,1280]{1,0:T(8,128)(2,1)S(1)}, u32[]{:S(2)}, u32[]{:S(2)}) collective-permute-start(bf16[192,1280]{1,0:T(8,128)(2,1)} %get-tuple-element.52), channel_id=1, source_target_pairs={{0,24},{4,28},{8,16},{12,20},{16,8},{20,12},{24,0},{28,4},{1,25},{... | collective-permute-start | bytes 1474568 | tf_op jit(solution)/shard_map/ppermute | solution.py:237
  81.9 2.0 %collective-permute-done.13.refs_2_ = bf16[192,1280]{1,0:T(8,128)(2,1)S(1)} collective-permute-done((bf16[192,1280]{1,0:T(8,128)(2,1)}, bf16[192,1280]{1,0:T(8,128)(2,1)S(1)}, u32[]{:S(2)}, u32[]{:S(2)}) %collective-permute-start.13) | collective-permute-done | bytes 491552 | tf_op jit(solution)/shard_map/ppermute | solution.py:237
  83.9 11.9 %collective-permute-done.14.refs_4_ = bf16[192,1280]{1,0:T(8,128)(2,1)S(1)} collective-permute-done((bf16[192,1280]{1,0:T(8,128)(2,1)}, bf16[192,1280]{1,0:T(8,128)(2,1)S(1)}, u32[]{:S(2)}, u32[]{:S(2)}) %collective-permute-start.14) | collective-permute-done | bytes 491552 | tf_op jit(solution)/shard_map/ppermute | solution.py:237
  96.0 5.7 %all-to-all-done.refs_0_ = bf16[4,256,768]{2,1,0:T(8,128)(2,1)S(1)} async-done(((bf16[4,256,768]{2,1,0:T(8,128)(2,1)}), bf16[4,256,768]{2,1,0:T(8,128)(2,1)S(1)}, u32[]{:S(2)}, u32[]{:S(2)}) %all-to-all-start) | async-done | bytes 1572896 | tf_op jit(solution)/shard_map/all_to_all | solution.py:220
  101.7 1.1 copy-done
  102.8 4.6 %shard_map.51 = (bf16[192,768]{1,0:T(8,128)(2,1)}, bf16[192,768]{1,0:T(8,128)(2,1)}, bf16[192,768]{1,0:T(8,128)(2,1)}, bf16[192,768]{1,0:T(8,128)(2,1)}) custom-call(bf16[4,192,512]{2,1,0:T(8,128)(2,1)} %get-tuple-element.44.own_ref, bf16[4,192,512]{2,1,0:T(8,128)(2,1)} %copy-done.4, bf16[4,256,768]{2,1,0:T(8,128)(2,1)} %copy-done), custom_call_target="tpu_custom_call" | custom-call | flops 1000000 | bytes 1000 | tf_op jit(solution)/shard_map/pallas_call | solution.py:91
  107.4 1.6 %collective-permute-start.17 = (bf16[192,768]{1,0:T(8,128)(2,1)}, bf16[192,768]{1,0:T(8,128)(2,1)S(1)}, u32[]{:S(2)}, u32[]{:S(2)}) collective-permute-start(bf16[192,768]{1,0:T(8,128)(2,1)} %get-tuple-element.57), channel_id=1, source_target_pairs={{0,8},{4,12},{8,0},{12,4},{16,24},{20,28},{24,16},{28,20},{1,9},{5... | collective-permute-start | bytes 884744 | tf_op jit(solution)/shard_map/ppermute | solution.py:237
  109.1 4.6 %shard_map.50 = (bf16[192,768]{1,0:T(8,128)(2,1)}, bf16[192,768]{1,0:T(8,128)(2,1)}, bf16[192,768]{1,0:T(8,128)(2,1)}, bf16[192,768]{1,0:T(8,128)(2,1)}) custom-call(bf16[4,192,512]{2,1,0:T(8,128)(2,1)} %get-tuple-element.40.own_ref, bf16[4,192,512]{2,1,0:T(8,128)(2,1)} %copy-done.2, bf16[4,256,768]{2,1,0:T(8,128)(2,1)} %copy-done), custom_call_target="tpu_custom_call" | custom-call | flops 1000000 | bytes 1000 | tf_op jit(solution)/shard_map/pallas_call | solution.py:91
  113.7 1.6 %collective-permute-start.19 = (bf16[192,768]{1,0:T(8,128)(2,1)}, bf16[192,768]{1,0:T(8,128)(2,1)S(1)}, u32[]{:S(2)}, u32[]{:S(2)}) collective-permute-start(bf16[192,768]{1,0:T(8,128)(2,1)} %get-tuple-element.59), channel_id=1, source_target_pairs={{0,16},{4,20},{8,24},{12,28},{16,0},{20,4},{24,8},{28,12},{1,17},{... | collective-permute-start | bytes 884744 | tf_op jit(solution)/shard_map/ppermute | solution.py:237
  115.9 1.9 %collective-permute-start.20 = (bf16[192,768]{1,0:T(8,128)(2,1)}, bf16[192,768]{1,0:T(8,128)(2,1)S(1)}, u32[]{:S(2)}, u32[]{:S(2)}) collective-permute-start(bf16[192,768]{1,0:T(8,128)(2,1)} %get-tuple-element.60), channel_id=1, source_target_pairs={{0,20},{4,16},{8,28},{12,24},{16,4},{20,0},{24,12},{28,8},{1,21},{... | collective-permute-start | bytes 884744 | tf_op jit(solution)/shard_map/ppermute | solution.py:237
  117.8 4.1 %collective-permute-done.17.refs_2_ = bf16[192,768]{1,0:T(8,128)(2,1)S(1)} collective-permute-done((bf16[192,768]{1,0:T(8,128)(2,1)}, bf16[192,768]{1,0:T(8,128)(2,1)S(1)}, u32[]{:S(2)}, u32[]{:S(2)}) %collective-permute-start.17) | collective-permute-done | bytes 294944 | tf_op jit(solution)/shard_map/ppermute | solution.py:237
  121.9 3.4 %collective-permute-start.21 = (bf16[192,768]{1,0:T(8,128)(2,1)}, bf16[192,768]{1,0:T(8,128)(2,1)S(1)}, u32[]{:S(2)}, u32[]{:S(2)}) collective-permute-start(bf16[192,768]{1,0:T(8,128)(2,1)} %get-tuple-element.61), channel_id=1, source_target_pairs={{0,24},{4,28},{8,16},{12,20},{16,8},{20,12},{24,0},{28,4},{1,25},{... | collective-permute-start | bytes 884744 | tf_op jit(solution)/shard_map/ppermute | solution.py:237
  125.3 2.5 %collective-permute-done.18.refs_3_ = bf16[192,768]{1,0:T(8,128)(2,1)S(1)} collective-permute-done((bf16[192,768]{1,0:T(8,128)(2,1)}, bf16[192,768]{1,0:T(8,128)(2,1)S(1)}, u32[]{:S(2)}, u32[]{:S(2)}) %collective-permute-start.18) | collective-permute-done | bytes 294944 | tf_op jit(solution)/shard_map/ppermute | solution.py:237
  127.7 3.6 %collective-permute-start.22 = (bf16[192,768]{1,0:T(8,128)(2,1)}, bf16[192,768]{1,0:T(8,128)(2,1)S(1)}, u32[]{:S(2)}, u32[]{:S(2)}) collective-permute-start(bf16[192,768]{1,0:T(8,128)(2,1)} %get-tuple-element.62), channel_id=1, source_target_pairs={{0,28},{4,24},{8,20},{12,16},{16,12},{20,8},{24,4},{28,0},{1,29},{... | collective-permute-start | bytes 884744 | tf_op jit(solution)/shard_map/ppermute | solution.py:237
  131.3 4.0 %shard_map.52.refs_8_ = bf16[4,1,192,4096]{3,2,1,0:T(8,128)(2,1)} custom-call(bf16[192,1280]{1,0:T(8,128)(2,1)} %get-tuple-element.63.refs_0_, bf16[192,1280]{1,0:T(8,128)(2,1)} %copy-done.15, bf16[192,1280]{1,0:T(8,128)(2,1)} %copy-done.13, bf16[192,1280]{1,0:T(8,128)(2,1)} %collective-permute-done.23.refs_3_, bf16[192,1280]{1,0:T(8,128)(2,1)} %copy-done.14, ...), custom_call_target="tpu_custom_call" | custom-call | tf_op jit(solution)/shard_map/pallas_call | solution.py:130
  135.4 6.6 %collective-permute-done.20.refs_5_ = bf16[192,768]{1,0:T(8,128)(2,1)S(1)} collective-permute-done((bf16[192,768]{1,0:T(8,128)(2,1)}, bf16[192,768]{1,0:T(8,128)(2,1)S(1)}, u32[]{:S(2)}, u32[]{:S(2)}) %collective-permute-start.20) | collective-permute-done | bytes 294944 | tf_op jit(solution)/shard_map/ppermute | solution.py:237
  142.1 0.7 copy-done.20
  143.1 3.0 %shard_map.53 = bf16[4,1,192,4096]{3,2,1,0:T(8,128)(2,1)} custom-call(bf16[192,768]{1,0:T(8,128)(2,1)} %get-tuple-element.55.refs_0_, bf16[192,768]{1,0:T(8,128)(2,1)} %copy-done.21, bf16[192,768]{1,0:T(8,128)(2,1)} %copy-done.17, bf16[192,768]{1,0:T(8,128)(2,1)} %copy-done.18, bf16[192,768]{1,0:T(8,128)(2,1)} %copy-done.19, ...), custom_call_target="tpu_custom_call", output_to_operand_aliasing={{}: (8, {})} | custom-call | tf_op jit(solution)/shard_map/pallas_call | solution.py:130
  (76 shorter events, 3.0 us)
Async XLA Ops:
  0.0 6.3 %copy-start.24 = (s32[1,128,2]{1,2,0:T(2,128)S(1)}, s32[1,128,2]{1,2,0:T(2,128)}, u32[]{:S(2)}) copy-start(s32[1,128,2]{1,2,0:T(2,128)} %param.5) | copy-start | bytes 3076
  0.0 6.3 %copy-start.25 = (f32[1,128,2]{1,2,0:T(2,128)S(1)}, f32[1,128,2]{1,2,0:T(2,128)}, u32[]{:S(2)}) copy-start(f32[1,128,2]{1,2,0:T(2,128)} %param.6) | copy-start | bytes 3076
  2.9 27.1 %copy-start.1 = (bf16[128,1280]{1,0:T(8,128)(2,1)}, bf16[128,1280]{1,0:T(8,128)(2,1)S(1)}, u32[]{:S(2)}) copy-start(bf16[128,1280]{1,0:T(8,128)(2,1)S(1)} %get-tuple-element.73) | copy-start | bytes 983044
  2.9 16.5 %collective-permute-start.3 = (bf16[128,2048]{1,0:T(8,128)(2,1)S(1)}, bf16[128,2048]{1,0:T(8,128)(2,1)S(1)}, u32[]{:S(2)}, u32[]{:S(2)}) collective-permute-start(bf16[128,2048]{1,0:T(8,128)(2,1)S(1)} %pad_maximum_fusion), channel_id=1, source_target_pairs={{0,28},{4,24},{8,20},{12,16},{16,12},{20,8},{24,4},{28,0},{1,29},{... | collective-permute-start | bytes 1572872 | tf_op jit(solution)/shard_map/ppermute | solution.py:204
  6.4 7.5 %collective-permute-start.2 = (f32[512]{0:T(512)S(1)}, f32[512]{0:T(512)S(1)}, u32[]{:S(2)}, u32[]{:S(2)}) collective-permute-start(f32[512]{0:T(512)S(1)} %get-tuple-element.78), channel_id=1, source_target_pairs={{0,3},{1,0},{2,1},{3,2},{4,7},{5,4},{6,5},{7,6},{8,11},{9,8},{10,9... | collective-permute-start | bytes 6152 | tf_op jit(solution)/shard_map/ppermute | solution.py:142
  10.0 4.6 %collective-permute-start.1 = (f32[512]{0:T(512)S(1)}, f32[512]{0:T(512)S(1)}, u32[]{:S(2)}, u32[]{:S(2)}) collective-permute-start(f32[512]{0:T(512)S(1)} %get-tuple-element.78), channel_id=1, source_target_pairs={{0,2},{1,3},{2,0},{3,1},{4,6},{5,7},{6,4},{7,5},{8,10},{9,11},{10,... | collective-permute-start | bytes 6152 | tf_op jit(solution)/shard_map/ppermute | solution.py:142
  10.0 5.4 %collective-permute-start = (f32[512]{0:T(512)S(1)}, f32[512]{0:T(512)S(1)}, u32[]{:S(2)}, u32[]{:S(2)}) collective-permute-start(f32[512]{0:T(512)S(1)} %get-tuple-element.78), channel_id=1, source_target_pairs={{0,1},{1,2},{2,3},{3,0},{4,5},{5,6},{6,7},{7,4},{8,9},{9,10},{10,1... | collective-permute-start | bytes 6152 | tf_op jit(solution)/shard_map/ppermute | solution.py:142
  11.0 15.2 %collective-permute-start.8 = (bf16[128,1280]{1,0:T(8,128)(2,1)S(1)}, bf16[128,1280]{1,0:T(8,128)(2,1)S(1)}, u32[]{:S(2)}, u32[]{:S(2)}) collective-permute-start(bf16[128,1280]{1,0:T(8,128)(2,1)S(1)} %get-tuple-element.73), channel_id=1, source_target_pairs={{0,3},{1,0},{2,1},{3,2},{4,7},{5,4},{6,5},{7,6},{8,11},{9,8},{10,9... | collective-permute-start | bytes 983048 | tf_op jit(solution)/shard_map/ppermute | solution.py:142
  13.8 16.2 %collective-permute-start.7 = (bf16[128,1280]{1,0:T(8,128)(2,1)S(1)}, bf16[128,1280]{1,0:T(8,128)(2,1)S(1)}, u32[]{:S(2)}, u32[]{:S(2)}) collective-permute-start(bf16[128,1280]{1,0:T(8,128)(2,1)S(1)} %get-tuple-element.73), channel_id=1, source_target_pairs={{0,1},{1,2},{2,3},{3,0},{4,5},{5,6},{6,7},{7,4},{8,9},{9,10},{10,1... | collective-permute-start | bytes 983048 | tf_op jit(solution)/shard_map/ppermute | solution.py:142
  19.4 13.9 %copy-start.3 = (bf16[4,192,512]{2,1,0:T(8,128)(2,1)S(1)}, bf16[4,192,512]{2,1,0:T(8,128)(2,1)}, u32[]{:S(2)}) copy-start(bf16[4,192,512]{2,1,0:T(8,128)(2,1)} %get-tuple-element.44.own_ref) | copy-start | bytes 2359300
  20.3 23.9 %collective-permute-start.6 = (bf16[4,192,512]{2,1,0:T(8,128)(2,1)}, bf16[4,192,512]{2,1,0:T(8,128)(2,1)S(1)}, u32[]{:S(2)}, u32[]{:S(2)}) collective-permute-start(bf16[4,192,512]{2,1,0:T(8,128)(2,1)} %get-tuple-element.40.own_ref), channel_id=1, source_target_pairs={{0,28},{4,24},{8,20},{12,16},{16,12},{20,8},{24,4},{28,0},{1,29},{... | collective-permute-start | bytes 2359304 | tf_op jit(solution)/shard_map/ppermute | solution.py:209
  22.6 21.5 %copy-start.10 = (bf16[128,2048]{1,0:T(8,128)(2,1)S(1)}, bf16[128,2048]{1,0:T(8,128)(2,1)}, u32[]{:S(2)}) copy-start(bf16[128,2048]{1,0:T(8,128)(2,1)} %copy-done.9) | copy-start | bytes 1572868
  22.6 14.5 %collective-permute-start.5 = (bf16[128,1280]{1,0:T(8,128)(2,1)}, bf16[128,1280]{1,0:T(8,128)(2,1)S(1)}, u32[]{:S(2)}, u32[]{:S(2)}) collective-permute-start(bf16[128,1280]{1,0:T(8,128)(2,1)} %slice.28), channel_id=1, source_target_pairs={{0,3},{1,0},{2,1},{3,2},{4,7},{5,4},{6,5},{7,6},{8,11},{9,8},{10,9... | collective-permute-start | bytes 983048 | tf_op jit(solution)/shard_map/ppermute | solution.py:142
  26.3 17.9 %collective-permute-start.4 = (bf16[128,1280]{1,0:T(8,128)(2,1)}, bf16[128,1280]{1,0:T(8,128)(2,1)S(1)}, u32[]{:S(2)}, u32[]{:S(2)}) collective-permute-start(bf16[128,1280]{1,0:T(8,128)(2,1)} %slice.28), channel_id=1, source_target_pairs={{0,1},{1,2},{2,3},{3,0},{4,5},{5,6},{6,7},{7,4},{8,9},{9,10},{10,1... | collective-permute-start | bytes 983048 | tf_op jit(solution)/shard_map/ppermute | solution.py:142
  26.3 4.6 %copy-start.5 = (bf16[128,1280]{1,0:T(8,128)(2,1)}, bf16[128,1280]{1,0:T(8,128)(2,1)S(1)}, u32[]{:S(2)}) copy-start(bf16[128,1280]{1,0:T(8,128)(2,1)S(1)} %collective-permute-done.8) | copy-start | bytes 983044
  30.0 15.1 %copy-start.6 = (bf16[128,1280]{1,0:T(8,128)(2,1)}, bf16[128,1280]{1,0:T(8,128)(2,1)S(1)}, u32[]{:S(2)}) copy-start(bf16[128,1280]{1,0:T(8,128)(2,1)S(1)} %collective-permute-done.7) | copy-start | bytes 983044
  30.8 19.6 %collective-permute-start.9 = (bf16[128,1280]{1,0:T(8,128)(2,1)}, bf16[128,1280]{1,0:T(8,128)(2,1)S(1)}, u32[]{:S(2)}, u32[]{:S(2)}) collective-permute-start(bf16[128,1280]{1,0:T(8,128)(2,1)} %select_select_fusion.1), channel_id=1, source_target_pairs={{0,2},{2,3},{3,1},{1,0},{4,6},{6,7},{7,5},{5,4},{8,10},{10,11},{11... | collective-permute-start | bytes 983048 | tf_op jit(solution)/shard_map/ppermute | solution.py:152
  33.3 24.6 %collective-permute-start.11 = (bf16[4,192,512]{2,1,0:T(8,128)(2,1)S(1)}, bf16[4,192,512]{2,1,0:T(8,128)(2,1)S(1)}, u32[]{:S(2)}, u32[]{:S(2)}) collective-permute-start(bf16[4,192,512]{2,1,0:T(8,128)(2,1)S(1)} %copy-done.3), channel_id=1, source_target_pairs={{0,28},{4,24},{8,20},{12,16},{16,12},{20,8},{24,4},{28,0},{1,29},{... | collective-permute-start | bytes 2359304 | tf_op jit(solution)/shard_map/ppermute | solution.py:209
  37.1 12.2 %copy-start.7 = (bf16[128,1280]{1,0:T(8,128)(2,1)}, bf16[128,1280]{1,0:T(8,128)(2,1)S(1)}, u32[]{:S(2)}) copy-start(bf16[128,1280]{1,0:T(8,128)(2,1)S(1)} %collective-permute-done.5) | copy-start | bytes 983044
  44.2 2.5 %copy-start.8 = (bf16[128,1280]{1,0:T(8,128)(2,1)}, bf16[128,1280]{1,0:T(8,128)(2,1)S(1)}, u32[]{:S(2)}) copy-start(bf16[128,1280]{1,0:T(8,128)(2,1)S(1)} %collective-permute-done.4.refs_2_) | copy-start | bytes 983044
  44.2 5.1 %copy-start.2 = (bf16[4,192,512]{2,1,0:T(8,128)(2,1)}, bf16[4,192,512]{2,1,0:T(8,128)(2,1)S(1)}, u32[]{:S(2)}) copy-start(bf16[4,192,512]{2,1,0:T(8,128)(2,1)S(1)} %collective-permute-done.6.mirror_ref) | copy-start | bytes 2359300
  45.2 15.7 %collective-permute-start.10 = (bf16[128,1280]{1,0:T(8,128)(2,1)}, bf16[128,1280]{1,0:T(8,128)(2,1)S(1)}, u32[]{:S(2)}, u32[]{:S(2)}) collective-permute-start(bf16[128,1280]{1,0:T(8,128)(2,1)} %get-tuple-element.76), channel_id=1, source_target_pairs={{0,2},{2,3},{3,1},{1,0},{4,6},{6,7},{7,5},{5,4},{8,10},{10,11},{11... | collective-permute-start | bytes 983048 | tf_op jit(solution)/shard_map/ppermute | solution.py:152
  50.4 15.4 %copy-start.11 = (bf16[128,1280]{1,0:T(8,128)(2,1)}, bf16[128,1280]{1,0:T(8,128)(2,1)S(1)}, u32[]{:S(2)}) copy-start(bf16[128,1280]{1,0:T(8,128)(2,1)S(1)} %collective-permute-done.9) | copy-start | bytes 983044
  57.9 0.9 copy-start.4
  61.6 40.0 %all-to-all-start = ((bf16[4,256,768]{2,1,0:T(8,128)(2,1)}), bf16[4,256,768]{2,1,0:T(8,128)(2,1)S(1)}, u32[]{:S(2)}, u32[]{:S(2)}) async-start(bf16[4,256,768]{2,1,0:T(8,128)(2,1)} %shard_map.47), calls=%async_computation | async-start | bytes 3145728 | tf_op jit(solution)/shard_map/all_to_all | solution.py:220
  71.8 12.1 %collective-permute-start.13 = (bf16[192,1280]{1,0:T(8,128)(2,1)}, bf16[192,1280]{1,0:T(8,128)(2,1)S(1)}, u32[]{:S(2)}, u32[]{:S(2)}) collective-permute-start(bf16[192,1280]{1,0:T(8,128)(2,1)} %get-tuple-element.50), channel_id=1, source_target_pairs={{0,8},{4,12},{8,0},{12,4},{16,24},{20,28},{24,16},{28,20},{1,9},{5... | collective-permute-start | bytes 1474568 | tf_op jit(solution)/shard_map/ppermute | solution.py:237
  72.4 23.4 %collective-permute-start.14 = (bf16[192,1280]{1,0:T(8,128)(2,1)}, bf16[192,1280]{1,0:T(8,128)(2,1)S(1)}, u32[]{:S(2)}, u32[]{:S(2)}) collective-permute-start(bf16[192,1280]{1,0:T(8,128)(2,1)} %get-tuple-element.51), channel_id=1, source_target_pairs={{0,16},{4,20},{8,24},{12,28},{16,0},{20,4},{24,8},{28,12},{1,17},{... | collective-permute-start | bytes 1474568 | tf_op jit(solution)/shard_map/ppermute | solution.py:237
  79.6 16.2 %collective-permute-start.12 = (bf16[192,1280]{1,0:T(8,128)(2,1)}, bf16[192,1280]{1,0:T(8,128)(2,1)S(1)}, u32[]{:S(2)}, u32[]{:S(2)}) collective-permute-start(bf16[192,1280]{1,0:T(8,128)(2,1)} %get-tuple-element.48), channel_id=1, source_target_pairs={{0,4},{4,0},{8,12},{12,8},{16,20},{20,16},{24,28},{28,24},{1,5},{5... | collective-permute-start | bytes 1474568 | tf_op jit(solution)/shard_map/ppermute | solution.py:237
  79.7 16.3 %collective-permute-start.15 = (bf16[192,1280]{1,0:T(8,128)(2,1)}, bf16[192,1280]{1,0:T(8,128)(2,1)S(1)}, u32[]{:S(2)}, u32[]{:S(2)}) collective-permute-start(bf16[192,1280]{1,0:T(8,128)(2,1)} %get-tuple-element.52), channel_id=1, source_target_pairs={{0,24},{4,28},{8,16},{12,20},{16,8},{20,12},{24,0},{28,4},{1,25},{... | collective-permute-start | bytes 1474568 | tf_op jit(solution)/shard_map/ppermute | solution.py:237
  81.6 32.1 %collective-permute-start.23 = (bf16[192,1280]{1,0:T(8,128)(2,1)}, bf16[192,1280]{1,0:T(8,128)(2,1)}, u32[]{:S(2)}, u32[]{:S(2)}) collective-permute-start(bf16[192,1280]{1,0:T(8,128)(2,1)} %get-tuple-element.66), channel_id=1, source_target_pairs={{0,12},{4,8},{8,4},{12,0},{16,28},{20,24},{24,20},{28,16},{1,13},{... | collective-permute-start | bytes 1474568 | tf_op jit(solution)/shard_map/ppermute | solution.py:237
  83.9 47.4 %copy-start.13 = (bf16[192,1280]{1,0:T(8,128)(2,1)}, bf16[192,1280]{1,0:T(8,128)(2,1)S(1)}, u32[]{:S(2)}) copy-start(bf16[192,1280]{1,0:T(8,128)(2,1)S(1)} %collective-permute-done.13.refs_2_) | copy-start | bytes 1474564
  83.9 32.0 %collective-permute-start.24 = (bf16[192,1280]{1,0:T(8,128)(2,1)}, bf16[192,1280]{1,0:T(8,128)(2,1)}, u32[]{:S(2)}, u32[]{:S(2)}) collective-permute-start(bf16[192,1280]{1,0:T(8,128)(2,1)} %get-tuple-element.68), channel_id=1, source_target_pairs={{0,20},{4,16},{8,28},{12,24},{16,4},{20,0},{24,12},{28,8},{1,21},{... | collective-permute-start | bytes 1474568 | tf_op jit(solution)/shard_map/ppermute | solution.py:237
  95.8 35.5 %copy-start.14 = (bf16[192,1280]{1,0:T(8,128)(2,1)}, bf16[192,1280]{1,0:T(8,128)(2,1)S(1)}, u32[]{:S(2)}) copy-start(bf16[192,1280]{1,0:T(8,128)(2,1)S(1)} %collective-permute-done.14.refs_4_) | copy-start | bytes 1474564
  95.8 22.0 %collective-permute-start.25 = (bf16[192,1280]{1,0:T(8,128)(2,1)}, bf16[192,1280]{1,0:T(8,128)(2,1)}, u32[]{:S(2)}, u32[]{:S(2)}) collective-permute-start(bf16[192,1280]{1,0:T(8,128)(2,1)} %get-tuple-element.70), channel_id=1, source_target_pairs={{0,28},{4,24},{8,20},{12,16},{16,12},{20,8},{24,4},{28,0},{1,29},{... | collective-permute-start | bytes 1474568 | tf_op jit(solution)/shard_map/ppermute | solution.py:237
  95.8 35.5 %copy-start.15 = (bf16[192,1280]{1,0:T(8,128)(2,1)}, bf16[192,1280]{1,0:T(8,128)(2,1)S(1)}, u32[]{:S(2)}) copy-start(bf16[192,1280]{1,0:T(8,128)(2,1)S(1)} %collective-permute-done.12.refs_1_) | copy-start | bytes 1474564
  96.0 35.4 %copy-start.16 = (bf16[192,1280]{1,0:T(8,128)(2,1)}, bf16[192,1280]{1,0:T(8,128)(2,1)S(1)}, u32[]{:S(2)}) copy-start(bf16[192,1280]{1,0:T(8,128)(2,1)S(1)} %collective-permute-done.15.refs_6_) | copy-start | bytes 1474564
  101.7 1.1 copy-start
  107.4 14.5 %collective-permute-start.17 = (bf16[192,768]{1,0:T(8,128)(2,1)}, bf16[192,768]{1,0:T(8,128)(2,1)S(1)}, u32[]{:S(2)}, u32[]{:S(2)}) collective-permute-start(bf16[192,768]{1,0:T(8,128)(2,1)} %get-tuple-element.57), channel_id=1, source_target_pairs={{0,8},{4,12},{8,0},{12,4},{16,24},{20,28},{24,16},{28,20},{1,9},{5... | collective-permute-start | bytes 884744 | tf_op jit(solution)/shard_map/ppermute | solution.py:237
  109.1 18.7 %collective-permute-start.18 = (bf16[192,768]{1,0:T(8,128)(2,1)}, bf16[192,768]{1,0:T(8,128)(2,1)S(1)}, u32[]{:S(2)}, u32[]{:S(2)}) collective-permute-start(bf16[192,768]{1,0:T(8,128)(2,1)} %get-tuple-element.58), channel_id=1, source_target_pairs={{0,12},{4,8},{8,4},{12,0},{16,28},{20,24},{24,20},{28,16},{1,13},{... | collective-permute-start | bytes 884744 | tf_op jit(solution)/shard_map/ppermute | solution.py:237
  113.7 21.7 %collective-permute-start.19 = (bf16[192,768]{1,0:T(8,128)(2,1)}, bf16[192,768]{1,0:T(8,128)(2,1)S(1)}, u32[]{:S(2)}, u32[]{:S(2)}) collective-permute-start(bf16[192,768]{1,0:T(8,128)(2,1)} %get-tuple-element.59), channel_id=1, source_target_pairs={{0,16},{4,20},{8,24},{12,28},{16,0},{20,4},{24,8},{28,12},{1,17},{... | collective-permute-start | bytes 884744 | tf_op jit(solution)/shard_map/ppermute | solution.py:237
  115.9 26.1 %collective-permute-start.20 = (bf16[192,768]{1,0:T(8,128)(2,1)}, bf16[192,768]{1,0:T(8,128)(2,1)S(1)}, u32[]{:S(2)}, u32[]{:S(2)}) collective-permute-start(bf16[192,768]{1,0:T(8,128)(2,1)} %get-tuple-element.60), channel_id=1, source_target_pairs={{0,20},{4,16},{8,28},{12,24},{16,4},{20,0},{24,12},{28,8},{1,21},{... | collective-permute-start | bytes 884744 | tf_op jit(solution)/shard_map/ppermute | solution.py:237
  117.8 24.3 %collective-permute-start.16 = (bf16[192,768]{1,0:T(8,128)(2,1)}, bf16[192,768]{1,0:T(8,128)(2,1)S(1)}, u32[]{:S(2)}, u32[]{:S(2)}) collective-permute-start(bf16[192,768]{1,0:T(8,128)(2,1)} %get-tuple-element.56), channel_id=1, source_target_pairs={{0,4},{4,0},{8,12},{12,8},{16,20},{20,16},{24,28},{28,24},{1,5},{5... | collective-permute-start | bytes 884744 | tf_op jit(solution)/shard_map/ppermute | solution.py:237
  121.9 13.5 %copy-start.17 = (bf16[192,768]{1,0:T(8,128)(2,1)}, bf16[192,768]{1,0:T(8,128)(2,1)S(1)}, u32[]{:S(2)}) copy-start(bf16[192,768]{1,0:T(8,128)(2,1)S(1)} %collective-permute-done.17.refs_2_) | copy-start | bytes 884740
  121.9 20.1 %collective-permute-start.21 = (bf16[192,768]{1,0:T(8,128)(2,1)}, bf16[192,768]{1,0:T(8,128)(2,1)S(1)}, u32[]{:S(2)}, u32[]{:S(2)}) collective-permute-start(bf16[192,768]{1,0:T(8,128)(2,1)} %get-tuple-element.61), channel_id=1, source_target_pairs={{0,24},{4,28},{8,16},{12,20},{16,8},{20,12},{24,0},{28,4},{1,25},{... | collective-permute-start | bytes 884744 | tf_op jit(solution)/shard_map/ppermute | solution.py:237
  127.7 7.7 %copy-start.18 = (bf16[192,768]{1,0:T(8,128)(2,1)}, bf16[192,768]{1,0:T(8,128)(2,1)S(1)}, u32[]{:S(2)}) copy-start(bf16[192,768]{1,0:T(8,128)(2,1)S(1)} %collective-permute-done.18.refs_3_) | copy-start | bytes 884740
  127.7 14.3 %collective-permute-start.22 = (bf16[192,768]{1,0:T(8,128)(2,1)}, bf16[192,768]{1,0:T(8,128)(2,1)S(1)}, u32[]{:S(2)}, u32[]{:S(2)}) collective-permute-start(bf16[192,768]{1,0:T(8,128)(2,1)} %get-tuple-element.62), channel_id=1, source_target_pairs={{0,28},{4,24},{8,20},{12,16},{16,12},{20,8},{24,4},{28,0},{1,29},{... | collective-permute-start | bytes 884744 | tf_op jit(solution)/shard_map/ppermute | solution.py:237
  135.4 6.7 %copy-start.19 = (bf16[192,768]{1,0:T(8,128)(2,1)}, bf16[192,768]{1,0:T(8,128)(2,1)S(1)}, u32[]{:S(2)}) copy-start(bf16[192,768]{1,0:T(8,128)(2,1)S(1)} %collective-permute-done.19.refs_4_) | copy-start | bytes 884740
  142.1 1.0 copy-start.23
  (5 other events, 4.1 us)

commit v4 on v3

--- a/solution.py
+++ b/solution.py
@@ -79,15 +79,16 @@
     own = jnp.dot(own_ref[...].reshape(count * rows, depth), packed[:depth], preferred_element_type=jnp.float32)
     mirror = jnp.dot(mirror_ref[...].reshape(count * rows, depth), packed[depth:], preferred_element_type=jnp.float32)
     for i, out in enumerate(outs):
-        j = count - 1 - i
+        j = i ^ 1
         total = own[i * rows : (i + 1) * rows] + mirror[j * rows : (j + 1) * rows]
         out[...] = total.astype(jnp.bfloat16)
 
 
-def product(own_acts, mirror_acts, cots, layout, tokens, tile):
-    count, rows, depth = own_acts.shape
+def product(own_acts, mirror_acts, cots, layout, tokens, tile, part, parts):
+    masks, rows, depth = own_acts.shape
+    count = masks // parts
     width = cots[0].shape[-1]
-    acts_spec = pl.BlockSpec((count, rows, depth), lambda n: (0, 0, 0))
+    acts_spec = pl.BlockSpec((count, rows, depth), lambda n: (part, 0, 0))
     return pl.pallas_call(
         partial(product_kernel, tokens=tokens, layout=layout),
         grid=(width // tile,),
@@ -187,21 +188,23 @@
     mirror = [(i, n_section - 1 - i) for i in range(n_section)]
     upper = section >= n_section // 2
     quarter = n_section // 4
-    near = [start + i for i in range(quarter // 2) for start in (quarter, 2 * quarter)]
-    near += [n_section - 1 - mask for mask in reversed(near)]
-    groups = [[mask for mask in range(n_section) if mask not in near], near]
+    near, far = [], []
+    for i in range(quarter // 2):
+        near += [quarter + i, n_section - 1 - quarter - i, 2 * quarter + i, n_section - 1 - 2 * quarter - i]
+    for i in range(quarter):
+        far += [i, n_section - 1 - i]
+    groups = [far, near]
     short = n_expert == 4
+    cot = cotangent[0]
+    given = jnp.where(upper, cot[:, :half_width], cot[:, half_width:])
+    cot, given = lax.optimization_barrier((cot, given))
+    kept = jnp.where(upper, cot[:, half_width:], cot[:, :half_width])
+    kept, routes, gate_prob = lax.optimization_barrier((kept, routes, gate_prob))
+    kept = [kept[:, offset : offset + span] for offset, span in zip(offsets, widths)]
     meta = jnp.concatenate([routes[0].astype(jnp.float32), gate_prob[0]], 1).T.reshape(-1)
     metas = jnp.stack(ring(meta, "expert", n_expert)) if short else lax.all_gather(meta, "expert")
     acts = token_acts(metas, hidden[0, 0], groups, top, tokens // mb_count, short)
-    cot = cotangent[0]
-    kept, given = [], []
-    for offset, span in zip(offsets, widths):
-        low = cot[:, offset : offset + span]
-        high = cot[:, half_width + offset : half_width + offset + span]
-        kept.append(jnp.where(upper, high, low))
-        given.append(jnp.where(upper, low, high))
-    taken = lax.ppermute(jnp.concatenate(given, 1), "section", mirror)
+    taken = lax.ppermute(given, "section", mirror)
     taken = [taken[:, offset : offset + span] for offset, span in zip(offsets, widths)]
     if short:
         kept_first = shift(kept[0], "expert", n_expert, 1)
@@ -230,7 +233,10 @@
     for c, (offset, span) in enumerate(zip(offsets, widths)):
         pieces = [None] * n_section
         for g, masks in enumerate(groups):
-            sums = list(product(acts[g], mirror_acts[g], cots[c], layouts[c], tokens, tile_of(span)))
+            parts = 2 if c == 0 else 1
+            sums = []
+            for part in range(parts):
+                sums += product(acts[g], mirror_acts[g], cots[c], layouts[c], tokens, tile_of(span), part, parts)
             for mask, rows in zip(masks, sums):
                 pieces[mask] = rows
                 if mask:

time: 147 us -> 144 us (0.980)
  waiting for transfers between devices: 58.8 us -> 52.3 us
  Pallas kernels: 34.4 us -> 39.9 us
  other arithmetic: 5.34 us -> 3.73 us
    ppermute x14, waiting for transfers between devices: 27.9 us -> 22 us  [local(): lax.ppermute(rows, 'section', [(i, i ^ mask) for i in range(n_section)])]
    pallas_call x4 -> x6, Pallas kernels: 21.3 us -> 26.8 us  [product(): pl.pallas_call(partial(product_kernel, tokens=tokens, layout=layout), gri...]
    ppermute x2, waiting for transfers between devices: 3.19 us -> 1.22 us  [pass_on(): return lax.ppermute(chosen, axis, [(0, 2), (2, 3), (3, 1), (1, 0)])]
    select_n x2, other arithmetic: 2.87 us -> 1.4 us  [the longest x1 1.34 us: local(): given = jnp.where(upper, cot[:, :half_width], cot[:, half_width:])]
    unnamed x52 -> x50, local copies, waits for them, and re-layouts: 4 us -> 3.05 us
  transfers between devices with their start and end apart: 27 -> 27, of which waited for: 16 -> 11; matrix products, arithmetic and copies ran while one was open for 3% -> 4% of each run, Pallas kernels for 21% -> 26%
where the time goes in v4:
time: 144 us
  waiting for transfers between devices  52.3 us (36%)
  starting transfers between devices  41.4 us (29%)
  Pallas kernels  39.9 us (28%)
  local copies, waits for them, and re-layouts  5.95 us (4%)
  other arithmetic  3.73 us (3%)
    pallas_call x6, Pallas kernels, product(): pl.pallas_call(partial(product_kernel, tokens=tokens, layout=layout), gri...  26.8 us
    ppermute x14, waiting for transfers between devices, local(): lax.ppermute(rows, 'section', [(i, i ^ mask) for i in range(n_section)])  22 us
    ppermute x14, starting transfers between devices, local(): lax.ppermute(rows, 'section', [(i, i ^ mask) for i in range(n_section)])  16.7 us
    ppermute x7, waiting for transfers between devices, shift(): lax.ppermute(block, axis, [(i, (i + step) % size) for i in range(size)])  15.6 us
    ppermute x7, starting transfers between devices, shift(): lax.ppermute(block, axis, [(i, (i + step) % size) for i in range(size)])  12.1 us
    pallas_call x2, Pallas kernels, join(): pl.pallas_call(partial(join_kernel, masks=masks, sections=sections, offse...  7.1 us
    ppermute x2, waiting for transfers between devices, local(): mirror_acts = [lax.ppermute(group, 'section', mirror) for group in held]  6.86 us
    all_to_all x1, waiting for transfers between devices, local(): lax.all_to_all(later, 'expert', split_axis=0, concat_axis=0, tiled=True)  6.65 us
  transfers between devices with their start and end apart: 27, of which 11 were waited for; matrix products, arithmetic and copies ran while one was open for 4% of the time, Pallas kernels for 26%

profile of v4, /device:TPU:0, one launch (start us, length us, event | category | flops | bytes accessed | tf_op | source)
XLA Modules:
  0.0 143.5 jit_solution(9766159915351929248)
XLA Ops:
  0.0 1.3 slice_select_fusion
  1.4 3.4 %collective-permute-start.3 = (bf16[128,2048]{1,0:T(8,128)(2,1)S(1)}, bf16[128,2048]{1,0:T(8,128)(2,1)S(1)}, u32[]{:S(2)}, u32[]{:S(2)}) collective-permute-start(bf16[128,2048]{1,0:T(8,128)(2,1)S(1)} %slice_select_fusion), channel_id=1, source_target_pairs={{0,28},{4,24},{8,20},{12,16},{16,12},{20,8},{24,4},{28,0},{1,29},{... | collective-permute-start | bytes 1572872 | tf_op jit(solution)/shard_map/ppermute | solution.py:207
  4.9 3.7 %collective-permute-start.2 = (f32[512]{0:T(512)S(1)}, f32[512]{0:T(512)S(1)}, u32[]{:S(2)}, u32[]{:S(2)}) collective-permute-start(f32[512]{0:T(512)S(1)} %get-tuple-element.86), channel_id=1, source_target_pairs={{0,3},{1,0},{2,1},{3,2},{4,7},{5,4},{6,5},{7,6},{8,11},{9,8},{10,9... | collective-permute-start | bytes 6152 | tf_op jit(solution)/shard_map/ppermute | solution.py:143
  8.5 1.0 collective-permute-start
  9.5 0.8 slice.29
  10.3 2.5 %collective-permute-start.7 = (bf16[128,1280]{1,0:T(8,128)(2,1)}, bf16[128,1280]{1,0:T(8,128)(2,1)S(1)}, u32[]{:S(2)}, u32[]{:S(2)}) collective-permute-start(bf16[128,1280]{1,0:T(8,128)(2,1)} %slice.29), channel_id=1, source_target_pairs={{0,1},{1,2},{2,3},{3,0},{4,5},{5,6},{6,7},{7,4},{8,9},{9,10},{10,1... | collective-permute-start | bytes 983048 | tf_op jit(solution)/shard_map/ppermute | solution.py:143
  12.8 1.3 collective-permute-start.8
  14.8 3.4 %shard_map.46 = (bf16[4,192,512]{2,1,0:T(8,128)(2,1)}, bf16[4,192,512]{2,1,0:T(8,128)(2,1)}) custom-call(f32[4,512]{1,0:T(4,128)} %pad_maximum_fusion.meta_ref, bf16[2,4,64,1536]{3,2,1,0:T(8,128)(2,1)} %bitcast.50), custom_call_target="tpu_custom_call" | custom-call | flops 1000000 | bytes 1000 | tf_op jit(solution)/shard_map/pallas_call | solution.py:57
  18.1 0.8 slice.34
  19.0 2.0 %collective-permute-start.6 = (bf16[4,192,512]{2,1,0:T(8,128)(2,1)}, bf16[4,192,512]{2,1,0:T(8,128)(2,1)S(1)}, u32[]{:S(2)}, u32[]{:S(2)}) collective-permute-start(bf16[4,192,512]{2,1,0:T(8,128)(2,1)} %get-tuple-element.49.own_ref), channel_id=1, source_target_pairs={{0,28},{4,24},{8,20},{12,16},{16,12},{20,8},{24,4},{28,0},{1,29},{... | collective-permute-start | bytes 2359304 | tf_op jit(solution)/shard_map/ppermute | solution.py:212
  21.8 3.6 %collective-permute-start.5 = (bf16[128,1280]{1,0:T(8,128)(2,1)}, bf16[128,1280]{1,0:T(8,128)(2,1)S(1)}, u32[]{:S(2)}, u32[]{:S(2)}) collective-permute-start(bf16[128,1280]{1,0:T(8,128)(2,1)} %slice.34), channel_id=1, source_target_pairs={{0,3},{1,0},{2,1},{3,2},{4,7},{5,4},{6,5},{7,6},{8,11},{9,8},{10,9... | collective-permute-start | bytes 983048 | tf_op jit(solution)/shard_map/ppermute | solution.py:143
  25.4 3.6 %collective-permute-done.8 = bf16[128,1280]{1,0:T(8,128)(2,1)S(1)} collective-permute-done((bf16[128,1280]{1,0:T(8,128)(2,1)}, bf16[128,1280]{1,0:T(8,128)(2,1)S(1)}, u32[]{:S(2)}, u32[]{:S(2)}) %collective-permute-start.8) | collective-permute-done | bytes 327712 | tf_op jit(solution)/shard_map/ppermute | solution.py:143
  29.0 0.8 select_select_fusion.1
  29.8 1.6 %collective-permute-start.9 = (bf16[128,1280]{1,0:T(8,128)(2,1)S(1)}, bf16[128,1280]{1,0:T(8,128)(2,1)S(1)}, u32[]{:S(2)}, u32[]{:S(2)}) collective-permute-start(bf16[128,1280]{1,0:T(8,128)(2,1)S(1)} %get-tuple-element.83), channel_id=1, source_target_pairs={{0,2},{2,3},{3,1},{1,0},{4,6},{6,7},{7,5},{5,4},{8,10},{10,11},{11... | collective-permute-start | bytes 983048 | tf_op jit(solution)/shard_map/ppermute | solution.py:153
  31.4 0.7 slice.35.refs_1_
  32.1 5.0 %collective-permute-done.5 = bf16[128,1280]{1,0:T(8,128)(2,1)S(1)} collective-permute-done((bf16[128,1280]{1,0:T(8,128)(2,1)}, bf16[128,1280]{1,0:T(8,128)(2,1)S(1)}, u32[]{:S(2)}, u32[]{:S(2)}) %collective-permute-start.5) | collective-permute-done | bytes 327712 | tf_op jit(solution)/shard_map/ppermute | solution.py:143
  37.1 7.0 %collective-permute-done.4.refs_2_ = bf16[128,1280]{1,0:T(8,128)(2,1)S(1)} collective-permute-done((bf16[128,1280]{1,0:T(8,128)(2,1)}, bf16[128,1280]{1,0:T(8,128)(2,1)S(1)}, u32[]{:S(2)}, u32[]{:S(2)}) %collective-permute-start.4) | collective-permute-done | bytes 327712 | tf_op jit(solution)/shard_map/ppermute | solution.py:143
  44.1 0.9 slice_bitcast_fusion
  44.9 1.2 collective-permute-start.10
  46.2 2.7 %shard_map.47 = bf16[4,256,768]{2,1,0:T(8,128)(2,1)} custom-call(bf16[128,768]{1,0:T(8,128)(2,1)} %slice.30.refs_0_, bf16[128,768]{1,0:T(8,128)(2,1)} %slice.35.refs_1_, bf16[128,1280]{1,0:T(8,128)(2,1)} %copy-done.4), custom_call_target="tpu_custom_call" | custom-call | flops 99999997952 | bytes 1000000 | tf_op jit(solution)/shard_map/pallas_call | solution.py:166
  48.9 1.2 collective-permute-done.9
  50.0 6.9 %collective-permute-done.11.mirror_ref = bf16[4,192,512]{2,1,0:T(8,128)(2,1)} collective-permute-done((bf16[4,192,512]{2,1,0:T(8,128)(2,1)S(1)}, bf16[4,192,512]{2,1,0:T(8,128)(2,1)}, u32[]{:S(2)}, u32[]{:S(2)}) %collective-permute-start.11) | collective-permute-done | bytes 786464 | tf_op jit(solution)/shard_map/ppermute | solution.py:212
  56.9 0.7 copy-done.8
  57.7 4.4 %all-to-all-start = ((bf16[4,256,768]{2,1,0:T(8,128)(2,1)}), bf16[4,256,768]{2,1,0:T(8,128)(2,1)S(1)}, u32[]{:S(2)}, u32[]{:S(2)}) async-start(bf16[4,256,768]{2,1,0:T(8,128)(2,1)} %shard_map.47), calls=%async_computation | async-start | bytes 3145728 | tf_op jit(solution)/shard_map/all_to_all | solution.py:223
  62.0 4.5 %shard_map.49 = (bf16[192,1280]{1,0:T(8,128)(2,1)}, bf16[192,1280]{1,0:T(8,128)(2,1)}) custom-call(bf16[4,192,512]{2,1,0:T(8,128)(2,1)} %get-tuple-element.54.own_ref, bf16[4,192,512]{2,1,0:T(8,128)(2,1)} %collective-permute-done.11.mirror_ref, bf16[1,128,1280]{2,1,0:T(8,128)(2,1)} %get-tuple-element.84.refs_0_, bf16[1,128,1280]{2,1,0:T(8,128)(2,1)} %bitcast.24, ...), custom_call_target="tpu_custom_call" | custom-call | flops 1000000 | bytes 1000 | tf_op jit(solution)/shard_map/pallas_call | solution.py:92
  66.5 1.6 %collective-permute-start.13 = (bf16[192,1280]{1,0:T(8,128)(2,1)}, bf16[192,1280]{1,0:T(8,128)(2,1)S(1)}, u32[]{:S(2)}, u32[]{:S(2)}) collective-permute-start(bf16[192,1280]{1,0:T(8,128)(2,1)} %get-tuple-element.60), channel_id=1, source_target_pairs={{0,8},{4,12},{8,0},{12,4},{16,24},{20,28},{24,16},{28,20},{1,9},{5... | collective-permute-start | bytes 1474568 | tf_op jit(solution)/shard_map/ppermute | solution.py:243
  68.8 4.4 %shard_map.48 = (bf16[192,1280]{1,0:T(8,128)(2,1)}, bf16[192,1280]{1,0:T(8,128)(2,1)}) custom-call(bf16[4,192,512]{2,1,0:T(8,128)(2,1)} %get-tuple-element.49.own_ref, bf16[4,192,512]{2,1,0:T(8,128)(2,1)} %copy-done.5, bf16[1,128,1280]{2,1,0:T(8,128)(2,1)} %get-tuple-element.84.refs_0_, bf16[1,128,1280]{2,1,0:T(8,128)(2,1)} %bitcast.25, ...), custom_call_target="tpu_custom_call" | custom-call | flops 1000000 | bytes 1000 | tf_op jit(solution)/shard_map/pallas_call | solution.py:92
  73.2 1.0 collective-permute-start.12
  74.6 4.4 %shard_map.53 = (bf16[192,1280]{1,0:T(8,128)(2,1)}, bf16[192,1280]{1,0:T(8,128)(2,1)}) custom-call(bf16[4,192,512]{2,1,0:T(8,128)(2,1)} %get-tuple-element.54.own_ref, bf16[4,192,512]{2,1,0:T(8,128)(2,1)} %collective-permute-done.11.mirror_ref, bf16[1,128,1280]{2,1,0:T(8,128)(2,1)} %get-tuple-element.84.refs_0_, bf16[1,128,1280]{2,1,0:T(8,128)(2,1)} %bitcast.26, ...), custom_call_target="tpu_custom_call" | custom-call | flops 1000000 | bytes 1000 | tf_op jit(solution)/shard_map/pallas_call | solution.py:92
  79.0 4.4 %shard_map.52 = (bf16[192,1280]{1,0:T(8,128)(2,1)}, bf16[192,1280]{1,0:T(8,128)(2,1)}) custom-call(bf16[4,192,512]{2,1,0:T(8,128)(2,1)} %get-tuple-element.49.own_ref, bf16[4,192,512]{2,1,0:T(8,128)(2,1)} %copy-done.5, bf16[1,128,1280]{2,1,0:T(8,128)(2,1)} %get-tuple-element.84.refs_0_, bf16[1,128,1280]{2,1,0:T(8,128)(2,1)} %bitcast.27, ...), custom_call_target="tpu_custom_call" | custom-call | flops 1000000 | bytes 1000 | tf_op jit(solution)/shard_map/pallas_call | solution.py:92
  83.4 1.1 collective-permute-start.23
  84.5 1.5 %collective-permute-start.24 = (bf16[192,1280]{1,0:T(8,128)(2,1)}, bf16[192,1280]{1,0:T(8,128)(2,1)}, u32[]{:S(2)}, u32[]{:S(2)}) collective-permute-start(bf16[192,1280]{1,0:T(8,128)(2,1)} %get-tuple-element.77), channel_id=1, source_target_pairs={{0,16},{4,20},{8,24},{12,28},{16,0},{20,4},{24,8},{28,12},{1,17},{... | collective-permute-start | bytes 1474568 | tf_op jit(solution)/shard_map/ppermute | solution.py:243
  86.0 6.1 %collective-permute-done.14.refs_5_ = bf16[192,1280]{1,0:T(8,128)(2,1)S(1)} collective-permute-done((bf16[192,1280]{1,0:T(8,128)(2,1)}, bf16[192,1280]{1,0:T(8,128)(2,1)S(1)}, u32[]{:S(2)}, u32[]{:S(2)}) %collective-permute-start.14) | collective-permute-done | bytes 491552 | tf_op jit(solution)/shard_map/ppermute | solution.py:243
  92.6 6.7 %all-to-all-done.refs_0_ = bf16[4,256,768]{2,1,0:T(8,128)(2,1)S(1)} async-done(((bf16[4,256,768]{2,1,0:T(8,128)(2,1)}), bf16[4,256,768]{2,1,0:T(8,128)(2,1)S(1)}, u32[]{:S(2)}, u32[]{:S(2)}) %all-to-all-start) | async-done | bytes 1572896 | tf_op jit(solution)/shard_map/all_to_all | solution.py:223
  99.3 1.1 copy-done
  100.4 4.6 %shard_map.51 = (bf16[192,768]{1,0:T(8,128)(2,1)}, bf16[192,768]{1,0:T(8,128)(2,1)}, bf16[192,768]{1,0:T(8,128)(2,1)}, bf16[192,768]{1,0:T(8,128)(2,1)}) custom-call(bf16[4,192,512]{2,1,0:T(8,128)(2,1)} %get-tuple-element.54.own_ref, bf16[4,192,512]{2,1,0:T(8,128)(2,1)} %collective-permute-done.11.mirror_ref, bf16[4,256,768]{2,1,0:T(8,128)(2,1)} %copy-done), custom_call_target="tpu_custom_call" | custom-call | flops 1000000 | bytes 1000 | tf_op jit(solution)/shard_map/pallas_call | solution.py:92
  105.0 1.6 %collective-permute-start.17 = (bf16[192,768]{1,0:T(8,128)(2,1)}, bf16[192,768]{1,0:T(8,128)(2,1)S(1)}, u32[]{:S(2)}, u32[]{:S(2)}) collective-permute-start(bf16[192,768]{1,0:T(8,128)(2,1)} %get-tuple-element.67), channel_id=1, source_target_pairs={{0,8},{4,12},{8,0},{12,4},{16,24},{20,28},{24,16},{28,20},{1,9},{5... | collective-permute-start | bytes 884744 | tf_op jit(solution)/shard_map/ppermute | solution.py:243
  106.6 4.5 %shard_map.50 = (bf16[192,768]{1,0:T(8,128)(2,1)}, bf16[192,768]{1,0:T(8,128)(2,1)}, bf16[192,768]{1,0:T(8,128)(2,1)}, bf16[192,768]{1,0:T(8,128)(2,1)}) custom-call(bf16[4,192,512]{2,1,0:T(8,128)(2,1)} %get-tuple-element.49.own_ref, bf16[4,192,512]{2,1,0:T(8,128)(2,1)} %copy-done.5, bf16[4,256,768]{2,1,0:T(8,128)(2,1)} %copy-done), custom_call_target="tpu_custom_call" | custom-call | flops 1000000 | bytes 1000 | tf_op jit(solution)/shard_map/pallas_call | solution.py:92
  111.1 1.6 %collective-permute-start.19 = (bf16[192,768]{1,0:T(8,128)(2,1)}, bf16[192,768]{1,0:T(8,128)(2,1)S(1)}, u32[]{:S(2)}, u32[]{:S(2)}) collective-permute-start(bf16[192,768]{1,0:T(8,128)(2,1)} %get-tuple-element.69), channel_id=1, source_target_pairs={{0,16},{4,20},{8,24},{12,28},{16,0},{20,4},{24,8},{28,12},{1,17},{... | collective-permute-start | bytes 884744 | tf_op jit(solution)/shard_map/ppermute | solution.py:243
  112.7 0.7 collective-permute-done.24.refs_4_
  113.4 1.0 collective-permute-start.20
  114.7 4.2 %collective-permute-done.17.refs_2_ = bf16[192,768]{1,0:T(8,128)(2,1)S(1)} collective-permute-done((bf16[192,768]{1,0:T(8,128)(2,1)}, bf16[192,768]{1,0:T(8,128)(2,1)S(1)}, u32[]{:S(2)}, u32[]{:S(2)}) %collective-permute-start.17) | collective-permute-done | bytes 294944 | tf_op jit(solution)/shard_map/ppermute | solution.py:243
  118.9 2.5 %collective-permute-start.21 = (bf16[192,768]{1,0:T(8,128)(2,1)}, bf16[192,768]{1,0:T(8,128)(2,1)S(1)}, u32[]{:S(2)}, u32[]{:S(2)}) collective-permute-start(bf16[192,768]{1,0:T(8,128)(2,1)} %get-tuple-element.71), channel_id=1, source_target_pairs={{0,24},{4,28},{8,16},{12,20},{16,8},{20,12},{24,0},{28,4},{1,25},{... | collective-permute-start | bytes 884744 | tf_op jit(solution)/shard_map/ppermute | solution.py:243
  121.4 3.0 %collective-permute-done.18.refs_3_ = bf16[192,768]{1,0:T(8,128)(2,1)S(1)} collective-permute-done((bf16[192,768]{1,0:T(8,128)(2,1)}, bf16[192,768]{1,0:T(8,128)(2,1)S(1)}, u32[]{:S(2)}, u32[]{:S(2)}) %collective-permute-start.18) | collective-permute-done | bytes 294944 | tf_op jit(solution)/shard_map/ppermute | solution.py:243
  124.4 3.0 %collective-permute-start.22 = (bf16[192,768]{1,0:T(8,128)(2,1)}, bf16[192,768]{1,0:T(8,128)(2,1)S(1)}, u32[]{:S(2)}, u32[]{:S(2)}) collective-permute-start(bf16[192,768]{1,0:T(8,128)(2,1)} %get-tuple-element.72), channel_id=1, source_target_pairs={{0,28},{4,24},{8,20},{12,16},{16,12},{20,8},{24,4},{28,0},{1,29},{... | collective-permute-start | bytes 884744 | tf_op jit(solution)/shard_map/ppermute | solution.py:243
  127.4 4.0 %shard_map.54.refs_8_ = bf16[4,1,192,4096]{3,2,1,0:T(8,128)(2,1)} custom-call(bf16[192,1280]{1,0:T(8,128)(2,1)} %get-tuple-element.73.refs_0_, bf16[192,1280]{1,0:T(8,128)(2,1)} %copy-done.14, bf16[192,1280]{1,0:T(8,128)(2,1)} %copy-done.12, bf16[192,1280]{1,0:T(8,128)(2,1)} %collective-permute-done.23.refs_3_, ...), custom_call_target="tpu_custom_call" | custom-call | tf_op jit(solution)/shard_map/pallas_call | solution.py:131
  131.5 7.9 %collective-permute-done.20.refs_5_ = bf16[192,768]{1,0:T(8,128)(2,1)S(1)} collective-permute-done((bf16[192,768]{1,0:T(8,128)(2,1)}, bf16[192,768]{1,0:T(8,128)(2,1)S(1)}, u32[]{:S(2)}, u32[]{:S(2)}) %collective-permute-start.20) | collective-permute-done | bytes 294944 | tf_op jit(solution)/shard_map/ppermute | solution.py:243
  140.5 3.0 %shard_map.55 = bf16[4,1,192,4096]{3,2,1,0:T(8,128)(2,1)} custom-call(bf16[192,768]{1,0:T(8,128)(2,1)} %get-tuple-element.65.refs_0_, bf16[192,768]{1,0:T(8,128)(2,1)} %copy-done.20, bf16[192,768]{1,0:T(8,128)(2,1)} %copy-done.16, bf16[192,768]{1,0:T(8,128)(2,1)} %copy-done.17, bf16[192,768]{1,0:T(8,128)(2,1)} %copy-done.18, ...), custom_call_target="tpu_custom_call", output_to_operand_aliasing={{}: (8, {})} | custom-call | tf_op jit(solution)/shard_map/pallas_call | solution.py:131
  (77 shorter events, 4.4 us)
Async XLA Ops:
  0.0 4.8 %copy-start.9 = (bf16[1,128,4096]{2,1,0:T(8,128)(2,1)S(1)}, bf16[1,128,4096]{2,1,0:T(8,128)(2,1)}, u32[]{:S(2)}) copy-start(bf16[1,128,4096]{2,1,0:T(8,128)(2,1)} %param.4) | copy-start | bytes 3145732
  0.0 4.8 %copy-start.23 = (s32[1,128,2]{1,2,0:T(2,128)S(1)}, s32[1,128,2]{1,2,0:T(2,128)}, u32[]{:S(2)}) copy-start(s32[1,128,2]{1,2,0:T(2,128)} %param.5) | copy-start | bytes 3076
  0.0 4.8 %copy-start.24 = (f32[1,128,2]{1,2,0:T(2,128)S(1)}, f32[1,128,2]{1,2,0:T(2,128)}, u32[]{:S(2)}) copy-start(f32[1,128,2]{1,2,0:T(2,128)} %param.6) | copy-start | bytes 3076
  1.4 16.8 %collective-permute-start.3 = (bf16[128,2048]{1,0:T(8,128)(2,1)S(1)}, bf16[128,2048]{1,0:T(8,128)(2,1)S(1)}, u32[]{:S(2)}, u32[]{:S(2)}) collective-permute-start(bf16[128,2048]{1,0:T(8,128)(2,1)S(1)} %slice_select_fusion), channel_id=1, source_target_pairs={{0,28},{4,24},{8,20},{12,16},{16,12},{20,8},{24,4},{28,0},{1,29},{... | collective-permute-start | bytes 1572872 | tf_op jit(solution)/shard_map/ppermute | solution.py:207
  4.9 7.9 %collective-permute-start.2 = (f32[512]{0:T(512)S(1)}, f32[512]{0:T(512)S(1)}, u32[]{:S(2)}, u32[]{:S(2)}) collective-permute-start(f32[512]{0:T(512)S(1)} %get-tuple-element.86), channel_id=1, source_target_pairs={{0,3},{1,0},{2,1},{3,2},{4,7},{5,4},{6,5},{7,6},{8,11},{9,8},{10,9... | collective-permute-start | bytes 6152 | tf_op jit(solution)/shard_map/ppermute | solution.py:143
  8.5 5.6 %collective-permute-start.1 = (f32[512]{0:T(512)S(1)}, f32[512]{0:T(512)S(1)}, u32[]{:S(2)}, u32[]{:S(2)}) collective-permute-start(f32[512]{0:T(512)S(1)} %get-tuple-element.86), channel_id=1, source_target_pairs={{0,2},{1,3},{2,0},{3,1},{4,6},{5,7},{6,4},{7,5},{8,10},{9,11},{10,... | collective-permute-start | bytes 6152 | tf_op jit(solution)/shard_map/ppermute | solution.py:143
  8.5 5.6 %collective-permute-start = (f32[512]{0:T(512)S(1)}, f32[512]{0:T(512)S(1)}, u32[]{:S(2)}, u32[]{:S(2)}) collective-permute-start(f32[512]{0:T(512)S(1)} %get-tuple-element.86), channel_id=1, source_target_pairs={{0,1},{1,2},{2,3},{3,0},{4,5},{5,6},{6,7},{7,4},{8,9},{9,10},{10,1... | collective-permute-start | bytes 6152 | tf_op jit(solution)/shard_map/ppermute | solution.py:143
  10.3 15.0 %collective-permute-start.7 = (bf16[128,1280]{1,0:T(8,128)(2,1)}, bf16[128,1280]{1,0:T(8,128)(2,1)S(1)}, u32[]{:S(2)}, u32[]{:S(2)}) collective-permute-start(bf16[128,1280]{1,0:T(8,128)(2,1)} %slice.29), channel_id=1, source_target_pairs={{0,1},{1,2},{2,3},{3,0},{4,5},{5,6},{6,7},{7,4},{8,9},{9,10},{10,1... | collective-permute-start | bytes 983048 | tf_op jit(solution)/shard_map/ppermute | solution.py:143
  12.8 16.2 %collective-permute-start.8 = (bf16[128,1280]{1,0:T(8,128)(2,1)}, bf16[128,1280]{1,0:T(8,128)(2,1)S(1)}, u32[]{:S(2)}, u32[]{:S(2)}) collective-permute-start(bf16[128,1280]{1,0:T(8,128)(2,1)} %slice.29), channel_id=1, source_target_pairs={{0,3},{1,0},{2,1},{3,2},{4,7},{5,4},{6,5},{7,6},{8,11},{9,8},{10,9... | collective-permute-start | bytes 983048 | tf_op jit(solution)/shard_map/ppermute | solution.py:143
  18.1 13.3 %copy-start.6 = (bf16[4,192,512]{2,1,0:T(8,128)(2,1)S(1)}, bf16[4,192,512]{2,1,0:T(8,128)(2,1)}, u32[]{:S(2)}) copy-start(bf16[4,192,512]{2,1,0:T(8,128)(2,1)} %get-tuple-element.54.own_ref) | copy-start | bytes 2359300
  19.0 25.0 %collective-permute-start.6 = (bf16[4,192,512]{2,1,0:T(8,128)(2,1)}, bf16[4,192,512]{2,1,0:T(8,128)(2,1)S(1)}, u32[]{:S(2)}, u32[]{:S(2)}) collective-permute-start(bf16[4,192,512]{2,1,0:T(8,128)(2,1)} %get-tuple-element.49.own_ref), channel_id=1, source_target_pairs={{0,28},{4,24},{8,20},{12,16},{16,12},{20,8},{24,4},{28,0},{1,29},{... | collective-permute-start | bytes 2359304 | tf_op jit(solution)/shard_map/ppermute | solution.py:212
  21.8 9.6 %copy-start.11 = (bf16[128,2048]{1,0:T(8,128)(2,1)S(1)}, bf16[128,2048]{1,0:T(8,128)(2,1)}, u32[]{:S(2)}) copy-start(bf16[128,2048]{1,0:T(8,128)(2,1)} %copy-done.10) | copy-start | bytes 1572868
  21.8 15.3 %collective-permute-start.5 = (bf16[128,1280]{1,0:T(8,128)(2,1)}, bf16[128,1280]{1,0:T(8,128)(2,1)S(1)}, u32[]{:S(2)}, u32[]{:S(2)}) collective-permute-start(bf16[128,1280]{1,0:T(8,128)(2,1)} %slice.34), channel_id=1, source_target_pairs={{0,3},{1,0},{2,1},{3,2},{4,7},{5,4},{6,5},{7,6},{8,11},{9,8},{10,9... | collective-permute-start | bytes 983048 | tf_op jit(solution)/shard_map/ppermute | solution.py:143
  25.3 18.7 %collective-permute-start.4 = (bf16[128,1280]{1,0:T(8,128)(2,1)}, bf16[128,1280]{1,0:T(8,128)(2,1)S(1)}, u32[]{:S(2)}, u32[]{:S(2)}) collective-permute-start(bf16[128,1280]{1,0:T(8,128)(2,1)} %slice.34), channel_id=1, source_target_pairs={{0,1},{1,2},{2,3},{3,0},{4,5},{5,6},{6,7},{7,4},{8,9},{9,10},{10,1... | collective-permute-start | bytes 983048 | tf_op jit(solution)/shard_map/ppermute | solution.py:143
  25.3 19.6 %copy-start.1 = (bf16[128,1280]{1,0:T(8,128)(2,1)}, bf16[128,1280]{1,0:T(8,128)(2,1)S(1)}, u32[]{:S(2)}) copy-start(bf16[128,1280]{1,0:T(8,128)(2,1)S(1)} %collective-permute-done.7) | copy-start | bytes 983044
  29.0 16.0 %copy-start.2 = (bf16[128,1280]{1,0:T(8,128)(2,1)}, bf16[128,1280]{1,0:T(8,128)(2,1)S(1)}, u32[]{:S(2)}) copy-start(bf16[128,1280]{1,0:T(8,128)(2,1)S(1)} %collective-permute-done.8) | copy-start | bytes 983044
  29.8 20.2 %collective-permute-start.9 = (bf16[128,1280]{1,0:T(8,128)(2,1)S(1)}, bf16[128,1280]{1,0:T(8,128)(2,1)S(1)}, u32[]{:S(2)}, u32[]{:S(2)}) collective-permute-start(bf16[128,1280]{1,0:T(8,128)(2,1)S(1)} %get-tuple-element.83), channel_id=1, source_target_pairs={{0,2},{2,3},{3,1},{1,0},{4,6},{6,7},{7,5},{5,4},{8,10},{10,11},{11... | collective-permute-start | bytes 983048 | tf_op jit(solution)/shard_map/ppermute | solution.py:153
  31.4 25.5 %collective-permute-start.11 = (bf16[4,192,512]{2,1,0:T(8,128)(2,1)S(1)}, bf16[4,192,512]{2,1,0:T(8,128)(2,1)}, u32[]{:S(2)}, u32[]{:S(2)}) collective-permute-start(bf16[4,192,512]{2,1,0:T(8,128)(2,1)S(1)} %copy-done.6), channel_id=1, source_target_pairs={{0,28},{4,24},{8,20},{12,16},{16,12},{20,8},{24,4},{28,0},{1,29},{... | collective-permute-start | bytes 2359304 | tf_op jit(solution)/shard_map/ppermute | solution.py:212
  37.1 11.7 %copy-start.3 = (bf16[128,1280]{1,0:T(8,128)(2,1)}, bf16[128,1280]{1,0:T(8,128)(2,1)S(1)}, u32[]{:S(2)}) copy-start(bf16[128,1280]{1,0:T(8,128)(2,1)S(1)} %collective-permute-done.5) | copy-start | bytes 983044
  44.1 2.1 %copy-start.4 = (bf16[128,1280]{1,0:T(8,128)(2,1)}, bf16[128,1280]{1,0:T(8,128)(2,1)S(1)}, u32[]{:S(2)}) copy-start(bf16[128,1280]{1,0:T(8,128)(2,1)S(1)} %collective-permute-done.4.refs_2_) | copy-start | bytes 983044
  44.1 4.8 %copy-start.5 = (bf16[4,192,512]{2,1,0:T(8,128)(2,1)}, bf16[4,192,512]{2,1,0:T(8,128)(2,1)S(1)}, u32[]{:S(2)}) copy-start(bf16[4,192,512]{2,1,0:T(8,128)(2,1)S(1)} %collective-permute-done.6.mirror_ref) | copy-start | bytes 2359300
  44.9 12.0 %collective-permute-start.10 = (bf16[128,1280]{1,0:T(8,128)(2,1)S(1)}, bf16[128,1280]{1,0:T(8,128)(2,1)S(1)}, u32[]{:S(2)}, u32[]{:S(2)}) collective-permute-start(bf16[128,1280]{1,0:T(8,128)(2,1)S(1)} %get-tuple-element.82), channel_id=1, source_target_pairs={{0,2},{2,3},{3,1},{1,0},{4,6},{6,7},{7,5},{5,4},{8,10},{10,11},{11... | collective-permute-start | bytes 983048 | tf_op jit(solution)/shard_map/ppermute | solution.py:153
  50.0 6.9 %copy-start.7 = (bf16[128,1280]{1,0:T(8,128)(2,1)}, bf16[128,1280]{1,0:T(8,128)(2,1)S(1)}, u32[]{:S(2)}) copy-start(bf16[128,1280]{1,0:T(8,128)(2,1)S(1)} %collective-permute-done.9) | copy-start | bytes 983044
  57.7 41.6 %all-to-all-start = ((bf16[4,256,768]{2,1,0:T(8,128)(2,1)}), bf16[4,256,768]{2,1,0:T(8,128)(2,1)S(1)}, u32[]{:S(2)}, u32[]{:S(2)}) async-start(bf16[4,256,768]{2,1,0:T(8,128)(2,1)} %shard_map.47), calls=%async_computation | async-start | bytes 3145728 | tf_op jit(solution)/shard_map/all_to_all | solution.py:223
  66.5 18.0 %collective-permute-start.13 = (bf16[192,1280]{1,0:T(8,128)(2,1)}, bf16[192,1280]{1,0:T(8,128)(2,1)S(1)}, u32[]{:S(2)}, u32[]{:S(2)}) collective-permute-start(bf16[192,1280]{1,0:T(8,128)(2,1)} %get-tuple-element.60), channel_id=1, source_target_pairs={{0,8},{4,12},{8,0},{12,4},{16,24},{20,28},{24,16},{28,20},{1,9},{5... | collective-permute-start | bytes 1474568 | tf_op jit(solution)/shard_map/ppermute | solution.py:243
  68.1 24.0 %collective-permute-start.14 = (bf16[192,1280]{1,0:T(8,128)(2,1)}, bf16[192,1280]{1,0:T(8,128)(2,1)S(1)}, u32[]{:S(2)}, u32[]{:S(2)}) collective-permute-start(bf16[192,1280]{1,0:T(8,128)(2,1)} %get-tuple-element.61), channel_id=1, source_target_pairs={{0,20},{4,16},{8,28},{12,24},{16,4},{20,0},{24,12},{28,8},{1,21},{... | collective-permute-start | bytes 1474568 | tf_op jit(solution)/shard_map/ppermute | solution.py:243
  73.2 19.4 %collective-permute-start.12 = (bf16[192,1280]{1,0:T(8,128)(2,1)}, bf16[192,1280]{1,0:T(8,128)(2,1)S(1)}, u32[]{:S(2)}, u32[]{:S(2)}) collective-permute-start(bf16[192,1280]{1,0:T(8,128)(2,1)} %get-tuple-element.58), channel_id=1, source_target_pairs={{0,4},{4,0},{8,12},{12,8},{16,20},{20,16},{24,28},{28,24},{1,5},{5... | collective-permute-start | bytes 1474568 | tf_op jit(solution)/shard_map/ppermute | solution.py:243
  74.2 18.4 %collective-permute-start.15 = (bf16[192,1280]{1,0:T(8,128)(2,1)}, bf16[192,1280]{1,0:T(8,128)(2,1)S(1)}, u32[]{:S(2)}, u32[]{:S(2)}) collective-permute-start(bf16[192,1280]{1,0:T(8,128)(2,1)} %get-tuple-element.62), channel_id=1, source_target_pairs={{0,24},{4,28},{8,16},{12,20},{16,8},{20,12},{24,0},{28,4},{1,25},{... | collective-permute-start | bytes 1474568 | tf_op jit(solution)/shard_map/ppermute | solution.py:243
  83.4 27.7 %collective-permute-start.23 = (bf16[192,1280]{1,0:T(8,128)(2,1)}, bf16[192,1280]{1,0:T(8,128)(2,1)}, u32[]{:S(2)}, u32[]{:S(2)}) collective-permute-start(bf16[192,1280]{1,0:T(8,128)(2,1)} %get-tuple-element.76), channel_id=1, source_target_pairs={{0,12},{4,8},{8,4},{12,0},{16,28},{20,24},{24,20},{28,16},{1,13},{... | collective-permute-start | bytes 1474568 | tf_op jit(solution)/shard_map/ppermute | solution.py:243
  84.5 42.9 %copy-start.12 = (bf16[192,1280]{1,0:T(8,128)(2,1)}, bf16[192,1280]{1,0:T(8,128)(2,1)S(1)}, u32[]{:S(2)}) copy-start(bf16[192,1280]{1,0:T(8,128)(2,1)S(1)} %collective-permute-done.13.refs_2_) | copy-start | bytes 1474564
  84.5 28.9 %collective-permute-start.24 = (bf16[192,1280]{1,0:T(8,128)(2,1)}, bf16[192,1280]{1,0:T(8,128)(2,1)}, u32[]{:S(2)}, u32[]{:S(2)}) collective-permute-start(bf16[192,1280]{1,0:T(8,128)(2,1)} %get-tuple-element.77), channel_id=1, source_target_pairs={{0,16},{4,20},{8,24},{12,28},{16,0},{20,4},{24,8},{28,12},{1,17},{... | collective-permute-start | bytes 1474568 | tf_op jit(solution)/shard_map/ppermute | solution.py:243
  92.1 35.3 %copy-start.13 = (bf16[192,1280]{1,0:T(8,128)(2,1)}, bf16[192,1280]{1,0:T(8,128)(2,1)S(1)}, u32[]{:S(2)}) copy-start(bf16[192,1280]{1,0:T(8,128)(2,1)S(1)} %collective-permute-done.14.refs_5_) | copy-start | bytes 1474564
  92.1 22.3 %collective-permute-start.25 = (bf16[192,1280]{1,0:T(8,128)(2,1)}, bf16[192,1280]{1,0:T(8,128)(2,1)}, u32[]{:S(2)}, u32[]{:S(2)}) collective-permute-start(bf16[192,1280]{1,0:T(8,128)(2,1)} %get-tuple-element.80), channel_id=1, source_target_pairs={{0,28},{4,24},{8,20},{12,16},{16,12},{20,8},{24,4},{28,0},{1,29},{... | collective-permute-start | bytes 1474568 | tf_op jit(solution)/shard_map/ppermute | solution.py:243
  92.6 34.8 %copy-start.14 = (bf16[192,1280]{1,0:T(8,128)(2,1)}, bf16[192,1280]{1,0:T(8,128)(2,1)S(1)}, u32[]{:S(2)}) copy-start(bf16[192,1280]{1,0:T(8,128)(2,1)S(1)} %collective-permute-done.12.refs_1_) | copy-start | bytes 1474564
  92.6 34.8 %copy-start.15 = (bf16[192,1280]{1,0:T(8,128)(2,1)}, bf16[192,1280]{1,0:T(8,128)(2,1)S(1)}, u32[]{:S(2)}) copy-start(bf16[192,1280]{1,0:T(8,128)(2,1)S(1)} %collective-permute-done.15.refs_6_) | copy-start | bytes 1474564
  99.3 1.1 copy-start
  105.0 13.9 %collective-permute-start.17 = (bf16[192,768]{1,0:T(8,128)(2,1)}, bf16[192,768]{1,0:T(8,128)(2,1)S(1)}, u32[]{:S(2)}, u32[]{:S(2)}) collective-permute-start(bf16[192,768]{1,0:T(8,128)(2,1)} %get-tuple-element.67), channel_id=1, source_target_pairs={{0,8},{4,12},{8,0},{12,4},{16,24},{20,28},{24,16},{28,20},{1,9},{5... | collective-permute-start | bytes 884744 | tf_op jit(solution)/shard_map/ppermute | solution.py:243
  106.5 17.8 %collective-permute-start.18 = (bf16[192,768]{1,0:T(8,128)(2,1)}, bf16[192,768]{1,0:T(8,128)(2,1)S(1)}, u32[]{:S(2)}, u32[]{:S(2)}) collective-permute-start(bf16[192,768]{1,0:T(8,128)(2,1)} %get-tuple-element.68), channel_id=1, source_target_pairs={{0,12},{4,8},{8,4},{12,0},{16,28},{20,24},{24,20},{28,16},{1,13},{... | collective-permute-start | bytes 884744 | tf_op jit(solution)/shard_map/ppermute | solution.py:243
  111.1 20.4 %collective-permute-start.19 = (bf16[192,768]{1,0:T(8,128)(2,1)}, bf16[192,768]{1,0:T(8,128)(2,1)S(1)}, u32[]{:S(2)}, u32[]{:S(2)}) collective-permute-start(bf16[192,768]{1,0:T(8,128)(2,1)} %get-tuple-element.69), channel_id=1, source_target_pairs={{0,16},{4,20},{8,24},{12,28},{16,0},{20,4},{24,8},{28,12},{1,17},{... | collective-permute-start | bytes 884744 | tf_op jit(solution)/shard_map/ppermute | solution.py:243
  113.4 26.0 %collective-permute-start.20 = (bf16[192,768]{1,0:T(8,128)(2,1)}, bf16[192,768]{1,0:T(8,128)(2,1)S(1)}, u32[]{:S(2)}, u32[]{:S(2)}) collective-permute-start(bf16[192,768]{1,0:T(8,128)(2,1)} %get-tuple-element.70), channel_id=1, source_target_pairs={{0,20},{4,16},{8,28},{12,24},{16,4},{20,0},{24,12},{28,8},{1,21},{... | collective-permute-start | bytes 884744 | tf_op jit(solution)/shard_map/ppermute | solution.py:243
  114.4 25.0 %collective-permute-start.16 = (bf16[192,768]{1,0:T(8,128)(2,1)}, bf16[192,768]{1,0:T(8,128)(2,1)S(1)}, u32[]{:S(2)}, u32[]{:S(2)}) collective-permute-start(bf16[192,768]{1,0:T(8,128)(2,1)} %get-tuple-element.66), channel_id=1, source_target_pairs={{0,4},{4,0},{8,12},{12,8},{16,20},{20,16},{24,28},{28,24},{1,5},{5... | collective-permute-start | bytes 884744 | tf_op jit(solution)/shard_map/ppermute | solution.py:243
  118.9 12.6 %copy-start.16 = (bf16[192,768]{1,0:T(8,128)(2,1)}, bf16[192,768]{1,0:T(8,128)(2,1)S(1)}, u32[]{:S(2)}) copy-start(bf16[192,768]{1,0:T(8,128)(2,1)S(1)} %collective-permute-done.17.refs_2_) | copy-start | bytes 884740
  118.9 20.6 %collective-permute-start.21 = (bf16[192,768]{1,0:T(8,128)(2,1)}, bf16[192,768]{1,0:T(8,128)(2,1)S(1)}, u32[]{:S(2)}, u32[]{:S(2)}) collective-permute-start(bf16[192,768]{1,0:T(8,128)(2,1)} %get-tuple-element.71), channel_id=1, source_target_pairs={{0,24},{4,28},{8,16},{12,20},{16,8},{20,12},{24,0},{28,4},{1,25},{... | collective-permute-start | bytes 884744 | tf_op jit(solution)/shard_map/ppermute | solution.py:243
  124.4 7.1 %copy-start.17 = (bf16[192,768]{1,0:T(8,128)(2,1)}, bf16[192,768]{1,0:T(8,128)(2,1)S(1)}, u32[]{:S(2)}) copy-start(bf16[192,768]{1,0:T(8,128)(2,1)S(1)} %collective-permute-done.18.refs_3_) | copy-start | bytes 884740
  124.4 15.1 %collective-permute-start.22 = (bf16[192,768]{1,0:T(8,128)(2,1)}, bf16[192,768]{1,0:T(8,128)(2,1)S(1)}, u32[]{:S(2)}, u32[]{:S(2)}) collective-permute-start(bf16[192,768]{1,0:T(8,128)(2,1)} %get-tuple-element.72), channel_id=1, source_target_pairs={{0,28},{4,24},{8,20},{12,16},{16,12},{20,8},{24,4},{28,0},{1,29},{... | collective-permute-start | bytes 884744 | tf_op jit(solution)/shard_map/ppermute | solution.py:243
  131.5 8.0 %copy-start.18 = (bf16[192,768]{1,0:T(8,128)(2,1)}, bf16[192,768]{1,0:T(8,128)(2,1)S(1)}, u32[]{:S(2)}) copy-start(bf16[192,768]{1,0:T(8,128)(2,1)S(1)} %collective-permute-done.19.refs_4_) | copy-start | bytes 884740
  139.5 0.9 copy-start.21
  139.5 1.0 copy-start.22
  (4 other events, 3.2 us)

commit v5 on v4

--- a/solution.py
+++ b/solution.py
@@ -208,9 +208,9 @@
     taken = [taken[:, offset : offset + span] for offset, span in zip(offsets, widths)]
     if short:
         kept_first = shift(kept[0], "expert", n_expert, 1)
-        *held, _ = lax.optimization_barrier((*acts, taken[0]))
+        *held, sent_back = lax.optimization_barrier((*acts, kept[0]))
         mirror_acts = [lax.ppermute(group, "section", mirror) for group in held]
-        kept_back = shift(kept[0], "expert", n_expert, 3)
+        kept_back = shift(sent_back, "expert", n_expert, 3)
         kept_passed = pass_on(kept[0], kept_first, kept_back, "expert")
         taken_first, taken_back = shift(taken[0], "expert", n_expert, 1), shift(taken[0], "expert", n_expert, 3)
         taken_first, taken_back, mirror_acts[0] = lax.optimization_barrier((taken_first, taken_back, mirror_acts[0]))

time: 144 us -> 143 us (level)
  starting transfers between devices: 41.4 us -> 34.7 us
  waiting for transfers between devices: 52.3 us -> 55.5 us
  other arithmetic: 3.73 us -> 5.65 us
    ppermute x2, waiting for transfers between devices: 6.86 us -> 13.3 us  [local(): mirror_acts = [lax.ppermute(group, 'section', mirror) for group in held]]
    ppermute x7, waiting for transfers between devices: 15.6 us -> 9.38 us  [shift(): lax.ppermute(block, axis, [(i, (i + step) % size) for i in range(size)])]
    ppermute x14, starting transfers between devices: 16.7 us -> 13.1 us  [local(): lax.ppermute(rows, 'section', [(i, i ^ mask) for i in range(n_section)])]
    ppermute x14, waiting for transfers between devices: 22 us -> 25.4 us  [local(): lax.ppermute(rows, 'section', [(i, i ^ mask) for i in range(n_section)])]
    ppermute x7, starting transfers between devices: 12.1 us -> 9.82 us  [shift(): lax.ppermute(block, axis, [(i, (i + step) % size) for i in range(size)])]
    unnamed x50 -> x46, local copies, waits for them, and re-layouts: 3.05 us -> 3 us
  transfers between devices with their start and end apart: 27 -> 27, of which waited for: 11 -> 14; matrix products, arithmetic and copies ran while one was open for 4% -> 5% of each run, Pallas kernels for 26% -> 26%
where the time goes in v5:
time: 143 us; the launch traced here: 142 us
  waiting for transfers between devices  55.5 us (39%)
  Pallas kernels  39.9 us (28%)
  starting transfers between devices  34.7 us (24%)
  local copies, waits for them, and re-layouts  6.33 us (4%)
  other arithmetic  5.65 us (4%)
    pallas_call x6, Pallas kernels, product(): pl.pallas_call(partial(product_kernel, tokens=tokens, layout=layout), gri...  26.7 us
    ppermute x14, waiting for transfers between devices, local(): lax.ppermute(rows, 'section', [(i, i ^ mask) for i in range(n_section)])  25.4 us
    ppermute x2, waiting for transfers between devices, local(): mirror_acts = [lax.ppermute(group, 'section', mirror) for group in held]  13.3 us
    ppermute x14, starting transfers between devices, local(): lax.ppermute(rows, 'section', [(i, i ^ mask) for i in range(n_section)])  13.1 us
    ppermute x7, starting transfers between devices, shift(): lax.ppermute(block, axis, [(i, (i + step) % size) for i in range(size)])  9.82 us
    ppermute x7, waiting for transfers between devices, shift(): lax.ppermute(block, axis, [(i, (i + step) % size) for i in range(size)])  9.38 us
    pallas_call x2, Pallas kernels, join(): pl.pallas_call(partial(join_kernel, masks=masks, sections=sections, offse...  7.1 us
    all_to_all x1, waiting for transfers between devices, local(): lax.all_to_all(later, 'expert', split_axis=0, concat_axis=0, tiled=True)  6.48 us
  transfers between devices with their start and end apart: 27, of which 14 were waited for; matrix products, arithmetic and copies ran while one was open for 5% of the time, Pallas kernels for 26%

profile of v5, /device:TPU:0, one launch (start us, length us, event | category | flops | bytes accessed | tf_op | source)
XLA Modules:
  0.0 142.3 jit_solution(18148092364814467306)
XLA Ops:
  0.0 2.1 %slice_select_fusion = bf16[128,2048]{1,0:T(8,128)(2,1)} fusion(bf16[128,4096]{1,0:T(8,128)(2,1)} %bitcast.48, pred[]{:T(512)S(6)} %ge.3), kind=kLoop, calls=%fused_computation | loop fusion | flops 262144 | bytes 1572865 | tf_op jit(solution)/shard_map/jit(_where)/select_n | solution.py:199
  2.1 3.3 %collective-permute-start.3 = (bf16[128,2048]{1,0:T(8,128)(2,1)}, bf16[128,2048]{1,0:T(8,128)(2,1)}, u32[]{:S(2)}, u32[]{:S(2)}) collective-permute-start(bf16[128,2048]{1,0:T(8,128)(2,1)} %slice_select_fusion), channel_id=1, source_target_pairs={{0,28},{4,24},{8,20},{12,16},{16,12},{20,8},{24,4},{28,0},{1,29},{... | collective-permute-start | bytes 1572872 | tf_op jit(solution)/shard_map/ppermute | solution.py:207
  5.6 3.7 %collective-permute-start.2 = (f32[512]{0:T(512)S(1)}, f32[512]{0:T(512)S(1)}, u32[]{:S(2)}, u32[]{:S(2)}) collective-permute-start(f32[512]{0:T(512)S(1)} %get-tuple-element.88), channel_id=1, source_target_pairs={{0,3},{1,0},{2,1},{3,2},{4,7},{5,4},{6,5},{7,6},{8,11},{9,8},{10,9... | collective-permute-start | bytes 6152 | tf_op jit(solution)/shard_map/ppermute | solution.py:143
  9.2 1.0 collective-permute-start
  10.3 2.5 %collective-permute-start.7 = (bf16[128,1280]{1,0:T(8,128)(2,1)S(1)}, bf16[128,1280]{1,0:T(8,128)(2,1)S(1)}, u32[]{:S(2)}, u32[]{:S(2)}) collective-permute-start(bf16[128,1280]{1,0:T(8,128)(2,1)S(1)} %slice.29), channel_id=1, source_target_pairs={{0,1},{1,2},{2,3},{3,0},{4,5},{5,6},{6,7},{7,4},{8,9},{9,10},{10,1... | collective-permute-start | bytes 983048 | tf_op jit(solution)/shard_map/ppermute | solution.py:143
  12.8 0.9 collective-permute-done.1
  13.7 0.9 collective-permute-done
  15.3 3.4 %shard_map.46 = (bf16[4,192,512]{2,1,0:T(8,128)(2,1)}, bf16[4,192,512]{2,1,0:T(8,128)(2,1)}) custom-call(f32[4,512]{1,0:T(4,128)} %pad_maximum_fusion.meta_ref, bf16[2,4,64,1536]{3,2,1,0:T(8,128)(2,1)} %bitcast.50), custom_call_target="tpu_custom_call" | custom-call | flops 1000000 | bytes 1000 | tf_op jit(solution)/shard_map/pallas_call | solution.py:57
  19.2 0.7 slice.30.refs_0_
  19.9 2.6 %collective-permute-start.11 = (bf16[4,192,512]{2,1,0:T(8,128)(2,1)}, bf16[4,192,512]{2,1,0:T(8,128)(2,1)S(1)}, u32[]{:S(2)}, u32[]{:S(2)}) collective-permute-start(bf16[4,192,512]{2,1,0:T(8,128)(2,1)} %get-tuple-element.56.own_ref), channel_id=1, source_target_pairs={{0,28},{4,24},{8,20},{12,16},{16,12},{20,8},{24,4},{28,0},{1,29},{... | collective-permute-start | bytes 2359304 | tf_op jit(solution)/shard_map/ppermute | solution.py:212
  22.5 1.0 slice.34
  23.5 2.1 %collective-permute-start.5 = (bf16[128,1280]{1,0:T(8,128)(2,1)S(1)}, bf16[128,1280]{1,0:T(8,128)(2,1)S(1)}, u32[]{:S(2)}, u32[]{:S(2)}) collective-permute-start(bf16[128,1280]{1,0:T(8,128)(2,1)S(1)} %slice.34), channel_id=1, source_target_pairs={{0,3},{1,0},{2,1},{3,2},{4,7},{5,4},{6,5},{7,6},{8,11},{9,8},{10,9... | collective-permute-start | bytes 983048 | tf_op jit(solution)/shard_map/ppermute | solution.py:143
  25.6 3.7 %collective-permute-done.8 = bf16[128,1280]{1,0:T(8,128)(2,1)S(1)} collective-permute-done((bf16[128,1280]{1,0:T(8,128)(2,1)S(1)}, bf16[128,1280]{1,0:T(8,128)(2,1)S(1)}, u32[]{:S(2)}, u32[]{:S(2)}) %collective-permute-start.8) | collective-permute-done | bytes 327712 | tf_op jit(solution)/shard_map/ppermute | solution.py:143
  29.3 1.0 select_select_fusion.1
  30.2 1.1 collective-permute-start.9
  31.4 1.6 %slice.35.refs_1_ = bf16[128,768]{1,0:T(8,128)(2,1)} slice(bf16[128,2048]{1,0:T(8,128)(2,1)} %collective-permute-done.3), slice={[0:128], [1280:2048]} | slice | bytes 393216 | tf_op jit(solution)/shard_map/slice | solution.py:208
  33.0 7.1 %collective-permute-done.6.mirror_ref = bf16[4,192,512]{2,1,0:T(8,128)(2,1)S(1)} collective-permute-done((bf16[4,192,512]{2,1,0:T(8,128)(2,1)}, bf16[4,192,512]{2,1,0:T(8,128)(2,1)S(1)}, u32[]{:S(2)}, u32[]{:S(2)}) %collective-permute-start.6) | collective-permute-done | bytes 786464 | tf_op jit(solution)/shard_map/ppermute | solution.py:212
  40.0 2.7 %collective-permute-done.5 = bf16[128,1280]{1,0:T(8,128)(2,1)S(1)} collective-permute-done((bf16[128,1280]{1,0:T(8,128)(2,1)S(1)}, bf16[128,1280]{1,0:T(8,128)(2,1)S(1)}, u32[]{:S(2)}, u32[]{:S(2)}) %collective-permute-start.5) | collective-permute-done | bytes 327712 | tf_op jit(solution)/shard_map/ppermute | solution.py:143
  42.7 1.2 collective-permute-done.4.refs_2_
  43.9 1.9 %slice_bitcast_fusion = (bf16[1,128,1280]{2,1,0:T(8,128)(2,1)}, bf16[128,1280]{1,0:T(8,128)(2,1)S(1)}) fusion(bf16[128,2048]{1,0:T(8,128)(2,1)} %collective-permute-done.3, bf16[128,1280]{1,0:T(8,128)(2,1)S(1)} %collective-permute-done.4.refs_2_, bf16[128,1280]{1,0:T(8,128)(2,1)S(1)} %collective-permute-done.5, pred[]{:T(512)S(6)} %eq.9, pred[]{:T(512)S(6)} %eq.8), kind=kLoop, calls=%fused_computation.8 | loop fusion | flops 327680 | bytes 1638402 | tf_op jit(solution)/shard_map/broadcast_in_dim | solution.py:225
  45.8 1.1 collective-permute-start.10
  46.9 2.7 %shard_map.47 = bf16[4,256,768]{2,1,0:T(8,128)(2,1)} custom-call(bf16[128,768]{1,0:T(8,128)(2,1)} %slice.30.refs_0_, bf16[128,768]{1,0:T(8,128)(2,1)} %slice.35.refs_1_, bf16[128,1280]{1,0:T(8,128)(2,1)} %copy-done.4), custom_call_target="tpu_custom_call" | custom-call | flops 99999997952 | bytes 1000000 | tf_op jit(solution)/shard_map/pallas_call | solution.py:166
  49.6 0.8 collective-permute-done.9
  50.3 6.2 %collective-permute-done.11.mirror_ref = bf16[4,192,512]{2,1,0:T(8,128)(2,1)S(1)} collective-permute-done((bf16[4,192,512]{2,1,0:T(8,128)(2,1)}, bf16[4,192,512]{2,1,0:T(8,128)(2,1)S(1)}, u32[]{:S(2)}, u32[]{:S(2)}) %collective-permute-start.11) | collective-permute-done | bytes 786464 | tf_op jit(solution)/shard_map/ppermute | solution.py:212
  56.8 0.7 copy-done.6
  57.6 3.6 %all-to-all-start = ((bf16[4,256,768]{2,1,0:T(8,128)(2,1)}), bf16[4,256,768]{2,1,0:T(8,128)(2,1)S(1)}, u32[]{:S(2)}, u32[]{:S(2)}) async-start(bf16[4,256,768]{2,1,0:T(8,128)(2,1)} %shard_map.47), calls=%async_computation | async-start | bytes 3145728 | tf_op jit(solution)/shard_map/all_to_all | solution.py:223
  61.2 4.5 %shard_map.49 = (bf16[192,1280]{1,0:T(8,128)(2,1)}, bf16[192,1280]{1,0:T(8,128)(2,1)}) custom-call(bf16[4,192,512]{2,1,0:T(8,128)(2,1)} %get-tuple-element.56.own_ref, bf16[4,192,512]{2,1,0:T(8,128)(2,1)} %copy-done.6, bf16[1,128,1280]{2,1,0:T(8,128)(2,1)} %get-tuple-element.86.refs_0_, bf16[1,128,1280]{2,1,0:T(8,128)(2,1)} %bitcast.24, ...), custom_call_target="tpu_custom_call" | custom-call | flops 1000000 | bytes 1000 | tf_op jit(solution)/shard_map/pallas_call | solution.py:92
  66.7 4.3 %shard_map.48 = (bf16[192,1280]{1,0:T(8,128)(2,1)}, bf16[192,1280]{1,0:T(8,128)(2,1)}) custom-call(bf16[4,192,512]{2,1,0:T(8,128)(2,1)} %get-tuple-element.51.own_ref, bf16[4,192,512]{2,1,0:T(8,128)(2,1)} %copy-done.5, bf16[1,128,1280]{2,1,0:T(8,128)(2,1)} %get-tuple-element.86.refs_0_, bf16[1,128,1280]{2,1,0:T(8,128)(2,1)} %bitcast.25, ...), custom_call_target="tpu_custom_call" | custom-call | flops 1000000 | bytes 1000 | tf_op jit(solution)/shard_map/pallas_call | solution.py:92
  71.0 0.7 collective-permute-start.12
  71.8 2.0 %collective-permute-start.15 = (bf16[192,1280]{1,0:T(8,128)(2,1)}, bf16[192,1280]{1,0:T(8,128)(2,1)S(1)}, u32[]{:S(2)}, u32[]{:S(2)}) collective-permute-start(bf16[192,1280]{1,0:T(8,128)(2,1)} %get-tuple-element.64), channel_id=1, source_target_pairs={{0,24},{4,28},{8,16},{12,20},{16,8},{20,12},{24,0},{28,4},{1,25},{... | collective-permute-start | bytes 1474568 | tf_op jit(solution)/shard_map/ppermute | solution.py:243
  73.8 4.4 %shard_map.53 = (bf16[192,1280]{1,0:T(8,128)(2,1)}, bf16[192,1280]{1,0:T(8,128)(2,1)}) custom-call(bf16[4,192,512]{2,1,0:T(8,128)(2,1)} %get-tuple-element.56.own_ref, bf16[4,192,512]{2,1,0:T(8,128)(2,1)} %copy-done.6, bf16[1,128,1280]{2,1,0:T(8,128)(2,1)} %get-tuple-element.86.refs_0_, bf16[1,128,1280]{2,1,0:T(8,128)(2,1)} %bitcast.26, ...), custom_call_target="tpu_custom_call" | custom-call | flops 1000000 | bytes 1000 | tf_op jit(solution)/shard_map/pallas_call | solution.py:92
  78.2 4.4 %shard_map.52 = (bf16[192,1280]{1,0:T(8,128)(2,1)}, bf16[192,1280]{1,0:T(8,128)(2,1)}) custom-call(bf16[4,192,512]{2,1,0:T(8,128)(2,1)} %get-tuple-element.51.own_ref, bf16[4,192,512]{2,1,0:T(8,128)(2,1)} %copy-done.5, bf16[1,128,1280]{2,1,0:T(8,128)(2,1)} %get-tuple-element.86.refs_0_, bf16[1,128,1280]{2,1,0:T(8,128)(2,1)} %bitcast.27, ...), custom_call_target="tpu_custom_call" | custom-call | flops 1000000 | bytes 1000 | tf_op jit(solution)/shard_map/pallas_call | solution.py:92
  82.7 0.9 collective-permute-start.24
  83.6 6.7 %collective-permute-done.14.refs_5_ = bf16[192,1280]{1,0:T(8,128)(2,1)S(1)} collective-permute-done((bf16[192,1280]{1,0:T(8,128)(2,1)}, bf16[192,1280]{1,0:T(8,128)(2,1)S(1)}, u32[]{:S(2)}, u32[]{:S(2)}) %collective-permute-start.14) | collective-permute-done | bytes 491552 | tf_op jit(solution)/shard_map/ppermute | solution.py:243
  90.3 1.5 %collective-permute-start.25 = (bf16[192,1280]{1,0:T(8,128)(2,1)}, bf16[192,1280]{1,0:T(8,128)(2,1)}, u32[]{:S(2)}, u32[]{:S(2)}) collective-permute-start(bf16[192,1280]{1,0:T(8,128)(2,1)} %get-tuple-element.82), channel_id=1, source_target_pairs={{0,28},{4,24},{8,20},{12,16},{16,12},{20,8},{24,4},{28,0},{1,29},{... | collective-permute-start | bytes 1474568 | tf_op jit(solution)/shard_map/ppermute | solution.py:243
  91.9 6.5 %all-to-all-done.refs_0_ = bf16[4,256,768]{2,1,0:T(8,128)(2,1)S(1)} async-done(((bf16[4,256,768]{2,1,0:T(8,128)(2,1)}), bf16[4,256,768]{2,1,0:T(8,128)(2,1)S(1)}, u32[]{:S(2)}, u32[]{:S(2)}) %all-to-all-start) | async-done | bytes 1572896 | tf_op jit(solution)/shard_map/all_to_all | solution.py:223
  98.3 1.1 copy-done
  99.5 4.6 %shard_map.51 = (bf16[192,768]{1,0:T(8,128)(2,1)}, bf16[192,768]{1,0:T(8,128)(2,1)}, bf16[192,768]{1,0:T(8,128)(2,1)}, bf16[192,768]{1,0:T(8,128)(2,1)}) custom-call(bf16[4,192,512]{2,1,0:T(8,128)(2,1)} %get-tuple-element.56.own_ref, bf16[4,192,512]{2,1,0:T(8,128)(2,1)} %copy-done.6, bf16[4,256,768]{2,1,0:T(8,128)(2,1)} %copy-done), custom_call_target="tpu_custom_call" | custom-call | flops 1000000 | bytes 1000 | tf_op jit(solution)/shard_map/pallas_call | solution.py:92
  104.6 4.6 %shard_map.50 = (bf16[192,768]{1,0:T(8,128)(2,1)}, bf16[192,768]{1,0:T(8,128)(2,1)}, bf16[192,768]{1,0:T(8,128)(2,1)}, bf16[192,768]{1,0:T(8,128)(2,1)}) custom-call(bf16[4,192,512]{2,1,0:T(8,128)(2,1)} %get-tuple-element.51.own_ref, bf16[4,192,512]{2,1,0:T(8,128)(2,1)} %copy-done.5, bf16[4,256,768]{2,1,0:T(8,128)(2,1)} %copy-done), custom_call_target="tpu_custom_call" | custom-call | flops 1000000 | bytes 1000 | tf_op jit(solution)/shard_map/pallas_call | solution.py:92
  109.1 1.4 collective-permute-start.19
  110.5 1.6 %collective-permute-start.20 = (bf16[192,768]{1,0:T(8,128)(2,1)}, bf16[192,768]{1,0:T(8,128)(2,1)S(1)}, u32[]{:S(2)}, u32[]{:S(2)}) collective-permute-start(bf16[192,768]{1,0:T(8,128)(2,1)} %get-tuple-element.72), channel_id=1, source_target_pairs={{0,20},{4,16},{8,28},{12,24},{16,4},{20,0},{24,12},{28,8},{1,21},{... | collective-permute-start | bytes 884744 | tf_op jit(solution)/shard_map/ppermute | solution.py:243
  112.2 5.9 %collective-permute-done.17.refs_2_ = bf16[192,768]{1,0:T(8,128)(2,1)S(1)} collective-permute-done((bf16[192,768]{1,0:T(8,128)(2,1)}, bf16[192,768]{1,0:T(8,128)(2,1)S(1)}, u32[]{:S(2)}, u32[]{:S(2)}) %collective-permute-start.17) | collective-permute-done | bytes 294944 | tf_op jit(solution)/shard_map/ppermute | solution.py:243
  118.1 0.9 collective-permute-start.21
  119.0 3.6 %collective-permute-done.18.refs_3_ = bf16[192,768]{1,0:T(8,128)(2,1)S(1)} collective-permute-done((bf16[192,768]{1,0:T(8,128)(2,1)}, bf16[192,768]{1,0:T(8,128)(2,1)S(1)}, u32[]{:S(2)}, u32[]{:S(2)}) %collective-permute-start.18) | collective-permute-done | bytes 294944 | tf_op jit(solution)/shard_map/ppermute | solution.py:243
  122.6 2.5 %collective-permute-start.22 = (bf16[192,768]{1,0:T(8,128)(2,1)}, bf16[192,768]{1,0:T(8,128)(2,1)S(1)}, u32[]{:S(2)}, u32[]{:S(2)}) collective-permute-start(bf16[192,768]{1,0:T(8,128)(2,1)} %get-tuple-element.74), channel_id=1, source_target_pairs={{0,28},{4,24},{8,20},{12,16},{16,12},{20,8},{24,4},{28,0},{1,29},{... | collective-permute-start | bytes 884744 | tf_op jit(solution)/shard_map/ppermute | solution.py:243
  125.0 4.0 %shard_map.54.refs_8_ = bf16[4,1,192,4096]{3,2,1,0:T(8,128)(2,1)} custom-call(bf16[192,1280]{1,0:T(8,128)(2,1)} %get-tuple-element.75.refs_0_, bf16[192,1280]{1,0:T(8,128)(2,1)} %copy-done.12, bf16[192,1280]{1,0:T(8,128)(2,1)} %copy-done.10, bf16[192,1280]{1,0:T(8,128)(2,1)} %collective-permute-done.23.refs_3_, ...), custom_call_target="tpu_custom_call" | custom-call | tf_op jit(solution)/shard_map/pallas_call | solution.py:131
  129.1 9.1 %collective-permute-done.20.refs_5_ = bf16[192,768]{1,0:T(8,128)(2,1)S(1)} collective-permute-done((bf16[192,768]{1,0:T(8,128)(2,1)}, bf16[192,768]{1,0:T(8,128)(2,1)S(1)}, u32[]{:S(2)}, u32[]{:S(2)}) %collective-permute-start.20) | collective-permute-done | bytes 294944 | tf_op jit(solution)/shard_map/ppermute | solution.py:243
  139.3 3.0 %shard_map.55 = bf16[4,1,192,4096]{3,2,1,0:T(8,128)(2,1)} custom-call(bf16[192,768]{1,0:T(8,128)(2,1)} %get-tuple-element.67.refs_0_, bf16[192,768]{1,0:T(8,128)(2,1)} %copy-done.18, bf16[192,768]{1,0:T(8,128)(2,1)} %copy-done.14, bf16[192,768]{1,0:T(8,128)(2,1)} %copy-done.15, bf16[192,768]{1,0:T(8,128)(2,1)} %copy-done.16, ...), custom_call_target="tpu_custom_call", output_to_operand_aliasing={{}: (8, {})} | custom-call | tf_op jit(solution)/shard_map/pallas_call | solution.py:131
  (73 shorter events, 4.3 us)
Async XLA Ops:
  0.0 5.5 %copy-start.9 = (bf16[1,128,4096]{2,1,0:T(8,128)(2,1)S(1)}, bf16[1,128,4096]{2,1,0:T(8,128)(2,1)}, u32[]{:S(2)}) copy-start(bf16[1,128,4096]{2,1,0:T(8,128)(2,1)} %param.4) | copy-start | bytes 3145732
  0.0 5.5 %copy-start.21 = (s32[1,128,2]{1,2,0:T(2,128)S(1)}, s32[1,128,2]{1,2,0:T(2,128)}, u32[]{:S(2)}) copy-start(s32[1,128,2]{1,2,0:T(2,128)} %param.5) | copy-start | bytes 3076
  0.0 5.6 %copy-start.22 = (f32[1,128,2]{1,2,0:T(2,128)S(1)}, f32[1,128,2]{1,2,0:T(2,128)}, u32[]{:S(2)}) copy-start(f32[1,128,2]{1,2,0:T(2,128)} %param.6) | copy-start | bytes 3076
  2.1 20.4 %collective-permute-start.3 = (bf16[128,2048]{1,0:T(8,128)(2,1)}, bf16[128,2048]{1,0:T(8,128)(2,1)}, u32[]{:S(2)}, u32[]{:S(2)}) collective-permute-start(bf16[128,2048]{1,0:T(8,128)(2,1)} %slice_select_fusion), channel_id=1, source_target_pairs={{0,28},{4,24},{8,20},{12,16},{16,12},{20,8},{24,4},{28,0},{1,29},{... | collective-permute-start | bytes 1572872 | tf_op jit(solution)/shard_map/ppermute | solution.py:207
  5.6 7.2 %collective-permute-start.2 = (f32[512]{0:T(512)S(1)}, f32[512]{0:T(512)S(1)}, u32[]{:S(2)}, u32[]{:S(2)}) collective-permute-start(f32[512]{0:T(512)S(1)} %get-tuple-element.88), channel_id=1, source_target_pairs={{0,3},{1,0},{2,1},{3,2},{4,7},{5,4},{6,5},{7,6},{8,11},{9,8},{10,9... | collective-permute-start | bytes 6152 | tf_op jit(solution)/shard_map/ppermute | solution.py:143
  9.2 4.5 %collective-permute-start.1 = (f32[512]{0:T(512)S(1)}, f32[512]{0:T(512)S(1)}, u32[]{:S(2)}, u32[]{:S(2)}) collective-permute-start(f32[512]{0:T(512)S(1)} %get-tuple-element.88), channel_id=1, source_target_pairs={{0,2},{1,3},{2,0},{3,1},{4,6},{5,7},{6,4},{7,5},{8,10},{9,11},{10,... | collective-permute-start | bytes 6152 | tf_op jit(solution)/shard_map/ppermute | solution.py:143
  9.2 5.4 %collective-permute-start = (f32[512]{0:T(512)S(1)}, f32[512]{0:T(512)S(1)}, u32[]{:S(2)}, u32[]{:S(2)}) collective-permute-start(f32[512]{0:T(512)S(1)} %get-tuple-element.88), channel_id=1, source_target_pairs={{0,1},{1,2},{2,3},{3,0},{4,5},{5,6},{6,7},{7,4},{8,9},{9,10},{10,1... | collective-permute-start | bytes 6152 | tf_op jit(solution)/shard_map/ppermute | solution.py:143
  10.3 15.3 %collective-permute-start.7 = (bf16[128,1280]{1,0:T(8,128)(2,1)S(1)}, bf16[128,1280]{1,0:T(8,128)(2,1)S(1)}, u32[]{:S(2)}, u32[]{:S(2)}) collective-permute-start(bf16[128,1280]{1,0:T(8,128)(2,1)S(1)} %slice.29), channel_id=1, source_target_pairs={{0,1},{1,2},{2,3},{3,0},{4,5},{5,6},{6,7},{7,4},{8,9},{9,10},{10,1... | collective-permute-start | bytes 983048 | tf_op jit(solution)/shard_map/ppermute | solution.py:143
  18.6 10.6 %collective-permute-start.8 = (bf16[128,1280]{1,0:T(8,128)(2,1)S(1)}, bf16[128,1280]{1,0:T(8,128)(2,1)S(1)}, u32[]{:S(2)}, u32[]{:S(2)}) collective-permute-start(bf16[128,1280]{1,0:T(8,128)(2,1)S(1)} %slice.29), channel_id=1, source_target_pairs={{0,3},{1,0},{2,1},{3,2},{4,7},{5,4},{6,5},{7,6},{8,11},{9,8},{10,9... | collective-permute-start | bytes 983048 | tf_op jit(solution)/shard_map/ppermute | solution.py:143
  19.2 20.9 %collective-permute-start.6 = (bf16[4,192,512]{2,1,0:T(8,128)(2,1)}, bf16[4,192,512]{2,1,0:T(8,128)(2,1)S(1)}, u32[]{:S(2)}, u32[]{:S(2)}) collective-permute-start(bf16[4,192,512]{2,1,0:T(8,128)(2,1)} %get-tuple-element.51.own_ref), channel_id=1, source_target_pairs={{0,28},{4,24},{8,20},{12,16},{16,12},{20,8},{24,4},{28,0},{1,29},{... | collective-permute-start | bytes 2359304 | tf_op jit(solution)/shard_map/ppermute | solution.py:212
  19.9 36.7 %collective-permute-start.11 = (bf16[4,192,512]{2,1,0:T(8,128)(2,1)}, bf16[4,192,512]{2,1,0:T(8,128)(2,1)S(1)}, u32[]{:S(2)}, u32[]{:S(2)}) collective-permute-start(bf16[4,192,512]{2,1,0:T(8,128)(2,1)} %get-tuple-element.56.own_ref), channel_id=1, source_target_pairs={{0,28},{4,24},{8,20},{12,16},{16,12},{20,8},{24,4},{28,0},{1,29},{... | collective-permute-start | bytes 2359304 | tf_op jit(solution)/shard_map/ppermute | solution.py:212
  23.5 19.2 %collective-permute-start.5 = (bf16[128,1280]{1,0:T(8,128)(2,1)S(1)}, bf16[128,1280]{1,0:T(8,128)(2,1)S(1)}, u32[]{:S(2)}, u32[]{:S(2)}) collective-permute-start(bf16[128,1280]{1,0:T(8,128)(2,1)S(1)} %slice.34), channel_id=1, source_target_pairs={{0,3},{1,0},{2,1},{3,2},{4,7},{5,4},{6,5},{7,6},{8,11},{9,8},{10,9... | collective-permute-start | bytes 983048 | tf_op jit(solution)/shard_map/ppermute | solution.py:143
  25.6 20.2 %copy-start.1 = (bf16[128,1280]{1,0:T(8,128)(2,1)}, bf16[128,1280]{1,0:T(8,128)(2,1)S(1)}, u32[]{:S(2)}) copy-start(bf16[128,1280]{1,0:T(8,128)(2,1)S(1)} %collective-permute-done.7) | copy-start | bytes 983044
  25.6 18.3 %collective-permute-start.4 = (bf16[128,1280]{1,0:T(8,128)(2,1)S(1)}, bf16[128,1280]{1,0:T(8,128)(2,1)S(1)}, u32[]{:S(2)}, u32[]{:S(2)}) collective-permute-start(bf16[128,1280]{1,0:T(8,128)(2,1)S(1)} %slice.34), channel_id=1, source_target_pairs={{0,1},{1,2},{2,3},{3,0},{4,5},{5,6},{6,7},{7,4},{8,9},{9,10},{10,1... | collective-permute-start | bytes 983048 | tf_op jit(solution)/shard_map/ppermute | solution.py:143
  29.3 16.5 %copy-start.2 = (bf16[128,1280]{1,0:T(8,128)(2,1)}, bf16[128,1280]{1,0:T(8,128)(2,1)S(1)}, u32[]{:S(2)}) copy-start(bf16[128,1280]{1,0:T(8,128)(2,1)S(1)} %collective-permute-done.8) | copy-start | bytes 983044
  30.2 20.1 %collective-permute-start.9 = (bf16[128,1280]{1,0:T(8,128)(2,1)}, bf16[128,1280]{1,0:T(8,128)(2,1)S(1)}, u32[]{:S(2)}, u32[]{:S(2)}) collective-permute-start(bf16[128,1280]{1,0:T(8,128)(2,1)} %get-tuple-element.85), channel_id=1, source_target_pairs={{0,2},{2,3},{3,1},{1,0},{4,6},{6,7},{7,5},{5,4},{8,10},{10,11},{11... | collective-permute-start | bytes 983048 | tf_op jit(solution)/shard_map/ppermute | solution.py:153
  40.0 9.5 %copy-start.5 = (bf16[4,192,512]{2,1,0:T(8,128)(2,1)}, bf16[4,192,512]{2,1,0:T(8,128)(2,1)S(1)}, u32[]{:S(2)}) copy-start(bf16[4,192,512]{2,1,0:T(8,128)(2,1)S(1)} %collective-permute-done.6.mirror_ref) | copy-start | bytes 2359300
  42.7 6.9 %copy-start.3 = (bf16[128,1280]{1,0:T(8,128)(2,1)}, bf16[128,1280]{1,0:T(8,128)(2,1)S(1)}, u32[]{:S(2)}) copy-start(bf16[128,1280]{1,0:T(8,128)(2,1)S(1)} %collective-permute-done.5) | copy-start | bytes 983044
  43.9 3.0 %copy-start.4 = (bf16[128,1280]{1,0:T(8,128)(2,1)}, bf16[128,1280]{1,0:T(8,128)(2,1)S(1)}, u32[]{:S(2)}) copy-start(bf16[128,1280]{1,0:T(8,128)(2,1)S(1)} %collective-permute-done.4.refs_2_) | copy-start | bytes 983044
  45.8 11.0 %collective-permute-start.10 = (bf16[128,1280]{1,0:T(8,128)(2,1)S(1)}, bf16[128,1280]{1,0:T(8,128)(2,1)S(1)}, u32[]{:S(2)}, u32[]{:S(2)}) collective-permute-start(bf16[128,1280]{1,0:T(8,128)(2,1)S(1)} %get-tuple-element.84), channel_id=1, source_target_pairs={{0,2},{2,3},{3,1},{1,0},{4,6},{6,7},{7,5},{5,4},{8,10},{10,11},{11... | collective-permute-start | bytes 983048 | tf_op jit(solution)/shard_map/ppermute | solution.py:153
  50.3 10.9 %copy-start.7 = (bf16[128,1280]{1,0:T(8,128)(2,1)}, bf16[128,1280]{1,0:T(8,128)(2,1)S(1)}, u32[]{:S(2)}) copy-start(bf16[128,1280]{1,0:T(8,128)(2,1)S(1)} %collective-permute-done.9) | copy-start | bytes 983044
  56.6 0.9 copy-start.6
  57.6 40.7 %all-to-all-start = ((bf16[4,256,768]{2,1,0:T(8,128)(2,1)}), bf16[4,256,768]{2,1,0:T(8,128)(2,1)S(1)}, u32[]{:S(2)}, u32[]{:S(2)}) async-start(bf16[4,256,768]{2,1,0:T(8,128)(2,1)} %shard_map.47), calls=%async_computation | async-start | bytes 3145728 | tf_op jit(solution)/shard_map/all_to_all | solution.py:223
  65.7 17.0 %collective-permute-start.13 = (bf16[192,1280]{1,0:T(8,128)(2,1)}, bf16[192,1280]{1,0:T(8,128)(2,1)S(1)}, u32[]{:S(2)}, u32[]{:S(2)}) collective-permute-start(bf16[192,1280]{1,0:T(8,128)(2,1)} %get-tuple-element.62), channel_id=1, source_target_pairs={{0,8},{4,12},{8,0},{12,4},{16,24},{20,28},{24,16},{28,20},{1,9},{5... | collective-permute-start | bytes 1474568 | tf_op jit(solution)/shard_map/ppermute | solution.py:243
  66.3 24.0 %collective-permute-start.14 = (bf16[192,1280]{1,0:T(8,128)(2,1)}, bf16[192,1280]{1,0:T(8,128)(2,1)S(1)}, u32[]{:S(2)}, u32[]{:S(2)}) collective-permute-start(bf16[192,1280]{1,0:T(8,128)(2,1)} %get-tuple-element.63), channel_id=1, source_target_pairs={{0,20},{4,16},{8,28},{12,24},{16,4},{20,0},{24,12},{28,8},{1,21},{... | collective-permute-start | bytes 1474568 | tf_op jit(solution)/shard_map/ppermute | solution.py:243
  71.0 20.8 %collective-permute-start.12 = (bf16[192,1280]{1,0:T(8,128)(2,1)}, bf16[192,1280]{1,0:T(8,128)(2,1)S(1)}, u32[]{:S(2)}, u32[]{:S(2)}) collective-permute-start(bf16[192,1280]{1,0:T(8,128)(2,1)} %get-tuple-element.60), channel_id=1, source_target_pairs={{0,4},{4,0},{8,12},{12,8},{16,20},{20,16},{24,28},{28,24},{1,5},{5... | collective-permute-start | bytes 1474568 | tf_op jit(solution)/shard_map/ppermute | solution.py:243
  71.8 20.1 %collective-permute-start.15 = (bf16[192,1280]{1,0:T(8,128)(2,1)}, bf16[192,1280]{1,0:T(8,128)(2,1)S(1)}, u32[]{:S(2)}, u32[]{:S(2)}) collective-permute-start(bf16[192,1280]{1,0:T(8,128)(2,1)} %get-tuple-element.64), channel_id=1, source_target_pairs={{0,24},{4,28},{8,16},{12,20},{16,8},{20,12},{24,0},{28,4},{1,25},{... | collective-permute-start | bytes 1474568 | tf_op jit(solution)/shard_map/ppermute | solution.py:243
  82.6 26.5 %collective-permute-start.23 = (bf16[192,1280]{1,0:T(8,128)(2,1)}, bf16[192,1280]{1,0:T(8,128)(2,1)}, u32[]{:S(2)}, u32[]{:S(2)}) collective-permute-start(bf16[192,1280]{1,0:T(8,128)(2,1)} %get-tuple-element.78), channel_id=1, source_target_pairs={{0,12},{4,8},{8,4},{12,0},{16,28},{20,24},{24,20},{28,16},{1,13},{... | collective-permute-start | bytes 1474568 | tf_op jit(solution)/shard_map/ppermute | solution.py:243
  82.7 42.3 %copy-start.10 = (bf16[192,1280]{1,0:T(8,128)(2,1)}, bf16[192,1280]{1,0:T(8,128)(2,1)S(1)}, u32[]{:S(2)}) copy-start(bf16[192,1280]{1,0:T(8,128)(2,1)S(1)} %collective-permute-done.13.refs_2_) | copy-start | bytes 1474564
  82.7 27.8 %collective-permute-start.24 = (bf16[192,1280]{1,0:T(8,128)(2,1)}, bf16[192,1280]{1,0:T(8,128)(2,1)}, u32[]{:S(2)}, u32[]{:S(2)}) collective-permute-start(bf16[192,1280]{1,0:T(8,128)(2,1)} %get-tuple-element.79), channel_id=1, source_target_pairs={{0,16},{4,20},{8,24},{12,28},{16,0},{20,4},{24,8},{28,12},{1,17},{... | collective-permute-start | bytes 1474568 | tf_op jit(solution)/shard_map/ppermute | solution.py:243
  90.3 34.7 %copy-start.11 = (bf16[192,1280]{1,0:T(8,128)(2,1)}, bf16[192,1280]{1,0:T(8,128)(2,1)S(1)}, u32[]{:S(2)}) copy-start(bf16[192,1280]{1,0:T(8,128)(2,1)S(1)} %collective-permute-done.14.refs_5_) | copy-start | bytes 1474564
  90.3 21.8 %collective-permute-start.25 = (bf16[192,1280]{1,0:T(8,128)(2,1)}, bf16[192,1280]{1,0:T(8,128)(2,1)}, u32[]{:S(2)}, u32[]{:S(2)}) collective-permute-start(bf16[192,1280]{1,0:T(8,128)(2,1)} %get-tuple-element.82), channel_id=1, source_target_pairs={{0,28},{4,24},{8,20},{12,16},{16,12},{20,8},{24,4},{28,0},{1,29},{... | collective-permute-start | bytes 1474568 | tf_op jit(solution)/shard_map/ppermute | solution.py:243
  91.8 33.2 %copy-start.12 = (bf16[192,1280]{1,0:T(8,128)(2,1)}, bf16[192,1280]{1,0:T(8,128)(2,1)S(1)}, u32[]{:S(2)}) copy-start(bf16[192,1280]{1,0:T(8,128)(2,1)S(1)} %collective-permute-done.12.refs_1_) | copy-start | bytes 1474564
  91.9 33.2 %copy-start.13 = (bf16[192,1280]{1,0:T(8,128)(2,1)}, bf16[192,1280]{1,0:T(8,128)(2,1)S(1)}, u32[]{:S(2)}) copy-start(bf16[192,1280]{1,0:T(8,128)(2,1)S(1)} %collective-permute-done.15.refs_6_) | copy-start | bytes 1474564
  98.3 1.1 copy-start
  104.0 14.1 %collective-permute-start.17 = (bf16[192,768]{1,0:T(8,128)(2,1)}, bf16[192,768]{1,0:T(8,128)(2,1)S(1)}, u32[]{:S(2)}, u32[]{:S(2)}) collective-permute-start(bf16[192,768]{1,0:T(8,128)(2,1)} %get-tuple-element.69), channel_id=1, source_target_pairs={{0,8},{4,12},{8,0},{12,4},{16,24},{20,28},{24,16},{28,20},{1,9},{5... | collective-permute-start | bytes 884744 | tf_op jit(solution)/shard_map/ppermute | solution.py:243
  104.6 18.0 %collective-permute-start.18 = (bf16[192,768]{1,0:T(8,128)(2,1)}, bf16[192,768]{1,0:T(8,128)(2,1)S(1)}, u32[]{:S(2)}, u32[]{:S(2)}) collective-permute-start(bf16[192,768]{1,0:T(8,128)(2,1)} %get-tuple-element.70), channel_id=1, source_target_pairs={{0,12},{4,8},{8,4},{12,0},{16,28},{20,24},{24,20},{28,16},{1,13},{... | collective-permute-start | bytes 884744 | tf_op jit(solution)/shard_map/ppermute | solution.py:243
  109.1 20.0 %collective-permute-start.19 = (bf16[192,768]{1,0:T(8,128)(2,1)}, bf16[192,768]{1,0:T(8,128)(2,1)S(1)}, u32[]{:S(2)}, u32[]{:S(2)}) collective-permute-start(bf16[192,768]{1,0:T(8,128)(2,1)} %get-tuple-element.71), channel_id=1, source_target_pairs={{0,16},{4,20},{8,24},{12,28},{16,0},{20,4},{24,8},{28,12},{1,17},{... | collective-permute-start | bytes 884744 | tf_op jit(solution)/shard_map/ppermute | solution.py:243
  110.5 27.7 %collective-permute-start.20 = (bf16[192,768]{1,0:T(8,128)(2,1)}, bf16[192,768]{1,0:T(8,128)(2,1)S(1)}, u32[]{:S(2)}, u32[]{:S(2)}) collective-permute-start(bf16[192,768]{1,0:T(8,128)(2,1)} %get-tuple-element.72), channel_id=1, source_target_pairs={{0,20},{4,16},{8,28},{12,24},{16,4},{20,0},{24,12},{28,8},{1,21},{... | collective-permute-start | bytes 884744 | tf_op jit(solution)/shard_map/ppermute | solution.py:243
  112.2 26.1 %collective-permute-start.16 = (bf16[192,768]{1,0:T(8,128)(2,1)}, bf16[192,768]{1,0:T(8,128)(2,1)S(1)}, u32[]{:S(2)}, u32[]{:S(2)}) collective-permute-start(bf16[192,768]{1,0:T(8,128)(2,1)} %get-tuple-element.68), channel_id=1, source_target_pairs={{0,4},{4,0},{8,12},{12,8},{16,20},{20,16},{24,28},{28,24},{1,5},{5... | collective-permute-start | bytes 884744 | tf_op jit(solution)/shard_map/ppermute | solution.py:243
  118.1 11.0 %copy-start.14 = (bf16[192,768]{1,0:T(8,128)(2,1)}, bf16[192,768]{1,0:T(8,128)(2,1)S(1)}, u32[]{:S(2)}) copy-start(bf16[192,768]{1,0:T(8,128)(2,1)S(1)} %collective-permute-done.17.refs_2_) | copy-start | bytes 884740
  118.1 20.2 %collective-permute-start.21 = (bf16[192,768]{1,0:T(8,128)(2,1)}, bf16[192,768]{1,0:T(8,128)(2,1)S(1)}, u32[]{:S(2)}, u32[]{:S(2)}) collective-permute-start(bf16[192,768]{1,0:T(8,128)(2,1)} %get-tuple-element.73), channel_id=1, source_target_pairs={{0,24},{4,28},{8,16},{12,20},{16,8},{20,12},{24,0},{28,4},{1,25},{... | collective-permute-start | bytes 884744 | tf_op jit(solution)/shard_map/ppermute | solution.py:243
  122.6 6.5 %copy-start.15 = (bf16[192,768]{1,0:T(8,128)(2,1)}, bf16[192,768]{1,0:T(8,128)(2,1)S(1)}, u32[]{:S(2)}) copy-start(bf16[192,768]{1,0:T(8,128)(2,1)S(1)} %collective-permute-done.18.refs_3_) | copy-start | bytes 884740
  122.6 15.7 %collective-permute-start.22 = (bf16[192,768]{1,0:T(8,128)(2,1)}, bf16[192,768]{1,0:T(8,128)(2,1)S(1)}, u32[]{:S(2)}, u32[]{:S(2)}) collective-permute-start(bf16[192,768]{1,0:T(8,128)(2,1)} %get-tuple-element.74), channel_id=1, source_target_pairs={{0,28},{4,24},{8,20},{12,16},{16,12},{20,8},{24,4},{28,0},{1,29},{... | collective-permute-start | bytes 884744 | tf_op jit(solution)/shard_map/ppermute | solution.py:243
  129.1 9.2 %copy-start.16 = (bf16[192,768]{1,0:T(8,128)(2,1)}, bf16[192,768]{1,0:T(8,128)(2,1)S(1)}, u32[]{:S(2)}) copy-start(bf16[192,768]{1,0:T(8,128)(2,1)S(1)} %collective-permute-done.19.refs_4_) | copy-start | bytes 884740
  138.3 0.8 copy-start.18
  138.3 0.9 copy-start.19
  138.3 1.0 copy-start.20
  (2 other events, 1.5 us)

commit v6 on v5

--- a/solution.py
+++ b/solution.py
@@ -196,9 +196,9 @@
     groups = [far, near]
     short = n_expert == 4
     cot = cotangent[0]
-    given = jnp.where(upper, cot[:, :half_width], cot[:, half_width:])
+    given = lax.dynamic_slice_in_dim(cot, jnp.where(upper, 0, half_width), half_width, 1)
     cot, given = lax.optimization_barrier((cot, given))
-    kept = jnp.where(upper, cot[:, half_width:], cot[:, :half_width])
+    kept = lax.dynamic_slice_in_dim(cot, jnp.where(upper, half_width, 0), half_width, 1)
     kept, routes, gate_prob = lax.optimization_barrier((kept, routes, gate_prob))
     kept = [kept[:, offset : offset + span] for offset, span in zip(offsets, widths)]
     meta = jnp.concatenate([routes[0].astype(jnp.float32), gate_prob[0]], 1).T.reshape(-1)

time: 143 us -> 144 us (level)
  local copies, waits for them, and re-layouts: 6.33 us -> 9.07 us
  other arithmetic: 5.65 us -> 3.63 us
  waiting for transfers between devices: 55.5 us -> 57 us
    select_n x2 -> x0, other arithmetic: 2.19 us -> none  [the longest x1 2.14 us: local(): given = jnp.where(upper, cot[:, :half_width], cot[:, half_width:])]
    ppermute x14, waiting for transfers between devices: 25.4 us -> 27.2 us  [local(): lax.ppermute(rows, 'section', [(i, i ^ mask) for i in range(n_section)])]
    ppermute x14, starting transfers between devices: 13.1 us -> 11.4 us  [local(): lax.ppermute(rows, 'section', [(i, i ^ mask) for i in range(n_section)])]
    ppermute x2, waiting for transfers between devices: 13.3 us -> 11.8 us  [local(): mirror_acts = [lax.ppermute(group, 'section', mirror) for group in held]]
    unnamed x46 -> x42, local copies, waits for them, and re-layouts: 3 us -> 4.13 us
  transfers between devices with their start and end apart: 27 -> 27, of which waited for: 14 -> 15; matrix products, arithmetic and copies ran while one was open for 5% -> 5% of each run, Pallas kernels for 26% -> 26%
where the time goes in v6:
time: 144 us; the launch traced here: 143 us
  waiting for transfers between devices  57 us (40%)
  Pallas kernels  39.8 us (28%)
  starting transfers between devices  33.4 us (23%)
  local copies, waits for them, and re-layouts  9.07 us (6%)
  other arithmetic  3.63 us (3%)
    ppermute x14, waiting for transfers between devices, local(): lax.ppermute(rows, 'section', [(i, i ^ mask) for i in range(n_section)])  27.2 us
    pallas_call x6, Pallas kernels, product(): pl.pallas_call(partial(product_kernel, tokens=tokens, layout=layout), gri...  26.6 us
    ppermute x2, waiting for transfers between devices, local(): mirror_acts = [lax.ppermute(group, 'section', mirror) for group in held]  11.8 us
    ppermute x14, starting transfers between devices, local(): lax.ppermute(rows, 'section', [(i, i ^ mask) for i in range(n_section)])  11.4 us
    ppermute x7, waiting for transfers between devices, shift(): lax.ppermute(block, axis, [(i, (i + step) % size) for i in range(size)])  10.3 us
    ppermute x7, starting transfers between devices, shift(): lax.ppermute(block, axis, [(i, (i + step) % size) for i in range(size)])  9.78 us
    pallas_call x2, Pallas kernels, join(): pl.pallas_call(partial(join_kernel, masks=masks, sections=sections, offse...  7.09 us
    all_to_all x1, waiting for transfers between devices, local(): lax.all_to_all(later, 'expert', split_axis=0, concat_axis=0, tiled=True)  6.56 us
  transfers between devices with their start and end apart: 27, of which 15 were waited for; matrix products, arithmetic and copies ran while one was open for 5% of the time, Pallas kernels for 26%

profile of v6, /device:TPU:0, one launch (start us, length us, event | category | flops | bytes accessed | tf_op | source)
XLA Modules:
  0.0 143.1 jit_solution(9906619155071293853)
XLA Ops:
  0.0 1.2 copy-done
  1.2 0.8 dynamic-slice_bitcast_fusion
  2.1 3.3 %collective-permute-start.3 = (bf16[128,2048]{1,0:T(8,128)(2,1)}, bf16[128,2048]{1,0:T(8,128)(2,1)}, u32[]{:S(2)}, u32[]{:S(2)}) collective-permute-start(bf16[128,2048]{1,0:T(8,128)(2,1)} %dynamic-slice_bitcast_fusion), channel_id=1, source_target_pairs={{0,28},{4,24},{8,20},{12,16},{16,12},{20,8},{24,4},{28,0},{1,29},{... | collective-permute-start | bytes 1572872 | tf_op jit(solution)/shard_map/ppermute | solution.py:207
  5.5 3.7 %collective-permute-start.2 = (f32[512]{0:T(512)S(1)}, f32[512]{0:T(512)S(1)}, u32[]{:S(2)}, u32[]{:S(2)}) collective-permute-start(f32[512]{0:T(512)S(1)} %get-tuple-element.88), channel_id=1, source_target_pairs={{0,3},{1,0},{2,1},{3,2},{4,7},{5,4},{6,5},{7,6},{8,11},{9,8},{10,9... | collective-permute-start | bytes 6152 | tf_op jit(solution)/shard_map/ppermute | solution.py:143
  9.2 1.0 collective-permute-start
  10.2 0.7 slice.13
  10.9 2.5 %collective-permute-start.7 = (bf16[128,1280]{1,0:T(8,128)(2,1)}, bf16[128,1280]{1,0:T(8,128)(2,1)S(1)}, u32[]{:S(2)}, u32[]{:S(2)}) collective-permute-start(bf16[128,1280]{1,0:T(8,128)(2,1)} %slice.13), channel_id=1, source_target_pairs={{0,1},{1,2},{2,3},{3,0},{4,5},{5,6},{6,7},{7,4},{8,9},{9,10},{10,1... | collective-permute-start | bytes 983048 | tf_op jit(solution)/shard_map/ppermute | solution.py:143
  13.6 0.9 collective-permute-done
  14.5 0.6 pad_maximum_fusion.meta_ref
  15.2 3.4 %shard_map.46 = (bf16[4,192,512]{2,1,0:T(8,128)(2,1)}, bf16[4,192,512]{2,1,0:T(8,128)(2,1)}) custom-call(f32[4,512]{1,0:T(4,128)} %pad_maximum_fusion.meta_ref, bf16[2,4,64,1536]{3,2,1,0:T(8,128)(2,1)} %bitcast.51), custom_call_target="tpu_custom_call" | custom-call | flops 1000000 | bytes 1000 | tf_op jit(solution)/shard_map/pallas_call | solution.py:57
  19.1 0.7 slice.14.refs_0_
  19.8 2.6 %collective-permute-start.11 = (bf16[4,192,512]{2,1,0:T(8,128)(2,1)}, bf16[4,192,512]{2,1,0:T(8,128)(2,1)}, u32[]{:S(2)}, u32[]{:S(2)}) collective-permute-start(bf16[4,192,512]{2,1,0:T(8,128)(2,1)} %get-tuple-element.56.own_ref), channel_id=1, source_target_pairs={{0,28},{4,24},{8,20},{12,16},{16,12},{20,8},{24,4},{28,0},{1,29},{... | collective-permute-start | bytes 2359304 | tf_op jit(solution)/shard_map/ppermute | solution.py:212
  22.4 1.0 slice.16
  23.4 2.1 %collective-permute-start.5 = (bf16[128,1280]{1,0:T(8,128)(2,1)S(1)}, bf16[128,1280]{1,0:T(8,128)(2,1)S(1)}, u32[]{:S(2)}, u32[]{:S(2)}) collective-permute-start(bf16[128,1280]{1,0:T(8,128)(2,1)S(1)} %slice.16), channel_id=1, source_target_pairs={{0,3},{1,0},{2,1},{3,2},{4,7},{5,4},{6,5},{7,6},{8,11},{9,8},{10,9... | collective-permute-start | bytes 983048 | tf_op jit(solution)/shard_map/ppermute | solution.py:143
  25.5 4.5 %collective-permute-done.8 = bf16[128,1280]{1,0:T(8,128)(2,1)S(1)} collective-permute-done((bf16[128,1280]{1,0:T(8,128)(2,1)}, bf16[128,1280]{1,0:T(8,128)(2,1)S(1)}, u32[]{:S(2)}, u32[]{:S(2)}) %collective-permute-start.8) | collective-permute-done | bytes 327712 | tf_op jit(solution)/shard_map/ppermute | solution.py:143
  30.0 1.0 select_select_fusion.1
  31.0 1.1 collective-permute-start.9
  32.1 1.6 %slice.17.refs_1_ = bf16[128,768]{1,0:T(8,128)(2,1)} slice(bf16[128,2048]{1,0:T(8,128)(2,1)} %collective-permute-done.3), slice={[0:128], [1280:2048]} | slice | bytes 393216 | tf_op jit(solution)/shard_map/slice | solution.py:208
  33.7 6.3 %collective-permute-done.6.mirror_ref = bf16[4,192,512]{2,1,0:T(8,128)(2,1)S(1)} collective-permute-done((bf16[4,192,512]{2,1,0:T(8,128)(2,1)}, bf16[4,192,512]{2,1,0:T(8,128)(2,1)S(1)}, u32[]{:S(2)}, u32[]{:S(2)}) %collective-permute-start.6) | collective-permute-done | bytes 786464 | tf_op jit(solution)/shard_map/ppermute | solution.py:212
  40.0 3.5 %collective-permute-done.5 = bf16[128,1280]{1,0:T(8,128)(2,1)S(1)} collective-permute-done((bf16[128,1280]{1,0:T(8,128)(2,1)S(1)}, bf16[128,1280]{1,0:T(8,128)(2,1)S(1)}, u32[]{:S(2)}, u32[]{:S(2)}) %collective-permute-start.5) | collective-permute-done | bytes 327712 | tf_op jit(solution)/shard_map/ppermute | solution.py:143
  43.4 1.2 collective-permute-done.4.refs_2_
  44.6 2.0 %slice_bitcast_fusion = (bf16[1,128,1280]{2,1,0:T(8,128)(2,1)}, bf16[128,1280]{1,0:T(8,128)(2,1)}) fusion(bf16[128,2048]{1,0:T(8,128)(2,1)} %collective-permute-done.3, bf16[128,1280]{1,0:T(8,128)(2,1)S(1)} %collective-permute-done.4.refs_2_, bf16[128,1280]{1,0:T(8,128)(2,1)S(1)} %collective-permute-done.5, pred[]{:T(512)S(6)} %eq.9, pred[]{:T(512)S(6)} %eq.8), kind=kLoop, calls=%fused_computation.8 | loop fusion | flops 327680 | bytes 1638402 | tf_op jit(solution)/shard_map/broadcast_in_dim | solution.py:225
  46.7 1.5 %collective-permute-start.10 = (bf16[128,1280]{1,0:T(8,128)(2,1)}, bf16[128,1280]{1,0:T(8,128)(2,1)S(1)}, u32[]{:S(2)}, u32[]{:S(2)}) collective-permute-start(bf16[128,1280]{1,0:T(8,128)(2,1)} %get-tuple-element.84), channel_id=1, source_target_pairs={{0,2},{2,3},{3,1},{1,0},{4,6},{6,7},{7,5},{5,4},{8,10},{10,11},{11... | collective-permute-start | bytes 983048 | tf_op jit(solution)/shard_map/ppermute | solution.py:153
  48.2 2.7 %shard_map.47 = bf16[4,256,768]{2,1,0:T(8,128)(2,1)} custom-call(bf16[128,768]{1,0:T(8,128)(2,1)} %slice.14.refs_0_, bf16[128,768]{1,0:T(8,128)(2,1)} %slice.17.refs_1_, bf16[128,1280]{1,0:T(8,128)(2,1)} %copy-done.5), custom_call_target="tpu_custom_call" | custom-call | flops 99999997952 | bytes 1000000 | tf_op jit(solution)/shard_map/pallas_call | solution.py:166
  51.1 5.5 %collective-permute-done.11.mirror_ref = bf16[4,192,512]{2,1,0:T(8,128)(2,1)} collective-permute-done((bf16[4,192,512]{2,1,0:T(8,128)(2,1)}, bf16[4,192,512]{2,1,0:T(8,128)(2,1)}, u32[]{:S(2)}, u32[]{:S(2)}) %collective-permute-start.11) | collective-permute-done | bytes 786464 | tf_op jit(solution)/shard_map/ppermute | solution.py:212
  56.6 1.0 collective-permute-done.10
  57.6 0.7 copy-done.8
  58.3 3.7 %all-to-all-start = ((bf16[4,256,768]{2,1,0:T(8,128)(2,1)}), bf16[4,256,768]{2,1,0:T(8,128)(2,1)S(1)}, u32[]{:S(2)}, u32[]{:S(2)}) async-start(bf16[4,256,768]{2,1,0:T(8,128)(2,1)} %shard_map.47), calls=%async_computation | async-start | bytes 3145728 | tf_op jit(solution)/shard_map/all_to_all | solution.py:223
  62.0 4.4 %shard_map.49 = (bf16[192,1280]{1,0:T(8,128)(2,1)}, bf16[192,1280]{1,0:T(8,128)(2,1)}) custom-call(bf16[4,192,512]{2,1,0:T(8,128)(2,1)} %get-tuple-element.56.own_ref, bf16[4,192,512]{2,1,0:T(8,128)(2,1)} %collective-permute-done.11.mirror_ref, bf16[1,128,1280]{2,1,0:T(8,128)(2,1)} %get-tuple-element.86.refs_0_, bf16[1,128,1280]{2,1,0:T(8,128)(2,1)} %bitcast.27, ...), custom_call_target="tpu_custom_call" | custom-call | flops 1000000 | bytes 1000 | tf_op jit(solution)/shard_map/pallas_call | solution.py:92
  67.0 4.3 %shard_map.48 = (bf16[192,1280]{1,0:T(8,128)(2,1)}, bf16[192,1280]{1,0:T(8,128)(2,1)}) custom-call(bf16[4,192,512]{2,1,0:T(8,128)(2,1)} %get-tuple-element.51.own_ref, bf16[4,192,512]{2,1,0:T(8,128)(2,1)} %copy-done.6, bf16[1,128,1280]{2,1,0:T(8,128)(2,1)} %get-tuple-element.86.refs_0_, bf16[1,128,1280]{2,1,0:T(8,128)(2,1)} %bitcast.28, ...), custom_call_target="tpu_custom_call" | custom-call | flops 1000000 | bytes 1000 | tf_op jit(solution)/shard_map/pallas_call | solution.py:92
  71.3 0.7 collective-permute-start.12
  72.0 2.5 %collective-permute-start.15 = (bf16[192,1280]{1,0:T(8,128)(2,1)}, bf16[192,1280]{1,0:T(8,128)(2,1)}, u32[]{:S(2)}, u32[]{:S(2)}) collective-permute-start(bf16[192,1280]{1,0:T(8,128)(2,1)} %get-tuple-element.64), channel_id=1, source_target_pairs={{0,24},{4,28},{8,16},{12,20},{16,8},{20,12},{24,0},{28,4},{1,25},{... | collective-permute-start | bytes 1474568 | tf_op jit(solution)/shard_map/ppermute | solution.py:243
  74.5 4.3 %shard_map.53 = (bf16[192,1280]{1,0:T(8,128)(2,1)}, bf16[192,1280]{1,0:T(8,128)(2,1)}) custom-call(bf16[4,192,512]{2,1,0:T(8,128)(2,1)} %get-tuple-element.56.own_ref, bf16[4,192,512]{2,1,0:T(8,128)(2,1)} %collective-permute-done.11.mirror_ref, bf16[1,128,1280]{2,1,0:T(8,128)(2,1)} %get-tuple-element.86.refs_0_, bf16[1,128,1280]{2,1,0:T(8,128)(2,1)} %bitcast.29, ...), custom_call_target="tpu_custom_call" | custom-call | flops 1000000 | bytes 1000 | tf_op jit(solution)/shard_map/pallas_call | solution.py:92
  78.8 4.5 %shard_map.52 = (bf16[192,1280]{1,0:T(8,128)(2,1)}, bf16[192,1280]{1,0:T(8,128)(2,1)}) custom-call(bf16[4,192,512]{2,1,0:T(8,128)(2,1)} %get-tuple-element.51.own_ref, bf16[4,192,512]{2,1,0:T(8,128)(2,1)} %copy-done.6, bf16[1,128,1280]{2,1,0:T(8,128)(2,1)} %get-tuple-element.86.refs_0_, bf16[1,128,1280]{2,1,0:T(8,128)(2,1)} %bitcast.30, ...), custom_call_target="tpu_custom_call" | custom-call | flops 1000000 | bytes 1000 | tf_op jit(solution)/shard_map/pallas_call | solution.py:92
  83.9 7.1 %collective-permute-done.14.refs_5_ = bf16[192,1280]{1,0:T(8,128)(2,1)S(1)} collective-permute-done((bf16[192,1280]{1,0:T(8,128)(2,1)}, bf16[192,1280]{1,0:T(8,128)(2,1)S(1)}, u32[]{:S(2)}, u32[]{:S(2)}) %collective-permute-start.14) | collective-permute-done | bytes 491552 | tf_op jit(solution)/shard_map/ppermute | solution.py:243
  91.0 1.5 %collective-permute-start.25 = (bf16[192,1280]{1,0:T(8,128)(2,1)}, bf16[192,1280]{1,0:T(8,128)(2,1)}, u32[]{:S(2)}, u32[]{:S(2)}) collective-permute-start(bf16[192,1280]{1,0:T(8,128)(2,1)} %get-tuple-element.82), channel_id=1, source_target_pairs={{0,28},{4,24},{8,20},{12,16},{16,12},{20,8},{24,4},{28,0},{1,29},{... | collective-permute-start | bytes 1474568 | tf_op jit(solution)/shard_map/ppermute | solution.py:243
  92.5 6.6 %all-to-all-done.refs_0_ = bf16[4,256,768]{2,1,0:T(8,128)(2,1)S(1)} async-done(((bf16[4,256,768]{2,1,0:T(8,128)(2,1)}), bf16[4,256,768]{2,1,0:T(8,128)(2,1)S(1)}, u32[]{:S(2)}, u32[]{:S(2)}) %all-to-all-start) | async-done | bytes 1572896 | tf_op jit(solution)/shard_map/all_to_all | solution.py:223
  99.1 1.1 copy-done.1
  100.2 4.5 %shard_map.51 = (bf16[192,768]{1,0:T(8,128)(2,1)}, bf16[192,768]{1,0:T(8,128)(2,1)}, bf16[192,768]{1,0:T(8,128)(2,1)}, bf16[192,768]{1,0:T(8,128)(2,1)}) custom-call(bf16[4,192,512]{2,1,0:T(8,128)(2,1)} %get-tuple-element.56.own_ref, bf16[4,192,512]{2,1,0:T(8,128)(2,1)} %collective-permute-done.11.mirror_ref, bf16[4,256,768]{2,1,0:T(8,128)(2,1)} %copy-done.1), custom_call_target="tpu_custom_call" | custom-call | flops 1000000 | bytes 1000 | tf_op jit(solution)/shard_map/pallas_call | solution.py:92
  105.3 4.6 %shard_map.50 = (bf16[192,768]{1,0:T(8,128)(2,1)}, bf16[192,768]{1,0:T(8,128)(2,1)}, bf16[192,768]{1,0:T(8,128)(2,1)}, bf16[192,768]{1,0:T(8,128)(2,1)}) custom-call(bf16[4,192,512]{2,1,0:T(8,128)(2,1)} %get-tuple-element.51.own_ref, bf16[4,192,512]{2,1,0:T(8,128)(2,1)} %copy-done.6, bf16[4,256,768]{2,1,0:T(8,128)(2,1)} %copy-done.1), custom_call_target="tpu_custom_call" | custom-call | flops 1000000 | bytes 1000 | tf_op jit(solution)/shard_map/pallas_call | solution.py:92
  111.0 1.9 %collective-permute-start.20 = (bf16[192,768]{1,0:T(8,128)(2,1)S(1)}, bf16[192,768]{1,0:T(8,128)(2,1)S(1)}, u32[]{:S(2)}, u32[]{:S(2)}) collective-permute-start(bf16[192,768]{1,0:T(8,128)(2,1)S(1)} %copy-done.20), channel_id=1, source_target_pairs={{0,20},{4,16},{8,28},{12,24},{16,4},{20,0},{24,12},{28,8},{1,21},{... | collective-permute-start | bytes 884744 | tf_op jit(solution)/shard_map/ppermute | solution.py:243
  112.9 5.9 %collective-permute-done.17.refs_2_ = bf16[192,768]{1,0:T(8,128)(2,1)S(1)} collective-permute-done((bf16[192,768]{1,0:T(8,128)(2,1)}, bf16[192,768]{1,0:T(8,128)(2,1)S(1)}, u32[]{:S(2)}, u32[]{:S(2)}) %collective-permute-start.17) | collective-permute-done | bytes 294944 | tf_op jit(solution)/shard_map/ppermute | solution.py:243
  119.3 4.0 %collective-permute-done.18.refs_3_ = bf16[192,768]{1,0:T(8,128)(2,1)S(1)} collective-permute-done((bf16[192,768]{1,0:T(8,128)(2,1)}, bf16[192,768]{1,0:T(8,128)(2,1)S(1)}, u32[]{:S(2)}, u32[]{:S(2)}) %collective-permute-start.18) | collective-permute-done | bytes 294944 | tf_op jit(solution)/shard_map/ppermute | solution.py:243
  123.3 2.0 %collective-permute-start.22 = (bf16[192,768]{1,0:T(8,128)(2,1)}, bf16[192,768]{1,0:T(8,128)(2,1)S(1)}, u32[]{:S(2)}, u32[]{:S(2)}) collective-permute-start(bf16[192,768]{1,0:T(8,128)(2,1)} %get-tuple-element.74), channel_id=1, source_target_pairs={{0,28},{4,24},{8,20},{12,16},{16,12},{20,8},{24,4},{28,0},{1,29},{... | collective-permute-start | bytes 884744 | tf_op jit(solution)/shard_map/ppermute | solution.py:243
  125.3 4.0 %shard_map.54.refs_8_ = bf16[4,1,192,4096]{3,2,1,0:T(8,128)(2,1)} custom-call(bf16[192,1280]{1,0:T(8,128)(2,1)} %get-tuple-element.75.refs_0_, bf16[192,1280]{1,0:T(8,128)(2,1)} %collective-permute-done.12.refs_1_, bf16[192,1280]{1,0:T(8,128)(2,1)} %copy-done.9, bf16[192,1280]{1,0:T(8,128)(2,1)} %collective-permute-done.23.refs_3_, ...), custom_call_target="tpu_custom_call" | custom-call | tf_op jit(solution)/shard_map/pallas_call | solution.py:131
  129.4 9.6 %collective-permute-done.20.refs_5_ = bf16[192,768]{1,0:T(8,128)(2,1)S(1)} collective-permute-done((bf16[192,768]{1,0:T(8,128)(2,1)S(1)}, bf16[192,768]{1,0:T(8,128)(2,1)S(1)}, u32[]{:S(2)}, u32[]{:S(2)}) %collective-permute-start.20) | collective-permute-done | bytes 294944 | tf_op jit(solution)/shard_map/ppermute | solution.py:243
  139.1 0.7 copy-done.14
  140.0 3.0 %shard_map.55 = bf16[4,1,192,4096]{3,2,1,0:T(8,128)(2,1)} custom-call(bf16[192,768]{1,0:T(8,128)(2,1)} %get-tuple-element.67.refs_0_, bf16[192,768]{1,0:T(8,128)(2,1)} %copy-done.15, bf16[192,768]{1,0:T(8,128)(2,1)} %copy-done.11, bf16[192,768]{1,0:T(8,128)(2,1)} %copy-done.12, bf16[192,768]{1,0:T(8,128)(2,1)} %copy-done.13, ...), custom_call_target="tpu_custom_call", output_to_operand_aliasing={{}: (8, {})} | custom-call | tf_op jit(solution)/shard_map/pallas_call | solution.py:131
  (69 shorter events, 4.8 us)
Async XLA Ops:
  0.0 1.2 copy-start
  0.0 5.5 %copy-start.19 = (f32[1,128,2]{1,2,0:T(2,128)S(1)}, f32[1,128,2]{1,2,0:T(2,128)}, u32[]{:S(2)}) copy-start(f32[1,128,2]{1,2,0:T(2,128)} %param.6) | copy-start | bytes 3076
  0.0 5.5 %copy-start.18 = (s32[1,128,2]{1,2,0:T(2,128)S(1)}, s32[1,128,2]{1,2,0:T(2,128)}, u32[]{:S(2)}) copy-start(s32[1,128,2]{1,2,0:T(2,128)} %param.5) | copy-start | bytes 3076
  2.1 20.4 %collective-permute-start.3 = (bf16[128,2048]{1,0:T(8,128)(2,1)}, bf16[128,2048]{1,0:T(8,128)(2,1)}, u32[]{:S(2)}, u32[]{:S(2)}) collective-permute-start(bf16[128,2048]{1,0:T(8,128)(2,1)} %dynamic-slice_bitcast_fusion), channel_id=1, source_target_pairs={{0,28},{4,24},{8,20},{12,16},{16,12},{20,8},{24,4},{28,0},{1,29},{... | collective-permute-start | bytes 1572872 | tf_op jit(solution)/shard_map/ppermute | solution.py:207
  5.5 7.9 %collective-permute-start.2 = (f32[512]{0:T(512)S(1)}, f32[512]{0:T(512)S(1)}, u32[]{:S(2)}, u32[]{:S(2)}) collective-permute-start(f32[512]{0:T(512)S(1)} %get-tuple-element.88), channel_id=1, source_target_pairs={{0,3},{1,0},{2,1},{3,2},{4,7},{5,4},{6,5},{7,6},{8,11},{9,8},{10,9... | collective-permute-start | bytes 6152 | tf_op jit(solution)/shard_map/ppermute | solution.py:143
  9.2 4.5 %collective-permute-start.1 = (f32[512]{0:T(512)S(1)}, f32[512]{0:T(512)S(1)}, u32[]{:S(2)}, u32[]{:S(2)}) collective-permute-start(f32[512]{0:T(512)S(1)} %get-tuple-element.88), channel_id=1, source_target_pairs={{0,2},{1,3},{2,0},{3,1},{4,6},{5,7},{6,4},{7,5},{8,10},{9,11},{10,... | collective-permute-start | bytes 6152 | tf_op jit(solution)/shard_map/ppermute | solution.py:143
  9.2 5.4 %collective-permute-start = (f32[512]{0:T(512)S(1)}, f32[512]{0:T(512)S(1)}, u32[]{:S(2)}, u32[]{:S(2)}) collective-permute-start(f32[512]{0:T(512)S(1)} %get-tuple-element.88), channel_id=1, source_target_pairs={{0,1},{1,2},{2,3},{3,0},{4,5},{5,6},{6,7},{7,4},{8,9},{9,10},{10,1... | collective-permute-start | bytes 6152 | tf_op jit(solution)/shard_map/ppermute | solution.py:143
  10.9 14.6 %collective-permute-start.7 = (bf16[128,1280]{1,0:T(8,128)(2,1)}, bf16[128,1280]{1,0:T(8,128)(2,1)S(1)}, u32[]{:S(2)}, u32[]{:S(2)}) collective-permute-start(bf16[128,1280]{1,0:T(8,128)(2,1)} %slice.13), channel_id=1, source_target_pairs={{0,1},{1,2},{2,3},{3,0},{4,5},{5,6},{6,7},{7,4},{8,9},{9,10},{10,1... | collective-permute-start | bytes 983048 | tf_op jit(solution)/shard_map/ppermute | solution.py:143
  18.5 11.5 %collective-permute-start.8 = (bf16[128,1280]{1,0:T(8,128)(2,1)}, bf16[128,1280]{1,0:T(8,128)(2,1)S(1)}, u32[]{:S(2)}, u32[]{:S(2)}) collective-permute-start(bf16[128,1280]{1,0:T(8,128)(2,1)} %slice.13), channel_id=1, source_target_pairs={{0,3},{1,0},{2,1},{3,2},{4,7},{5,4},{6,5},{7,6},{8,11},{9,8},{10,9... | collective-permute-start | bytes 983048 | tf_op jit(solution)/shard_map/ppermute | solution.py:143
  19.1 20.9 %collective-permute-start.6 = (bf16[4,192,512]{2,1,0:T(8,128)(2,1)}, bf16[4,192,512]{2,1,0:T(8,128)(2,1)S(1)}, u32[]{:S(2)}, u32[]{:S(2)}) collective-permute-start(bf16[4,192,512]{2,1,0:T(8,128)(2,1)} %get-tuple-element.51.own_ref), channel_id=1, source_target_pairs={{0,28},{4,24},{8,20},{12,16},{16,12},{20,8},{24,4},{28,0},{1,29},{... | collective-permute-start | bytes 2359304 | tf_op jit(solution)/shard_map/ppermute | solution.py:212
  19.8 36.8 %collective-permute-start.11 = (bf16[4,192,512]{2,1,0:T(8,128)(2,1)}, bf16[4,192,512]{2,1,0:T(8,128)(2,1)}, u32[]{:S(2)}, u32[]{:S(2)}) collective-permute-start(bf16[4,192,512]{2,1,0:T(8,128)(2,1)} %get-tuple-element.56.own_ref), channel_id=1, source_target_pairs={{0,28},{4,24},{8,20},{12,16},{16,12},{20,8},{24,4},{28,0},{1,29},{... | collective-permute-start | bytes 2359304 | tf_op jit(solution)/shard_map/ppermute | solution.py:212
  23.4 20.0 %collective-permute-start.5 = (bf16[128,1280]{1,0:T(8,128)(2,1)S(1)}, bf16[128,1280]{1,0:T(8,128)(2,1)S(1)}, u32[]{:S(2)}, u32[]{:S(2)}) collective-permute-start(bf16[128,1280]{1,0:T(8,128)(2,1)S(1)} %slice.16), channel_id=1, source_target_pairs={{0,3},{1,0},{2,1},{3,2},{4,7},{5,4},{6,5},{7,6},{8,11},{9,8},{10,9... | collective-permute-start | bytes 983048 | tf_op jit(solution)/shard_map/ppermute | solution.py:143
  25.5 21.2 %copy-start.2 = (bf16[128,1280]{1,0:T(8,128)(2,1)}, bf16[128,1280]{1,0:T(8,128)(2,1)S(1)}, u32[]{:S(2)}) copy-start(bf16[128,1280]{1,0:T(8,128)(2,1)S(1)} %collective-permute-done.7) | copy-start | bytes 983044
  25.5 19.1 %collective-permute-start.4 = (bf16[128,1280]{1,0:T(8,128)(2,1)S(1)}, bf16[128,1280]{1,0:T(8,128)(2,1)S(1)}, u32[]{:S(2)}, u32[]{:S(2)}) collective-permute-start(bf16[128,1280]{1,0:T(8,128)(2,1)S(1)} %slice.16), channel_id=1, source_target_pairs={{0,1},{1,2},{2,3},{3,0},{4,5},{5,6},{6,7},{7,4},{8,9},{9,10},{10,1... | collective-permute-start | bytes 983048 | tf_op jit(solution)/shard_map/ppermute | solution.py:143
  30.0 16.7 %copy-start.3 = (bf16[128,1280]{1,0:T(8,128)(2,1)}, bf16[128,1280]{1,0:T(8,128)(2,1)S(1)}, u32[]{:S(2)}) copy-start(bf16[128,1280]{1,0:T(8,128)(2,1)S(1)} %collective-permute-done.8) | copy-start | bytes 983044
  31.0 20.1 %collective-permute-start.9 = (bf16[128,1280]{1,0:T(8,128)(2,1)}, bf16[128,1280]{1,0:T(8,128)(2,1)S(1)}, u32[]{:S(2)}, u32[]{:S(2)}) collective-permute-start(bf16[128,1280]{1,0:T(8,128)(2,1)} %get-tuple-element.85), channel_id=1, source_target_pairs={{0,2},{2,3},{3,1},{1,0},{4,6},{6,7},{7,5},{5,4},{8,10},{10,11},{11... | collective-permute-start | bytes 983048 | tf_op jit(solution)/shard_map/ppermute | solution.py:153
  40.0 10.9 %copy-start.6 = (bf16[4,192,512]{2,1,0:T(8,128)(2,1)}, bf16[4,192,512]{2,1,0:T(8,128)(2,1)S(1)}, u32[]{:S(2)}) copy-start(bf16[4,192,512]{2,1,0:T(8,128)(2,1)S(1)} %collective-permute-done.6.mirror_ref) | copy-start | bytes 2359300
  43.4 7.4 %copy-start.4 = (bf16[128,1280]{1,0:T(8,128)(2,1)}, bf16[128,1280]{1,0:T(8,128)(2,1)S(1)}, u32[]{:S(2)}) copy-start(bf16[128,1280]{1,0:T(8,128)(2,1)S(1)} %collective-permute-done.5) | copy-start | bytes 983044
  44.6 3.5 %copy-start.5 = (bf16[128,1280]{1,0:T(8,128)(2,1)}, bf16[128,1280]{1,0:T(8,128)(2,1)S(1)}, u32[]{:S(2)}) copy-start(bf16[128,1280]{1,0:T(8,128)(2,1)S(1)} %collective-permute-done.4.refs_2_) | copy-start | bytes 983044
  46.7 10.9 %collective-permute-start.10 = (bf16[128,1280]{1,0:T(8,128)(2,1)}, bf16[128,1280]{1,0:T(8,128)(2,1)S(1)}, u32[]{:S(2)}, u32[]{:S(2)}) collective-permute-start(bf16[128,1280]{1,0:T(8,128)(2,1)} %get-tuple-element.84), channel_id=1, source_target_pairs={{0,2},{2,3},{3,1},{1,0},{4,6},{6,7},{7,5},{5,4},{8,10},{10,11},{11... | collective-permute-start | bytes 983048 | tf_op jit(solution)/shard_map/ppermute | solution.py:153
  51.1 6.5 %copy-start.7 = (bf16[128,1280]{1,0:T(8,128)(2,1)}, bf16[128,1280]{1,0:T(8,128)(2,1)S(1)}, u32[]{:S(2)}) copy-start(bf16[128,1280]{1,0:T(8,128)(2,1)S(1)} %collective-permute-done.9) | copy-start | bytes 983044
  57.6 0.7 copy-start.8
  58.3 40.8 %all-to-all-start = ((bf16[4,256,768]{2,1,0:T(8,128)(2,1)}), bf16[4,256,768]{2,1,0:T(8,128)(2,1)S(1)}, u32[]{:S(2)}, u32[]{:S(2)}) async-start(bf16[4,256,768]{2,1,0:T(8,128)(2,1)} %shard_map.47), calls=%async_computation | async-start | bytes 3145728 | tf_op jit(solution)/shard_map/all_to_all | solution.py:223
  66.4 17.0 %collective-permute-start.13 = (bf16[192,1280]{1,0:T(8,128)(2,1)}, bf16[192,1280]{1,0:T(8,128)(2,1)S(1)}, u32[]{:S(2)}, u32[]{:S(2)}) collective-permute-start(bf16[192,1280]{1,0:T(8,128)(2,1)} %get-tuple-element.62), channel_id=1, source_target_pairs={{0,8},{4,12},{8,0},{12,4},{16,24},{20,28},{24,16},{28,20},{1,9},{5... | collective-permute-start | bytes 1474568 | tf_op jit(solution)/shard_map/ppermute | solution.py:243
  67.0 24.0 %collective-permute-start.14 = (bf16[192,1280]{1,0:T(8,128)(2,1)}, bf16[192,1280]{1,0:T(8,128)(2,1)S(1)}, u32[]{:S(2)}, u32[]{:S(2)}) collective-permute-start(bf16[192,1280]{1,0:T(8,128)(2,1)} %get-tuple-element.63), channel_id=1, source_target_pairs={{0,20},{4,16},{8,28},{12,24},{16,4},{20,0},{24,12},{28,8},{1,21},{... | collective-permute-start | bytes 1474568 | tf_op jit(solution)/shard_map/ppermute | solution.py:243
  71.3 21.2 %collective-permute-start.12 = (bf16[192,1280]{1,0:T(8,128)(2,1)}, bf16[192,1280]{1,0:T(8,128)(2,1)}, u32[]{:S(2)}, u32[]{:S(2)}) collective-permute-start(bf16[192,1280]{1,0:T(8,128)(2,1)} %get-tuple-element.60), channel_id=1, source_target_pairs={{0,4},{4,0},{8,12},{12,8},{16,20},{20,16},{24,28},{28,24},{1,5},{5... | collective-permute-start | bytes 1474568 | tf_op jit(solution)/shard_map/ppermute | solution.py:243
  72.0 20.5 %collective-permute-start.15 = (bf16[192,1280]{1,0:T(8,128)(2,1)}, bf16[192,1280]{1,0:T(8,128)(2,1)}, u32[]{:S(2)}, u32[]{:S(2)}) collective-permute-start(bf16[192,1280]{1,0:T(8,128)(2,1)} %get-tuple-element.64), channel_id=1, source_target_pairs={{0,24},{4,28},{8,16},{12,20},{16,8},{20,12},{24,0},{28,4},{1,25},{... | collective-permute-start | bytes 1474568 | tf_op jit(solution)/shard_map/ppermute | solution.py:243
  83.3 26.6 %collective-permute-start.23 = (bf16[192,1280]{1,0:T(8,128)(2,1)}, bf16[192,1280]{1,0:T(8,128)(2,1)}, u32[]{:S(2)}, u32[]{:S(2)}) collective-permute-start(bf16[192,1280]{1,0:T(8,128)(2,1)} %get-tuple-element.78), channel_id=1, source_target_pairs={{0,12},{4,8},{8,4},{12,0},{16,28},{20,24},{24,20},{28,16},{1,13},{... | collective-permute-start | bytes 1474568 | tf_op jit(solution)/shard_map/ppermute | solution.py:243
  83.4 41.9 %copy-start.9 = (bf16[192,1280]{1,0:T(8,128)(2,1)}, bf16[192,1280]{1,0:T(8,128)(2,1)S(1)}, u32[]{:S(2)}) copy-start(bf16[192,1280]{1,0:T(8,128)(2,1)S(1)} %collective-permute-done.13.refs_2_) | copy-start | bytes 1474564
  83.4 27.6 %collective-permute-start.24 = (bf16[192,1280]{1,0:T(8,128)(2,1)}, bf16[192,1280]{1,0:T(8,128)(2,1)}, u32[]{:S(2)}, u32[]{:S(2)}) collective-permute-start(bf16[192,1280]{1,0:T(8,128)(2,1)} %get-tuple-element.79), channel_id=1, source_target_pairs={{0,16},{4,20},{8,24},{12,28},{16,0},{20,4},{24,8},{28,12},{1,17},{... | collective-permute-start | bytes 1474568 | tf_op jit(solution)/shard_map/ppermute | solution.py:243
  91.0 1.5 %copy-start.10 = (bf16[192,1280]{1,0:T(8,128)(2,1)}, bf16[192,1280]{1,0:T(8,128)(2,1)S(1)}, u32[]{:S(2)}) copy-start(bf16[192,1280]{1,0:T(8,128)(2,1)S(1)} %collective-permute-done.14.refs_5_) | copy-start | bytes 1474564
  91.0 21.9 %collective-permute-start.25 = (bf16[192,1280]{1,0:T(8,128)(2,1)}, bf16[192,1280]{1,0:T(8,128)(2,1)}, u32[]{:S(2)}, u32[]{:S(2)}) collective-permute-start(bf16[192,1280]{1,0:T(8,128)(2,1)} %get-tuple-element.82), channel_id=1, source_target_pairs={{0,28},{4,24},{8,20},{12,16},{16,12},{20,8},{24,4},{28,0},{1,29},{... | collective-permute-start | bytes 1474568 | tf_op jit(solution)/shard_map/ppermute | solution.py:243
  99.1 1.1 copy-start.1
  104.8 14.0 %collective-permute-start.17 = (bf16[192,768]{1,0:T(8,128)(2,1)}, bf16[192,768]{1,0:T(8,128)(2,1)S(1)}, u32[]{:S(2)}, u32[]{:S(2)}) collective-permute-start(bf16[192,768]{1,0:T(8,128)(2,1)} %get-tuple-element.69), channel_id=1, source_target_pairs={{0,8},{4,12},{8,0},{12,4},{16,24},{20,28},{24,16},{28,20},{1,9},{5... | collective-permute-start | bytes 884744 | tf_op jit(solution)/shard_map/ppermute | solution.py:243
  105.3 5.7 %copy-start.20 = (bf16[192,768]{1,0:T(8,128)(2,1)S(1)}, bf16[192,768]{1,0:T(8,128)(2,1)}, u32[]{:S(2)}) copy-start(bf16[192,768]{1,0:T(8,128)(2,1)} %get-tuple-element.72) | copy-start | bytes 884740
  105.3 18.0 %collective-permute-start.18 = (bf16[192,768]{1,0:T(8,128)(2,1)}, bf16[192,768]{1,0:T(8,128)(2,1)S(1)}, u32[]{:S(2)}, u32[]{:S(2)}) collective-permute-start(bf16[192,768]{1,0:T(8,128)(2,1)} %get-tuple-element.70), channel_id=1, source_target_pairs={{0,12},{4,8},{8,4},{12,0},{16,28},{20,24},{24,20},{28,16},{1,13},{... | collective-permute-start | bytes 884744 | tf_op jit(solution)/shard_map/ppermute | solution.py:243
  109.9 19.5 %collective-permute-start.19 = (bf16[192,768]{1,0:T(8,128)(2,1)}, bf16[192,768]{1,0:T(8,128)(2,1)S(1)}, u32[]{:S(2)}, u32[]{:S(2)}) collective-permute-start(bf16[192,768]{1,0:T(8,128)(2,1)} %get-tuple-element.71), channel_id=1, source_target_pairs={{0,16},{4,20},{8,24},{12,28},{16,0},{20,4},{24,8},{28,12},{1,17},{... | collective-permute-start | bytes 884744 | tf_op jit(solution)/shard_map/ppermute | solution.py:243
  111.0 28.0 %collective-permute-start.20 = (bf16[192,768]{1,0:T(8,128)(2,1)S(1)}, bf16[192,768]{1,0:T(8,128)(2,1)S(1)}, u32[]{:S(2)}, u32[]{:S(2)}) collective-permute-start(bf16[192,768]{1,0:T(8,128)(2,1)S(1)} %copy-done.20), channel_id=1, source_target_pairs={{0,20},{4,16},{8,28},{12,24},{16,4},{20,0},{24,12},{28,8},{1,21},{... | collective-permute-start | bytes 884744 | tf_op jit(solution)/shard_map/ppermute | solution.py:243
  112.9 26.1 %collective-permute-start.16 = (bf16[192,768]{1,0:T(8,128)(2,1)}, bf16[192,768]{1,0:T(8,128)(2,1)S(1)}, u32[]{:S(2)}, u32[]{:S(2)}) collective-permute-start(bf16[192,768]{1,0:T(8,128)(2,1)} %get-tuple-element.68), channel_id=1, source_target_pairs={{0,4},{4,0},{8,12},{12,8},{16,20},{20,16},{24,28},{28,24},{1,5},{5... | collective-permute-start | bytes 884744 | tf_op jit(solution)/shard_map/ppermute | solution.py:243
  118.8 10.6 %copy-start.11 = (bf16[192,768]{1,0:T(8,128)(2,1)}, bf16[192,768]{1,0:T(8,128)(2,1)S(1)}, u32[]{:S(2)}) copy-start(bf16[192,768]{1,0:T(8,128)(2,1)S(1)} %collective-permute-done.17.refs_2_) | copy-start | bytes 884740
  118.8 20.2 %collective-permute-start.21 = (bf16[192,768]{1,0:T(8,128)(2,1)}, bf16[192,768]{1,0:T(8,128)(2,1)S(1)}, u32[]{:S(2)}, u32[]{:S(2)}) collective-permute-start(bf16[192,768]{1,0:T(8,128)(2,1)} %get-tuple-element.73), channel_id=1, source_target_pairs={{0,24},{4,28},{8,16},{12,20},{16,8},{20,12},{24,0},{28,4},{1,25},{... | collective-permute-start | bytes 884744 | tf_op jit(solution)/shard_map/ppermute | solution.py:243
  123.3 6.1 %copy-start.12 = (bf16[192,768]{1,0:T(8,128)(2,1)}, bf16[192,768]{1,0:T(8,128)(2,1)S(1)}, u32[]{:S(2)}) copy-start(bf16[192,768]{1,0:T(8,128)(2,1)S(1)} %collective-permute-done.18.refs_3_) | copy-start | bytes 884740
  123.3 15.8 %collective-permute-start.22 = (bf16[192,768]{1,0:T(8,128)(2,1)}, bf16[192,768]{1,0:T(8,128)(2,1)S(1)}, u32[]{:S(2)}, u32[]{:S(2)}) collective-permute-start(bf16[192,768]{1,0:T(8,128)(2,1)} %get-tuple-element.74), channel_id=1, source_target_pairs={{0,28},{4,24},{8,20},{12,16},{16,12},{20,8},{24,4},{28,0},{1,29},{... | collective-permute-start | bytes 884744 | tf_op jit(solution)/shard_map/ppermute | solution.py:243
  129.4 9.7 %copy-start.13 = (bf16[192,768]{1,0:T(8,128)(2,1)}, bf16[192,768]{1,0:T(8,128)(2,1)S(1)}, u32[]{:S(2)}) copy-start(bf16[192,768]{1,0:T(8,128)(2,1)S(1)} %collective-permute-done.19.refs_4_) | copy-start | bytes 884740
  139.0 0.7 copy-start.14
  139.0 0.8 copy-start.15
  139.0 0.9 copy-start.16
  139.0 1.0 copy-start.17

commit v7 on v6

--- a/solution.py
+++ b/solution.py
@@ -197,7 +197,6 @@
     short = n_expert == 4
     cot = cotangent[0]
     given = lax.dynamic_slice_in_dim(cot, jnp.where(upper, 0, half_width), half_width, 1)
-    cot, given = lax.optimization_barrier((cot, given))
     kept = lax.dynamic_slice_in_dim(cot, jnp.where(upper, half_width, 0), half_width, 1)
     kept, routes, gate_prob = lax.optimization_barrier((kept, routes, gate_prob))
     kept = [kept[:, offset : offset + span] for offset, span in zip(offsets, widths)]

time: 144 us -> 143 us (level)
  waiting for transfers between devices: 57 us -> 55.4 us
    ppermute x14, waiting for transfers between devices: 27.2 us -> 25.3 us  [local(): lax.ppermute(rows, 'section', [(i, i ^ mask) for i in range(n_section)])]
    ppermute x14, starting transfers between devices: 11.4 us -> 13.2 us  [local(): lax.ppermute(rows, 'section', [(i, i ^ mask) for i in range(n_section)])]
    ppermute x2, waiting for transfers between devices: 11.8 us -> 13.3 us  [local(): mirror_acts = [lax.ppermute(group, 'section', mirror) for group in held]]
    unnamed x42 -> x44, local copies, waits for them, and re-layouts: 4.13 us -> 2.99 us
  transfers between devices with their start and end apart: 27 -> 27, of which waited for: 15 -> 14; matrix products, arithmetic and copies ran while one was open for 5% -> 5% of each run, Pallas kernels for 26% -> 26%
where the time goes in v7:
time: 143 us; the launch traced here: 142 us
  waiting for transfers between devices  55.4 us (39%)
  Pallas kernels  39.9 us (28%)
  starting transfers between devices  34.8 us (24%)
  local copies, waits for them, and re-layouts  8.43 us (6%)
  other arithmetic  3.45 us (2%)
    pallas_call x6, Pallas kernels, product(): pl.pallas_call(partial(product_kernel, tokens=tokens, layout=layout), gri...  26.7 us
    ppermute x14, waiting for transfers between devices, local(): lax.ppermute(rows, 'section', [(i, i ^ mask) for i in range(n_section)])  25.3 us
    ppermute x2, waiting for transfers between devices, local(): mirror_acts = [lax.ppermute(group, 'section', mirror) for group in held]  13.3 us
    ppermute x14, starting transfers between devices, local(): lax.ppermute(rows, 'section', [(i, i ^ mask) for i in range(n_section)])  13.2 us
    ppermute x7, starting transfers between devices, shift(): lax.ppermute(block, axis, [(i, (i + step) % size) for i in range(size)])  9.83 us
    ppermute x7, waiting for transfers between devices, shift(): lax.ppermute(block, axis, [(i, (i + step) % size) for i in range(size)])  9.37 us
    pallas_call x2, Pallas kernels, join(): pl.pallas_call(partial(join_kernel, masks=masks, sections=sections, offse...  7.1 us
    all_to_all x1, waiting for transfers between devices, local(): lax.all_to_all(later, 'expert', split_axis=0, concat_axis=0, tiled=True)  6.48 us
  transfers between devices with their start and end apart: 27, of which 14 were waited for; matrix products, arithmetic and copies ran while one was open for 5% of the time, Pallas kernels for 26%

profile of v7, /device:TPU:0, one launch (start us, length us, event | category | flops | bytes accessed | tf_op | source)
XLA Modules:
  0.0 142.2 jit_solution(2504221891251101168)
XLA Ops:
  0.0 2.1 %dynamic-slice_bitcast_fusion = (bf16[128,2048]{1,0:T(8,128)(2,1)}, bf16[128,2048]{1,0:T(8,128)(2,1)S(1)}) fusion(bf16[1,128,4096]{2,1,0:T(8,128)(2,1)} %param.4, s32[]{:T(128)S(6)} %select_n.32, s32[]{:T(128)S(6)} %select_n.31), kind=kLoop, calls=%fused_computation | loop fusion | bytes 2097160 | tf_op jit(solution)/shard_map/dynamic_slice | solution.py:199
  2.1 3.3 %collective-permute-start.3 = (bf16[128,2048]{1,0:T(8,128)(2,1)}, bf16[128,2048]{1,0:T(8,128)(2,1)}, u32[]{:S(2)}, u32[]{:S(2)}) collective-permute-start(bf16[128,2048]{1,0:T(8,128)(2,1)} %get-tuple-element.79), channel_id=1, source_target_pairs={{0,28},{4,24},{8,20},{12,16},{16,12},{20,8},{24,4},{28,0},{1,29},{... | collective-permute-start | bytes 1572872 | tf_op jit(solution)/shard_map/ppermute | solution.py:206
  5.5 3.7 %collective-permute-start.2 = (f32[512]{0:T(512)S(1)}, f32[512]{0:T(512)S(1)}, u32[]{:S(2)}, u32[]{:S(2)}) collective-permute-start(f32[512]{0:T(512)S(1)} %get-tuple-element.86), channel_id=1, source_target_pairs={{0,3},{1,0},{2,1},{3,2},{4,7},{5,4},{6,5},{7,6},{8,11},{9,8},{10,9... | collective-permute-start | bytes 6152 | tf_op jit(solution)/shard_map/ppermute | solution.py:143
  9.1 1.0 collective-permute-start
  10.2 2.5 %collective-permute-start.7 = (bf16[128,1280]{1,0:T(8,128)(2,1)S(1)}, bf16[128,1280]{1,0:T(8,128)(2,1)S(1)}, u32[]{:S(2)}, u32[]{:S(2)}) collective-permute-start(bf16[128,1280]{1,0:T(8,128)(2,1)S(1)} %slice.13), channel_id=1, source_target_pairs={{0,1},{1,2},{2,3},{3,0},{4,5},{5,6},{6,7},{7,4},{8,9},{9,10},{10,1... | collective-permute-start | bytes 983048 | tf_op jit(solution)/shard_map/ppermute | solution.py:143
  12.7 0.9 collective-permute-done.1
  13.6 0.9 collective-permute-done
  15.1 3.4 %shard_map.46 = (bf16[4,192,512]{2,1,0:T(8,128)(2,1)}, bf16[4,192,512]{2,1,0:T(8,128)(2,1)}) custom-call(f32[4,512]{1,0:T(4,128)} %pad_maximum_fusion.meta_ref, bf16[2,4,64,1536]{3,2,1,0:T(8,128)(2,1)} %bitcast.51), custom_call_target="tpu_custom_call" | custom-call | flops 1000000 | bytes 1000 | tf_op jit(solution)/shard_map/pallas_call | solution.py:57
  19.1 0.7 slice.14.refs_0_
  19.7 2.6 %collective-permute-start.11 = (bf16[4,192,512]{2,1,0:T(8,128)(2,1)}, bf16[4,192,512]{2,1,0:T(8,128)(2,1)S(1)}, u32[]{:S(2)}, u32[]{:S(2)}) collective-permute-start(bf16[4,192,512]{2,1,0:T(8,128)(2,1)} %get-tuple-element.52.own_ref), channel_id=1, source_target_pairs={{0,28},{4,24},{8,20},{12,16},{16,12},{20,8},{24,4},{28,0},{1,29},{... | collective-permute-start | bytes 2359304 | tf_op jit(solution)/shard_map/ppermute | solution.py:211
  22.4 1.0 slice.16
  23.4 2.1 %collective-permute-start.5 = (bf16[128,1280]{1,0:T(8,128)(2,1)S(1)}, bf16[128,1280]{1,0:T(8,128)(2,1)S(1)}, u32[]{:S(2)}, u32[]{:S(2)}) collective-permute-start(bf16[128,1280]{1,0:T(8,128)(2,1)S(1)} %slice.16), channel_id=1, source_target_pairs={{0,3},{1,0},{2,1},{3,2},{4,7},{5,4},{6,5},{7,6},{8,11},{9,8},{10,9... | collective-permute-start | bytes 983048 | tf_op jit(solution)/shard_map/ppermute | solution.py:143
  25.5 3.7 %collective-permute-done.8 = bf16[128,1280]{1,0:T(8,128)(2,1)S(1)} collective-permute-done((bf16[128,1280]{1,0:T(8,128)(2,1)S(1)}, bf16[128,1280]{1,0:T(8,128)(2,1)S(1)}, u32[]{:S(2)}, u32[]{:S(2)}) %collective-permute-start.8) | collective-permute-done | bytes 327712 | tf_op jit(solution)/shard_map/ppermute | solution.py:143
  29.2 1.0 select_select_fusion.1
  30.1 1.1 collective-permute-start.9
  31.2 1.6 %slice.17.refs_1_ = bf16[128,768]{1,0:T(8,128)(2,1)} slice(bf16[128,2048]{1,0:T(8,128)(2,1)} %collective-permute-done.3), slice={[0:128], [1280:2048]} | slice | bytes 393216 | tf_op jit(solution)/shard_map/slice | solution.py:207
  32.9 7.1 %collective-permute-done.6.mirror_ref = bf16[4,192,512]{2,1,0:T(8,128)(2,1)S(1)} collective-permute-done((bf16[4,192,512]{2,1,0:T(8,128)(2,1)}, bf16[4,192,512]{2,1,0:T(8,128)(2,1)S(1)}, u32[]{:S(2)}, u32[]{:S(2)}) %collective-permute-start.6) | collective-permute-done | bytes 786464 | tf_op jit(solution)/shard_map/ppermute | solution.py:211
  39.9 2.7 %collective-permute-done.5 = bf16[128,1280]{1,0:T(8,128)(2,1)S(1)} collective-permute-done((bf16[128,1280]{1,0:T(8,128)(2,1)S(1)}, bf16[128,1280]{1,0:T(8,128)(2,1)S(1)}, u32[]{:S(2)}, u32[]{:S(2)}) %collective-permute-start.5) | collective-permute-done | bytes 327712 | tf_op jit(solution)/shard_map/ppermute | solution.py:143
  42.6 1.2 collective-permute-done.4.refs_2_
  43.8 1.9 %slice_bitcast_fusion = (bf16[1,128,1280]{2,1,0:T(8,128)(2,1)}, bf16[128,1280]{1,0:T(8,128)(2,1)S(1)}) fusion(bf16[128,2048]{1,0:T(8,128)(2,1)} %collective-permute-done.3, bf16[128,1280]{1,0:T(8,128)(2,1)S(1)} %collective-permute-done.4.refs_2_, bf16[128,1280]{1,0:T(8,128)(2,1)S(1)} %collective-permute-done.5, pred[]{:T(512)S(6)} %eq.9, pred[]{:T(512)S(6)} %eq.8), kind=kLoop, calls=%fused_computation.8 | loop fusion | flops 327680 | bytes 1638402 | tf_op jit(solution)/shard_map/broadcast_in_dim | solution.py:224
  45.7 1.1 collective-permute-start.10
  46.8 2.7 %shard_map.47 = bf16[4,256,768]{2,1,0:T(8,128)(2,1)} custom-call(bf16[128,768]{1,0:T(8,128)(2,1)} %slice.14.refs_0_, bf16[128,768]{1,0:T(8,128)(2,1)} %slice.17.refs_1_, bf16[128,1280]{1,0:T(8,128)(2,1)} %copy-done.4), custom_call_target="tpu_custom_call" | custom-call | flops 99999997952 | bytes 1000000 | tf_op jit(solution)/shard_map/pallas_call | solution.py:166
  49.5 0.8 collective-permute-done.9
  50.2 6.2 %collective-permute-done.11.mirror_ref = bf16[4,192,512]{2,1,0:T(8,128)(2,1)S(1)} collective-permute-done((bf16[4,192,512]{2,1,0:T(8,128)(2,1)}, bf16[4,192,512]{2,1,0:T(8,128)(2,1)S(1)}, u32[]{:S(2)}, u32[]{:S(2)}) %collective-permute-start.11) | collective-permute-done | bytes 786464 | tf_op jit(solution)/shard_map/ppermute | solution.py:211
  56.7 0.7 copy-done.6
  57.5 3.6 %all-to-all-start = ((bf16[4,256,768]{2,1,0:T(8,128)(2,1)}), bf16[4,256,768]{2,1,0:T(8,128)(2,1)S(1)}, u32[]{:S(2)}, u32[]{:S(2)}) async-start(bf16[4,256,768]{2,1,0:T(8,128)(2,1)} %shard_map.47), calls=%async_computation | async-start | bytes 3145728 | tf_op jit(solution)/shard_map/all_to_all | solution.py:222
  61.1 4.5 %shard_map.49 = (bf16[192,1280]{1,0:T(8,128)(2,1)}, bf16[192,1280]{1,0:T(8,128)(2,1)}) custom-call(bf16[4,192,512]{2,1,0:T(8,128)(2,1)} %get-tuple-element.52.own_ref, bf16[4,192,512]{2,1,0:T(8,128)(2,1)} %copy-done.6, bf16[1,128,1280]{2,1,0:T(8,128)(2,1)} %get-tuple-element.84.refs_0_, bf16[1,128,1280]{2,1,0:T(8,128)(2,1)} %bitcast.27, ...), custom_call_target="tpu_custom_call" | custom-call | flops 1000000 | bytes 1000 | tf_op jit(solution)/shard_map/pallas_call | solution.py:92
  66.6 4.3 %shard_map.48 = (bf16[192,1280]{1,0:T(8,128)(2,1)}, bf16[192,1280]{1,0:T(8,128)(2,1)}) custom-call(bf16[4,192,512]{2,1,0:T(8,128)(2,1)} %get-tuple-element.47.own_ref, bf16[4,192,512]{2,1,0:T(8,128)(2,1)} %copy-done.5, bf16[1,128,1280]{2,1,0:T(8,128)(2,1)} %get-tuple-element.84.refs_0_, bf16[1,128,1280]{2,1,0:T(8,128)(2,1)} %bitcast.28, ...), custom_call_target="tpu_custom_call" | custom-call | flops 1000000 | bytes 1000 | tf_op jit(solution)/shard_map/pallas_call | solution.py:92
  70.9 0.7 collective-permute-start.12
  71.7 2.0 %collective-permute-start.15 = (bf16[192,1280]{1,0:T(8,128)(2,1)}, bf16[192,1280]{1,0:T(8,128)(2,1)S(1)}, u32[]{:S(2)}, u32[]{:S(2)}) collective-permute-start(bf16[192,1280]{1,0:T(8,128)(2,1)} %get-tuple-element.60), channel_id=1, source_target_pairs={{0,24},{4,28},{8,16},{12,20},{16,8},{20,12},{24,0},{28,4},{1,25},{... | collective-permute-start | bytes 1474568 | tf_op jit(solution)/shard_map/ppermute | solution.py:242
  73.6 4.4 %shard_map.53 = (bf16[192,1280]{1,0:T(8,128)(2,1)}, bf16[192,1280]{1,0:T(8,128)(2,1)}) custom-call(bf16[4,192,512]{2,1,0:T(8,128)(2,1)} %get-tuple-element.52.own_ref, bf16[4,192,512]{2,1,0:T(8,128)(2,1)} %copy-done.6, bf16[1,128,1280]{2,1,0:T(8,128)(2,1)} %get-tuple-element.84.refs_0_, bf16[1,128,1280]{2,1,0:T(8,128)(2,1)} %bitcast.29, ...), custom_call_target="tpu_custom_call" | custom-call | flops 1000000 | bytes 1000 | tf_op jit(solution)/shard_map/pallas_call | solution.py:92
  78.0 4.4 %shard_map.52 = (bf16[192,1280]{1,0:T(8,128)(2,1)}, bf16[192,1280]{1,0:T(8,128)(2,1)}) custom-call(bf16[4,192,512]{2,1,0:T(8,128)(2,1)} %get-tuple-element.47.own_ref, bf16[4,192,512]{2,1,0:T(8,128)(2,1)} %copy-done.5, bf16[1,128,1280]{2,1,0:T(8,128)(2,1)} %get-tuple-element.84.refs_0_, bf16[1,128,1280]{2,1,0:T(8,128)(2,1)} %bitcast.30, ...), custom_call_target="tpu_custom_call" | custom-call | flops 1000000 | bytes 1000 | tf_op jit(solution)/shard_map/pallas_call | solution.py:92
  82.6 0.9 collective-permute-start.24
  83.5 6.7 %collective-permute-done.14.refs_5_ = bf16[192,1280]{1,0:T(8,128)(2,1)S(1)} collective-permute-done((bf16[192,1280]{1,0:T(8,128)(2,1)}, bf16[192,1280]{1,0:T(8,128)(2,1)S(1)}, u32[]{:S(2)}, u32[]{:S(2)}) %collective-permute-start.14) | collective-permute-done | bytes 491552 | tf_op jit(solution)/shard_map/ppermute | solution.py:242
  90.2 1.5 %collective-permute-start.25 = (bf16[192,1280]{1,0:T(8,128)(2,1)}, bf16[192,1280]{1,0:T(8,128)(2,1)}, u32[]{:S(2)}, u32[]{:S(2)}) collective-permute-start(bf16[192,1280]{1,0:T(8,128)(2,1)} %get-tuple-element.78), channel_id=1, source_target_pairs={{0,28},{4,24},{8,20},{12,16},{16,12},{20,8},{24,4},{28,0},{1,29},{... | collective-permute-start | bytes 1474568 | tf_op jit(solution)/shard_map/ppermute | solution.py:242
  91.7 6.5 %all-to-all-done.refs_0_ = bf16[4,256,768]{2,1,0:T(8,128)(2,1)S(1)} async-done(((bf16[4,256,768]{2,1,0:T(8,128)(2,1)}), bf16[4,256,768]{2,1,0:T(8,128)(2,1)S(1)}, u32[]{:S(2)}, u32[]{:S(2)}) %all-to-all-start) | async-done | bytes 1572896 | tf_op jit(solution)/shard_map/all_to_all | solution.py:222
  98.2 1.1 copy-done
  99.4 4.6 %shard_map.51 = (bf16[192,768]{1,0:T(8,128)(2,1)}, bf16[192,768]{1,0:T(8,128)(2,1)}, bf16[192,768]{1,0:T(8,128)(2,1)}, bf16[192,768]{1,0:T(8,128)(2,1)}) custom-call(bf16[4,192,512]{2,1,0:T(8,128)(2,1)} %get-tuple-element.52.own_ref, bf16[4,192,512]{2,1,0:T(8,128)(2,1)} %copy-done.6, bf16[4,256,768]{2,1,0:T(8,128)(2,1)} %copy-done), custom_call_target="tpu_custom_call" | custom-call | flops 1000000 | bytes 1000 | tf_op jit(solution)/shard_map/pallas_call | solution.py:92
  104.5 4.6 %shard_map.50 = (bf16[192,768]{1,0:T(8,128)(2,1)}, bf16[192,768]{1,0:T(8,128)(2,1)}, bf16[192,768]{1,0:T(8,128)(2,1)}, bf16[192,768]{1,0:T(8,128)(2,1)}) custom-call(bf16[4,192,512]{2,1,0:T(8,128)(2,1)} %get-tuple-element.47.own_ref, bf16[4,192,512]{2,1,0:T(8,128)(2,1)} %copy-done.5, bf16[4,256,768]{2,1,0:T(8,128)(2,1)} %copy-done), custom_call_target="tpu_custom_call" | custom-call | flops 1000000 | bytes 1000 | tf_op jit(solution)/shard_map/pallas_call | solution.py:92
  109.0 1.4 collective-permute-start.19
  110.4 1.6 %collective-permute-start.20 = (bf16[192,768]{1,0:T(8,128)(2,1)}, bf16[192,768]{1,0:T(8,128)(2,1)S(1)}, u32[]{:S(2)}, u32[]{:S(2)}) collective-permute-start(bf16[192,768]{1,0:T(8,128)(2,1)} %get-tuple-element.68), channel_id=1, source_target_pairs={{0,20},{4,16},{8,28},{12,24},{16,4},{20,0},{24,12},{28,8},{1,21},{... | collective-permute-start | bytes 884744 | tf_op jit(solution)/shard_map/ppermute | solution.py:242
  112.1 5.9 %collective-permute-done.17.refs_2_ = bf16[192,768]{1,0:T(8,128)(2,1)S(1)} collective-permute-done((bf16[192,768]{1,0:T(8,128)(2,1)}, bf16[192,768]{1,0:T(8,128)(2,1)S(1)}, u32[]{:S(2)}, u32[]{:S(2)}) %collective-permute-start.17) | collective-permute-done | bytes 294944 | tf_op jit(solution)/shard_map/ppermute | solution.py:242
  118.0 0.9 collective-permute-start.21
  118.9 3.6 %collective-permute-done.18.refs_3_ = bf16[192,768]{1,0:T(8,128)(2,1)S(1)} collective-permute-done((bf16[192,768]{1,0:T(8,128)(2,1)}, bf16[192,768]{1,0:T(8,128)(2,1)S(1)}, u32[]{:S(2)}, u32[]{:S(2)}) %collective-permute-start.18) | collective-permute-done | bytes 294944 | tf_op jit(solution)/shard_map/ppermute | solution.py:242
  122.5 2.5 %collective-permute-start.22 = (bf16[192,768]{1,0:T(8,128)(2,1)}, bf16[192,768]{1,0:T(8,128)(2,1)S(1)}, u32[]{:S(2)}, u32[]{:S(2)}) collective-permute-start(bf16[192,768]{1,0:T(8,128)(2,1)} %get-tuple-element.70), channel_id=1, source_target_pairs={{0,28},{4,24},{8,20},{12,16},{16,12},{20,8},{24,4},{28,0},{1,29},{... | collective-permute-start | bytes 884744 | tf_op jit(solution)/shard_map/ppermute | solution.py:242
  124.9 4.0 %shard_map.54.refs_8_ = bf16[4,1,192,4096]{3,2,1,0:T(8,128)(2,1)} custom-call(bf16[192,1280]{1,0:T(8,128)(2,1)} %get-tuple-element.71.refs_0_, bf16[192,1280]{1,0:T(8,128)(2,1)} %copy-done.11, bf16[192,1280]{1,0:T(8,128)(2,1)} %copy-done.9, bf16[192,1280]{1,0:T(8,128)(2,1)} %collective-permute-done.23.refs_3_, ...), custom_call_target="tpu_custom_call" | custom-call | tf_op jit(solution)/shard_map/pallas_call | solution.py:131
  129.0 9.1 %collective-permute-done.20.refs_5_ = bf16[192,768]{1,0:T(8,128)(2,1)S(1)} collective-permute-done((bf16[192,768]{1,0:T(8,128)(2,1)}, bf16[192,768]{1,0:T(8,128)(2,1)S(1)}, u32[]{:S(2)}, u32[]{:S(2)}) %collective-permute-start.20) | collective-permute-done | bytes 294944 | tf_op jit(solution)/shard_map/ppermute | solution.py:242
  139.2 3.0 %shard_map.55 = bf16[4,1,192,4096]{3,2,1,0:T(8,128)(2,1)} custom-call(bf16[192,768]{1,0:T(8,128)(2,1)} %get-tuple-element.63.refs_0_, bf16[192,768]{1,0:T(8,128)(2,1)} %copy-done.17, bf16[192,768]{1,0:T(8,128)(2,1)} %copy-done.13, bf16[192,768]{1,0:T(8,128)(2,1)} %copy-done.14, bf16[192,768]{1,0:T(8,128)(2,1)} %copy-done.15, ...), custom_call_target="tpu_custom_call", output_to_operand_aliasing={{}: (8, {})} | custom-call | tf_op jit(solution)/shard_map/pallas_call | solution.py:131
  (70 shorter events, 4.4 us)
Async XLA Ops:
  0.0 5.5 %copy-start.21 = (f32[1,128,2]{1,2,0:T(2,128)S(1)}, f32[1,128,2]{1,2,0:T(2,128)}, u32[]{:S(2)}) copy-start(f32[1,128,2]{1,2,0:T(2,128)} %param.6) | copy-start | bytes 3076
  0.0 5.4 %copy-start.20 = (s32[1,128,2]{1,2,0:T(2,128)S(1)}, s32[1,128,2]{1,2,0:T(2,128)}, u32[]{:S(2)}) copy-start(s32[1,128,2]{1,2,0:T(2,128)} %param.5) | copy-start | bytes 3076
  2.1 20.3 %collective-permute-start.3 = (bf16[128,2048]{1,0:T(8,128)(2,1)}, bf16[128,2048]{1,0:T(8,128)(2,1)}, u32[]{:S(2)}, u32[]{:S(2)}) collective-permute-start(bf16[128,2048]{1,0:T(8,128)(2,1)} %get-tuple-element.79), channel_id=1, source_target_pairs={{0,28},{4,24},{8,20},{12,16},{16,12},{20,8},{24,4},{28,0},{1,29},{... | collective-permute-start | bytes 1572872 | tf_op jit(solution)/shard_map/ppermute | solution.py:206
  5.5 7.2 %collective-permute-start.2 = (f32[512]{0:T(512)S(1)}, f32[512]{0:T(512)S(1)}, u32[]{:S(2)}, u32[]{:S(2)}) collective-permute-start(f32[512]{0:T(512)S(1)} %get-tuple-element.86), channel_id=1, source_target_pairs={{0,3},{1,0},{2,1},{3,2},{4,7},{5,4},{6,5},{7,6},{8,11},{9,8},{10,9... | collective-permute-start | bytes 6152 | tf_op jit(solution)/shard_map/ppermute | solution.py:143
  9.1 4.5 %collective-permute-start.1 = (f32[512]{0:T(512)S(1)}, f32[512]{0:T(512)S(1)}, u32[]{:S(2)}, u32[]{:S(2)}) collective-permute-start(f32[512]{0:T(512)S(1)} %get-tuple-element.86), channel_id=1, source_target_pairs={{0,2},{1,3},{2,0},{3,1},{4,6},{5,7},{6,4},{7,5},{8,10},{9,11},{10,... | collective-permute-start | bytes 6152 | tf_op jit(solution)/shard_map/ppermute | solution.py:143
  9.1 5.4 %collective-permute-start = (f32[512]{0:T(512)S(1)}, f32[512]{0:T(512)S(1)}, u32[]{:S(2)}, u32[]{:S(2)}) collective-permute-start(f32[512]{0:T(512)S(1)} %get-tuple-element.86), channel_id=1, source_target_pairs={{0,1},{1,2},{2,3},{3,0},{4,5},{5,6},{6,7},{7,4},{8,9},{9,10},{10,1... | collective-permute-start | bytes 6152 | tf_op jit(solution)/shard_map/ppermute | solution.py:143
  10.2 15.3 %collective-permute-start.7 = (bf16[128,1280]{1,0:T(8,128)(2,1)S(1)}, bf16[128,1280]{1,0:T(8,128)(2,1)S(1)}, u32[]{:S(2)}, u32[]{:S(2)}) collective-permute-start(bf16[128,1280]{1,0:T(8,128)(2,1)S(1)} %slice.13), channel_id=1, source_target_pairs={{0,1},{1,2},{2,3},{3,0},{4,5},{5,6},{6,7},{7,4},{8,9},{9,10},{10,1... | collective-permute-start | bytes 983048 | tf_op jit(solution)/shard_map/ppermute | solution.py:143
  18.5 10.6 %collective-permute-start.8 = (bf16[128,1280]{1,0:T(8,128)(2,1)S(1)}, bf16[128,1280]{1,0:T(8,128)(2,1)S(1)}, u32[]{:S(2)}, u32[]{:S(2)}) collective-permute-start(bf16[128,1280]{1,0:T(8,128)(2,1)S(1)} %slice.13), channel_id=1, source_target_pairs={{0,3},{1,0},{2,1},{3,2},{4,7},{5,4},{6,5},{7,6},{8,11},{9,8},{10,9... | collective-permute-start | bytes 983048 | tf_op jit(solution)/shard_map/ppermute | solution.py:143
  19.1 20.9 %collective-permute-start.6 = (bf16[4,192,512]{2,1,0:T(8,128)(2,1)}, bf16[4,192,512]{2,1,0:T(8,128)(2,1)S(1)}, u32[]{:S(2)}, u32[]{:S(2)}) collective-permute-start(bf16[4,192,512]{2,1,0:T(8,128)(2,1)} %get-tuple-element.47.own_ref), channel_id=1, source_target_pairs={{0,28},{4,24},{8,20},{12,16},{16,12},{20,8},{24,4},{28,0},{1,29},{... | collective-permute-start | bytes 2359304 | tf_op jit(solution)/shard_map/ppermute | solution.py:211
  19.7 36.7 %collective-permute-start.11 = (bf16[4,192,512]{2,1,0:T(8,128)(2,1)}, bf16[4,192,512]{2,1,0:T(8,128)(2,1)S(1)}, u32[]{:S(2)}, u32[]{:S(2)}) collective-permute-start(bf16[4,192,512]{2,1,0:T(8,128)(2,1)} %get-tuple-element.52.own_ref), channel_id=1, source_target_pairs={{0,28},{4,24},{8,20},{12,16},{16,12},{20,8},{24,4},{28,0},{1,29},{... | collective-permute-start | bytes 2359304 | tf_op jit(solution)/shard_map/ppermute | solution.py:211
  23.4 19.2 %collective-permute-start.5 = (bf16[128,1280]{1,0:T(8,128)(2,1)S(1)}, bf16[128,1280]{1,0:T(8,128)(2,1)S(1)}, u32[]{:S(2)}, u32[]{:S(2)}) collective-permute-start(bf16[128,1280]{1,0:T(8,128)(2,1)S(1)} %slice.16), channel_id=1, source_target_pairs={{0,3},{1,0},{2,1},{3,2},{4,7},{5,4},{6,5},{7,6},{8,11},{9,8},{10,9... | collective-permute-start | bytes 983048 | tf_op jit(solution)/shard_map/ppermute | solution.py:143
  25.5 20.2 %copy-start.1 = (bf16[128,1280]{1,0:T(8,128)(2,1)}, bf16[128,1280]{1,0:T(8,128)(2,1)S(1)}, u32[]{:S(2)}) copy-start(bf16[128,1280]{1,0:T(8,128)(2,1)S(1)} %collective-permute-done.7) | copy-start | bytes 983044
  25.5 18.3 %collective-permute-start.4 = (bf16[128,1280]{1,0:T(8,128)(2,1)S(1)}, bf16[128,1280]{1,0:T(8,128)(2,1)S(1)}, u32[]{:S(2)}, u32[]{:S(2)}) collective-permute-start(bf16[128,1280]{1,0:T(8,128)(2,1)S(1)} %slice.16), channel_id=1, source_target_pairs={{0,1},{1,2},{2,3},{3,0},{4,5},{5,6},{6,7},{7,4},{8,9},{9,10},{10,1... | collective-permute-start | bytes 983048 | tf_op jit(solution)/shard_map/ppermute | solution.py:143
  29.1 16.5 %copy-start.2 = (bf16[128,1280]{1,0:T(8,128)(2,1)}, bf16[128,1280]{1,0:T(8,128)(2,1)S(1)}, u32[]{:S(2)}) copy-start(bf16[128,1280]{1,0:T(8,128)(2,1)S(1)} %collective-permute-done.8) | copy-start | bytes 983044
  30.1 20.1 %collective-permute-start.9 = (bf16[128,1280]{1,0:T(8,128)(2,1)}, bf16[128,1280]{1,0:T(8,128)(2,1)S(1)}, u32[]{:S(2)}, u32[]{:S(2)}) collective-permute-start(bf16[128,1280]{1,0:T(8,128)(2,1)} %get-tuple-element.83), channel_id=1, source_target_pairs={{0,2},{2,3},{3,1},{1,0},{4,6},{6,7},{7,5},{5,4},{8,10},{10,11},{11... | collective-permute-start | bytes 983048 | tf_op jit(solution)/shard_map/ppermute | solution.py:153
  39.9 9.5 %copy-start.5 = (bf16[4,192,512]{2,1,0:T(8,128)(2,1)}, bf16[4,192,512]{2,1,0:T(8,128)(2,1)S(1)}, u32[]{:S(2)}) copy-start(bf16[4,192,512]{2,1,0:T(8,128)(2,1)S(1)} %collective-permute-done.6.mirror_ref) | copy-start | bytes 2359300
  42.6 6.9 %copy-start.3 = (bf16[128,1280]{1,0:T(8,128)(2,1)}, bf16[128,1280]{1,0:T(8,128)(2,1)S(1)}, u32[]{:S(2)}) copy-start(bf16[128,1280]{1,0:T(8,128)(2,1)S(1)} %collective-permute-done.5) | copy-start | bytes 983044
  43.8 3.0 %copy-start.4 = (bf16[128,1280]{1,0:T(8,128)(2,1)}, bf16[128,1280]{1,0:T(8,128)(2,1)S(1)}, u32[]{:S(2)}) copy-start(bf16[128,1280]{1,0:T(8,128)(2,1)S(1)} %collective-permute-done.4.refs_2_) | copy-start | bytes 983044
  45.7 11.0 %collective-permute-start.10 = (bf16[128,1280]{1,0:T(8,128)(2,1)S(1)}, bf16[128,1280]{1,0:T(8,128)(2,1)S(1)}, u32[]{:S(2)}, u32[]{:S(2)}) collective-permute-start(bf16[128,1280]{1,0:T(8,128)(2,1)S(1)} %get-tuple-element.82), channel_id=1, source_target_pairs={{0,2},{2,3},{3,1},{1,0},{4,6},{6,7},{7,5},{5,4},{8,10},{10,11},{11... | collective-permute-start | bytes 983048 | tf_op jit(solution)/shard_map/ppermute | solution.py:153
  50.2 10.9 %copy-start.7 = (bf16[128,1280]{1,0:T(8,128)(2,1)}, bf16[128,1280]{1,0:T(8,128)(2,1)S(1)}, u32[]{:S(2)}) copy-start(bf16[128,1280]{1,0:T(8,128)(2,1)S(1)} %collective-permute-done.9) | copy-start | bytes 983044
  56.4 0.9 copy-start.6
  56.7 0.8 copy-start.8
  57.5 40.7 %all-to-all-start = ((bf16[4,256,768]{2,1,0:T(8,128)(2,1)}), bf16[4,256,768]{2,1,0:T(8,128)(2,1)S(1)}, u32[]{:S(2)}, u32[]{:S(2)}) async-start(bf16[4,256,768]{2,1,0:T(8,128)(2,1)} %shard_map.47), calls=%async_computation | async-start | bytes 3145728 | tf_op jit(solution)/shard_map/all_to_all | solution.py:222
  65.6 17.0 %collective-permute-start.13 = (bf16[192,1280]{1,0:T(8,128)(2,1)}, bf16[192,1280]{1,0:T(8,128)(2,1)S(1)}, u32[]{:S(2)}, u32[]{:S(2)}) collective-permute-start(bf16[192,1280]{1,0:T(8,128)(2,1)} %get-tuple-element.58), channel_id=1, source_target_pairs={{0,8},{4,12},{8,0},{12,4},{16,24},{20,28},{24,16},{28,20},{1,9},{5... | collective-permute-start | bytes 1474568 | tf_op jit(solution)/shard_map/ppermute | solution.py:242
  66.2 24.0 %collective-permute-start.14 = (bf16[192,1280]{1,0:T(8,128)(2,1)}, bf16[192,1280]{1,0:T(8,128)(2,1)S(1)}, u32[]{:S(2)}, u32[]{:S(2)}) collective-permute-start(bf16[192,1280]{1,0:T(8,128)(2,1)} %get-tuple-element.59), channel_id=1, source_target_pairs={{0,20},{4,16},{8,28},{12,24},{16,4},{20,0},{24,12},{28,8},{1,21},{... | collective-permute-start | bytes 1474568 | tf_op jit(solution)/shard_map/ppermute | solution.py:242
  70.9 20.8 %collective-permute-start.12 = (bf16[192,1280]{1,0:T(8,128)(2,1)}, bf16[192,1280]{1,0:T(8,128)(2,1)S(1)}, u32[]{:S(2)}, u32[]{:S(2)}) collective-permute-start(bf16[192,1280]{1,0:T(8,128)(2,1)} %get-tuple-element.56), channel_id=1, source_target_pairs={{0,4},{4,0},{8,12},{12,8},{16,20},{20,16},{24,28},{28,24},{1,5},{5... | collective-permute-start | bytes 1474568 | tf_op jit(solution)/shard_map/ppermute | solution.py:242
  71.7 20.1 %collective-permute-start.15 = (bf16[192,1280]{1,0:T(8,128)(2,1)}, bf16[192,1280]{1,0:T(8,128)(2,1)S(1)}, u32[]{:S(2)}, u32[]{:S(2)}) collective-permute-start(bf16[192,1280]{1,0:T(8,128)(2,1)} %get-tuple-element.60), channel_id=1, source_target_pairs={{0,24},{4,28},{8,16},{12,20},{16,8},{20,12},{24,0},{28,4},{1,25},{... | collective-permute-start | bytes 1474568 | tf_op jit(solution)/shard_map/ppermute | solution.py:242
  82.5 26.5 %collective-permute-start.23 = (bf16[192,1280]{1,0:T(8,128)(2,1)}, bf16[192,1280]{1,0:T(8,128)(2,1)}, u32[]{:S(2)}, u32[]{:S(2)}) collective-permute-start(bf16[192,1280]{1,0:T(8,128)(2,1)} %get-tuple-element.74), channel_id=1, source_target_pairs={{0,12},{4,8},{8,4},{12,0},{16,28},{20,24},{24,20},{28,16},{1,13},{... | collective-permute-start | bytes 1474568 | tf_op jit(solution)/shard_map/ppermute | solution.py:242
  82.6 42.4 %copy-start.9 = (bf16[192,1280]{1,0:T(8,128)(2,1)}, bf16[192,1280]{1,0:T(8,128)(2,1)S(1)}, u32[]{:S(2)}) copy-start(bf16[192,1280]{1,0:T(8,128)(2,1)S(1)} %collective-permute-done.13.refs_2_) | copy-start | bytes 1474564
  82.6 27.8 %collective-permute-start.24 = (bf16[192,1280]{1,0:T(8,128)(2,1)}, bf16[192,1280]{1,0:T(8,128)(2,1)}, u32[]{:S(2)}, u32[]{:S(2)}) collective-permute-start(bf16[192,1280]{1,0:T(8,128)(2,1)} %get-tuple-element.75), channel_id=1, source_target_pairs={{0,16},{4,20},{8,24},{12,28},{16,0},{20,4},{24,8},{28,12},{1,17},{... | collective-permute-start | bytes 1474568 | tf_op jit(solution)/shard_map/ppermute | solution.py:242
  90.2 34.7 %copy-start.10 = (bf16[192,1280]{1,0:T(8,128)(2,1)}, bf16[192,1280]{1,0:T(8,128)(2,1)S(1)}, u32[]{:S(2)}) copy-start(bf16[192,1280]{1,0:T(8,128)(2,1)S(1)} %collective-permute-done.14.refs_5_) | copy-start | bytes 1474564
  90.2 21.8 %collective-permute-start.25 = (bf16[192,1280]{1,0:T(8,128)(2,1)}, bf16[192,1280]{1,0:T(8,128)(2,1)}, u32[]{:S(2)}, u32[]{:S(2)}) collective-permute-start(bf16[192,1280]{1,0:T(8,128)(2,1)} %get-tuple-element.78), channel_id=1, source_target_pairs={{0,28},{4,24},{8,20},{12,16},{16,12},{20,8},{24,4},{28,0},{1,29},{... | collective-permute-start | bytes 1474568 | tf_op jit(solution)/shard_map/ppermute | solution.py:242
  91.7 33.2 %copy-start.11 = (bf16[192,1280]{1,0:T(8,128)(2,1)}, bf16[192,1280]{1,0:T(8,128)(2,1)S(1)}, u32[]{:S(2)}) copy-start(bf16[192,1280]{1,0:T(8,128)(2,1)S(1)} %collective-permute-done.12.refs_1_) | copy-start | bytes 1474564
  91.7 33.2 %copy-start.12 = (bf16[192,1280]{1,0:T(8,128)(2,1)}, bf16[192,1280]{1,0:T(8,128)(2,1)S(1)}, u32[]{:S(2)}) copy-start(bf16[192,1280]{1,0:T(8,128)(2,1)S(1)} %collective-permute-done.15.refs_6_) | copy-start | bytes 1474564
  98.2 1.1 copy-start
  103.9 14.1 %collective-permute-start.17 = (bf16[192,768]{1,0:T(8,128)(2,1)}, bf16[192,768]{1,0:T(8,128)(2,1)S(1)}, u32[]{:S(2)}, u32[]{:S(2)}) collective-permute-start(bf16[192,768]{1,0:T(8,128)(2,1)} %get-tuple-element.65), channel_id=1, source_target_pairs={{0,8},{4,12},{8,0},{12,4},{16,24},{20,28},{24,16},{28,20},{1,9},{5... | collective-permute-start | bytes 884744 | tf_op jit(solution)/shard_map/ppermute | solution.py:242
  104.5 18.0 %collective-permute-start.18 = (bf16[192,768]{1,0:T(8,128)(2,1)}, bf16[192,768]{1,0:T(8,128)(2,1)S(1)}, u32[]{:S(2)}, u32[]{:S(2)}) collective-permute-start(bf16[192,768]{1,0:T(8,128)(2,1)} %get-tuple-element.66), channel_id=1, source_target_pairs={{0,12},{4,8},{8,4},{12,0},{16,28},{20,24},{24,20},{28,16},{1,13},{... | collective-permute-start | bytes 884744 | tf_op jit(solution)/shard_map/ppermute | solution.py:242
  109.0 20.0 %collective-permute-start.19 = (bf16[192,768]{1,0:T(8,128)(2,1)}, bf16[192,768]{1,0:T(8,128)(2,1)S(1)}, u32[]{:S(2)}, u32[]{:S(2)}) collective-permute-start(bf16[192,768]{1,0:T(8,128)(2,1)} %get-tuple-element.67), channel_id=1, source_target_pairs={{0,16},{4,20},{8,24},{12,28},{16,0},{20,4},{24,8},{28,12},{1,17},{... | collective-permute-start | bytes 884744 | tf_op jit(solution)/shard_map/ppermute | solution.py:242
  110.4 27.7 %collective-permute-start.20 = (bf16[192,768]{1,0:T(8,128)(2,1)}, bf16[192,768]{1,0:T(8,128)(2,1)S(1)}, u32[]{:S(2)}, u32[]{:S(2)}) collective-permute-start(bf16[192,768]{1,0:T(8,128)(2,1)} %get-tuple-element.68), channel_id=1, source_target_pairs={{0,20},{4,16},{8,28},{12,24},{16,4},{20,0},{24,12},{28,8},{1,21},{... | collective-permute-start | bytes 884744 | tf_op jit(solution)/shard_map/ppermute | solution.py:242
  112.0 26.1 %collective-permute-start.16 = (bf16[192,768]{1,0:T(8,128)(2,1)}, bf16[192,768]{1,0:T(8,128)(2,1)S(1)}, u32[]{:S(2)}, u32[]{:S(2)}) collective-permute-start(bf16[192,768]{1,0:T(8,128)(2,1)} %get-tuple-element.64), channel_id=1, source_target_pairs={{0,4},{4,0},{8,12},{12,8},{16,20},{20,16},{24,28},{28,24},{1,5},{5... | collective-permute-start | bytes 884744 | tf_op jit(solution)/shard_map/ppermute | solution.py:242
  118.0 11.0 %copy-start.13 = (bf16[192,768]{1,0:T(8,128)(2,1)}, bf16[192,768]{1,0:T(8,128)(2,1)S(1)}, u32[]{:S(2)}) copy-start(bf16[192,768]{1,0:T(8,128)(2,1)S(1)} %collective-permute-done.17.refs_2_) | copy-start | bytes 884740
  118.0 20.2 %collective-permute-start.21 = (bf16[192,768]{1,0:T(8,128)(2,1)}, bf16[192,768]{1,0:T(8,128)(2,1)S(1)}, u32[]{:S(2)}, u32[]{:S(2)}) collective-permute-start(bf16[192,768]{1,0:T(8,128)(2,1)} %get-tuple-element.69), channel_id=1, source_target_pairs={{0,24},{4,28},{8,16},{12,20},{16,8},{20,12},{24,0},{28,4},{1,25},{... | collective-permute-start | bytes 884744 | tf_op jit(solution)/shard_map/ppermute | solution.py:242
  122.5 6.6 %copy-start.14 = (bf16[192,768]{1,0:T(8,128)(2,1)}, bf16[192,768]{1,0:T(8,128)(2,1)S(1)}, u32[]{:S(2)}) copy-start(bf16[192,768]{1,0:T(8,128)(2,1)S(1)} %collective-permute-done.18.refs_3_) | copy-start | bytes 884740
  122.5 15.7 %collective-permute-start.22 = (bf16[192,768]{1,0:T(8,128)(2,1)}, bf16[192,768]{1,0:T(8,128)(2,1)S(1)}, u32[]{:S(2)}, u32[]{:S(2)}) collective-permute-start(bf16[192,768]{1,0:T(8,128)(2,1)} %get-tuple-element.70), channel_id=1, source_target_pairs={{0,28},{4,24},{8,20},{12,16},{16,12},{20,8},{24,4},{28,0},{1,29},{... | collective-permute-start | bytes 884744 | tf_op jit(solution)/shard_map/ppermute | solution.py:242
  129.0 9.2 %copy-start.15 = (bf16[192,768]{1,0:T(8,128)(2,1)}, bf16[192,768]{1,0:T(8,128)(2,1)S(1)}, u32[]{:S(2)}) copy-start(bf16[192,768]{1,0:T(8,128)(2,1)S(1)} %collective-permute-done.19.refs_4_) | copy-start | bytes 884740
  138.1 0.8 copy-start.17
  138.2 0.9 copy-start.18
  138.2 1.0 copy-start.19
  (1 other events, 0.7 us)
